TPU v7x, 256 devices: a whole 4x4x8 slice. The times are simulated.
256 devices in a mesh: img: 32 (over z, x), tp: 8 (over y, core).
Axes of the slice: x: 4, y: 4, z: 8, core: 2. Of those that a mesh axis runs over, the one named last changes fastest.
Arguments:
- vision_tokens: bfloat16 [16384, 1280], P('img')
- inter_feats: bfloat16 [16384, 2560], P('img'), may hold values from -6 to 6
- fc1_weight: bfloat16 [1280, 2560], P(None, 'tp'), may hold values from -0.15625 to 0.15625
- fc2_weight: bfloat16 [2560, 1280], P('tp'), may hold values from -0.125 to 0.125
- proj_weight: bfloat16 [3840, 8192], P('img', 'tp'), may hold values from -0.09375 to 0.09375
- kv_weight: bfloat16 [8192, 2048], P('tp'), may hold values from -0.0625 to 0.0625
- tile_counts: int32 [128], replicated, may hold values from 1 to 4
- owner_map: int32 [128], replicated, may hold values from 0 to 31, as said below
- decode_hidden: bfloat16 [128, 8192], P(None, 'img'), may hold values from -6 to 6
- query_weight: bfloat16 [8192, 8192], P('img', 'tp'), may hold values from -0.0625 to 0.0625
Outputs:
- vision_states: bfloat16 [16384, 8192], P('img', 'tp')
- kv_cache: bfloat16 [256, 128, 2048], P('img', None, 'tp')
- attended: bfloat16 [256, 8192], P('img', 'tp')
Inputs may be any that keep to these rules, and one draw needn't show every extreme that they name: `owner_map`: among the 16 requests b * 16 to (b + 1) * 16 - 1 no owner is named more than 1 times. Every owner is named at least once and at most 8 times, and one owner exactly 8 times.
All inputs are finite; a program needn't handle non-finite values.
Results may differ from a plain program's by a relative error of at most 0.013.
Values may be sent and summed in bfloat16 or wider, within the bound.
No kernel may reach another device: no remote copies, remote signals or barrier semaphores. Data moves between devices by JAX's collectives and lax.ppermute only.
A program may use at most 64 MiB of HBM per device.

v0:
```python
import functools
import math

import jax
import jax.numpy as jnp
from jax import lax
from jax.experimental import pallas as pl
from jax.experimental.pallas import tpu as pltpu
from jax.sharding import Mesh, PartitionSpec as P

QH = 64
KVH = 8
HD = 128
TILES = 4
NZ, NX, NY, NC = 8, 4, 4, 2
NIMG = NZ * NX
BLOCK = 16
CAP = 8
GROUP = QH // KVH
KVW = 2 * HD
BF = jnp.bfloat16
F32 = jnp.float32
I32 = jnp.int32
VMEM_LIMIT = 14 * 2**20
COST = 1
LAST_COST = 10**8
HOPS = (0, -1, 1, 2)
HOPS = (0, -1, 1, 2)


def shift(value, axis, step):
    n = lax.axis_size(axis)
    return lax.ppermute(value, axis, [(i, (i + step) % n) for i in range(n)])


def tick(array):
    return array.reshape(-1, array.shape[-1])[:8, :HD]


def dot(a, b):
    return jnp.dot(a, b, preferred_element_type=F32)


def pick(array, index, axis=0):
    return lax.dynamic_index_in_dim(array, index, axis, keepdims=False)


def place(buffer, value, index, axis):
    return lax.dynamic_update_index_in_dim(buffer, value, index, axis)


def rms_scale(values, epsilon):
    return values * lax.rsqrt(jnp.mean(values * values, -1, keepdims=True) + epsilon)


def shape(dims, dtype=BF):
    return jax.ShapeDtypeStruct(dims, dtype)


def call(body, out_shape, scalars, operands, after=(), scratch=(), space=pltpu.VMEM, cost=COST):
    lead = len(scalars) + len(operands)

    def kernel(*refs):
        body(*refs[:lead], *refs[lead + len(after) :])

    smem, vmem = (pl.BlockSpec(memory_space=space) for space in (pltpu.SMEM, pltpu.VMEM))
    several = isinstance(out_shape, (list, tuple))
    return pl.pallas_call(
        kernel,
        in_specs=[smem] * len(scalars)
        + [pl.BlockSpec(memory_space=space)] * len(operands)
        + [pl.BlockSpec(memory_space=pl.ANY)] * len(after),
        out_specs=[vmem] * len(out_shape) if several else vmem,
        out_shape=out_shape,
        scratch_shapes=scratch,
        compiler_params=pltpu.CompilerParams(vmem_limit_bytes=VMEM_LIMIT),
        cost_estimate=pl.CostEstimate(flops=cost, bytes_accessed=cost, transcendentals=0),
    )(*scalars, *operands, *after)


def fold_body(core, proj, kv, send, keep):
    for here in range(NC):

        @pl.when(core[0] == here)
        def _(here=here):
            for y in range(NY):
                other, mine = (2 * y + 1 - here) * KVW, (2 * y + here) * KVW
                send[y] = dot(proj[...], kv[:, other : other + KVW]).astype(BF)
                keep[y] = dot(proj[...], kv[:, mine : mine + KVW])


def fold_weights(core, proj, kv):
    dims = (NY, proj.shape[0], KVW)
    return call(fold_body, [shape(dims), shape(dims, F32)], [core], [proj, kv])


def half_body(y, swapped, keep, up, down, across, own):
    for step, out in ((1, up), (NY - 1, down), (2, across)):
        place = (y[0] + step) % NY
        out[...] = (swapped[place].astype(F32) + keep[place]).astype(BF)
    own[...] = swapped[y[0]].astype(F32) + keep[y[0]]


def half_sums(y, swapped, keep, after=()):
    dims = keep.shape[1:]
    outs = [shape(dims)] * 3 + [shape(dims, F32)]
    return call(half_body, outs, [y], [swapped, keep], after)


def join_body(own, up, down, across, out):
    total = own[...] + up[...].astype(F32) + down[...].astype(F32) + across[...].astype(F32)
    out[...] = total.astype(BF)


def join(own, parts, after):
    return call(join_body, shape(own.shape), [], [own, *parts], after)


def block_body(x, own, left, right, far, out):
    for step, value in zip(HOPS, (own, left, right, far)):
        out[(x[0] + step) % NX] = value[...]


def in_order(x, parts, after):
    return call(block_body, shape((NX,) + parts[0].shape), [x], parts, after)


def layer_body(core, tokens, fc1, fc2, send, keep):
    half = tokens.shape[0] // NC

    def rows(which):
        wide = tokens[pl.ds(pl.multiple_of(which * half, half), half), :].astype(F32)
        center = wide - jnp.mean(wide, -1, keepdims=True)
        spread = jnp.mean(center * center, -1, keepdims=True)
        normed = (center * lax.rsqrt(spread + 1e-05)).astype(BF)
        value = lax.dot_general(
            normed, fc1[...], (((1,), (1,)), ((), ())), preferred_element_type=F32
        )
        hidden = (0.5 * value * (1.0 + lax.erf(value * math.sqrt(0.5)))).astype(BF)
        return dot(hidden, fc2[...])

    send[...] = rows(1 - core[0]).astype(BF).reshape(send.shape)
    keep[...] = rows(core[0]).reshape(keep.shape)


def layer(core, tokens, fc1, fc2, after):
    dims = (NY, tokens.shape[0] // (NC * NY), tokens.shape[1])
    return call(layer_body, [shape(dims), shape(dims, F32)], [core], [tokens, fc1, fc2], after)


def piece_body(place, own, up, down, across, tokens, out):
    total = own[...] + up[...].astype(F32) + down[...].astype(F32) + across[...].astype(F32)
    rows = own.shape[0]
    here = tokens[pl.ds(pl.multiple_of(place[0] * rows, rows), rows), :]
    out[...] = (here.astype(F32) + total).astype(BF)


def encoded_piece(place, own, parts, tokens, after):
    return call(piece_body, shape(own.shape), [place], [own, *parts, tokens], after)


def regroup_body(shard, encoded, inter, out):
    part = encoded.shape[0] // 4
    for r in range(0, encoded.shape[0], part):
        features = jnp.concatenate([encoded[r : r + part], inter[r : r + part]], 1)
        for x in range(NX):
            for half in range(2):
                places = range(half * NZ // 2, (half + 1) * NZ // 2)
                starts = [(z * NX + x) * shard for z in places]
                out[2 * x + half, r : r + part] = jnp.concatenate(
                    [features[:, s : s + shard] for s in starts], 1
                )


def regroup(encoded, inter, shard):
    dims = (2 * NX, encoded.shape[0], NZ // 2 * shard)
    return call(functools.partial(regroup_body, shard), shape(dims), [], [encoded, inter])


def relay_body(tile_len, owners, encoded, inter, weight, out, features, table, total, sems):
    split = encoded.shape[1]
    steps = weight.shape[0] // split
    copies = []
    for k in range(steps):
        rows = pl.ds(k * split, split)
        source = encoded if k == 0 else inter.at[:, pl.ds((k - 1) * split, split)]
        copies.append(pltpu.make_async_copy(source, features.at[k], sems.at[2 * k]))
        copies.append(pltpu.make_async_copy(weight.at[rows], table.at[k], sems.at[2 * k + 1]))
    for copy in copies:
        copy.start()
    out[...] = jnp.zeros_like(out)
    for k in range(steps):
        copies[2 * k].wait()
        copies[2 * k + 1].wait()
        if k == 0:
            total[...] = dot(features[k], table[k])
        else:
            total[...] += dot(features[k], table[k])
    keys = rms_scale(total[:, :HD], 1e-06)
    tokens = jnp.concatenate([keys, total[:, HD:]], 1).astype(BF)
    for q in range(BLOCK):
        owner = owners[q]

        @pl.when(owner >= 0)
        def _(q=q, owner=owner):
            out[owner] = tokens[q * tile_len : (q + 1) * tile_len]


def relay_rows(owners, encoded, inter, weight, after):
    rows, split = encoded.shape
    tile_len = rows // BLOCK
    width = weight.shape[1]
    steps = weight.shape[0] // split
    return call(
        functools.partial(relay_body, tile_len),
        shape((NIMG, tile_len, KVW)),
        [owners],
        [encoded, inter, weight],
        after,
        scratch=[
            pltpu.VMEM((steps, rows, split), BF),
            pltpu.VMEM((steps, split, width), BF),
            pltpu.VMEM((rows, width), F32),
            pltpu.SemaphoreType.DMA((2 * steps,)),
        ],
        space=pltpu.HBM,
    )


def query_body(hot, hidden, weight, out):
    out[...] = dot(dot(hot[...], hidden[...]).astype(BF), weight[...]).astype(BF).reshape(out.shape)


def query_part(hot, hidden, weight, after):
    out = shape((NIMG, CAP, weight.shape[1]))
    return call(query_body, out, [], [hot, hidden, weight], after)


def normed_body(parts, out):
    total = jnp.sum(parts[...].astype(F32), 0)
    for g in range(GROUP):
        out[g] = rms_scale(total[:, g * HD : (g + 1) * HD], 1e-06)


def normed_queries(parts):
    return call(normed_body, shape((GROUP, CAP, HD), F32), [], [parts])


def decode_body(info, arrived, queries, cache, attended):
    groups = NIMG // TILES
    tile_len = arrived.shape[1]
    length = TILES * tile_len
    results = []
    for c in range(CAP):
        block, present, count = info[0, c], info[1, c] > 0, info[2, c]
        for j in range(TILES):
            rows = arrived[j * groups + block]
            cache[c, j * tile_len : (j + 1) * tile_len, :] = jnp.where(
                present, rows, jnp.zeros_like(rows)
            )
        keys, values = cache[c, :, :HD], cache[c, :, HD:]
        heads = jnp.concatenate([queries[g, c : c + 1] for g in range(GROUP)], 0).astype(BF)
        scores = lax.dot_general(
            heads, keys, (((1,), (1,)), ((), ())), preferred_element_type=F32
        ) / math.sqrt(HD)
        tile = lax.broadcasted_iota(I32, (GROUP, length), 1) // tile_len
        weights = jnp.where(tile < count, jnp.exp(scores), 0.0).astype(BF)
        totals = jnp.sum(weights.astype(F32), -1, keepdims=True)
        result = dot(weights, values) / totals
        results.append(jnp.where(present, result, jnp.zeros_like(result)))
    for g in range(GROUP):
        column = jnp.concatenate([r[g : g + 1] for r in results], 0)
        attended[:, g * HD : (g + 1) * HD] = column.astype(BF)


def decode(info, arrived, queries):
    outs = [shape((CAP, TILES * arrived.shape[1], KVW)), shape((CAP, GROUP * HD))]
    return call(decode_body, outs, [info], [arrived, queries])


def near_body(x, feats, own, left, right, out):
    mid = own.shape[0] // 2
    here, before, after = ((x[0] + step) % NX * 2 for step in HOPS[:3])
    out[...] = dot(feats[here], own[:mid]) + dot(feats[here + 1], own[mid:])
    out[...] += dot(feats[before], left[...]) + dot(feats[after + 1], right[...])


def near_sum(x, feats, weights):
    dims = (feats.shape[1], weights[0].shape[1])
    return call(near_body, shape(dims, F32), [x], [feats, *weights])


def last_body(x, near, feats, left, right, first, second, out, places, sems):
    copies = [
        pltpu.make_async_copy(w, places.at[k], sems.at[k])
        for k, w in enumerate((left, right, first, second))
    ]
    for copy in copies:
        copy.start()
    before, after, across = ((x[0] + step) % NX * 2 for step in HOPS[1:])
    total = near[...]
    for k, row in enumerate((before + 1, after, across, across + 1)):
        copies[k].wait()
        total = total + dot(feats[row], places[k])
    out[...] = total.astype(BF)


def last_sum(x, near, feats, weights):
    dims = near.shape
    smem, vmem, hbm = (
        pl.BlockSpec(memory_space=space) for space in (pltpu.SMEM, pltpu.VMEM, pltpu.HBM)
    )
    return pl.pallas_call(
        last_body,
        in_specs=[smem, vmem, vmem] + [hbm] * 4,
        out_specs=vmem,
        out_shape=shape(dims),
        scratch_shapes=[
            pltpu.VMEM((4,) + weights[0].shape, BF),
            pltpu.SemaphoreType.DMA((4,)),
        ],
        compiler_params=pltpu.CompilerParams(vmem_limit_bytes=VMEM_LIMIT),
        cost_estimate=pl.CostEstimate(
            flops=LAST_COST, bytes_accessed=LAST_COST, transcendentals=0
        ),
    )(x, near, feats, *weights)


def per_device(
    vision_tokens,
    inter_feats,
    fc1_weight,
    fc2_weight,
    proj_weight,
    kv_weight,
    tile_counts,
    owner_map,
    decode_hidden,
    query_weight,
):
    zi, xi = lax.axis_index("z"), lax.axis_index("x")
    yi, ci = lax.axis_index("y"), lax.axis_index("c")
    img_index = zi * NX + xi
    core = ci.astype(I32)[None]
    column = xi.astype(I32)[None]
    there = yi.astype(I32)[None]
    rows, width = vision_tokens.shape
    shard = proj_weight.shape[0]
    tile_len = rows // BLOCK
    requests = tile_counts.shape[0]

    late = lax.all_gather(proj_weight, "z", axis=0, tiled=True)
    mid = late.shape[0] // 2
    left_first, right_second = shift(late[:mid], "x", 1), shift(late[mid:], "x", -1)
    left_second, right_first = shift(late[mid:], "x", 1), shift(late[:mid], "x", -1)
    far = [shift(left_first, "x", 1), shift(right_second, "x", -1)]

    fold_send, fold_keep = fold_weights(core, proj_weight, kv_weight)
    *fold_parts, fold_own = half_sums(there, shift(fold_send, "c", 1), fold_keep)

    send, keep = layer(core, vision_tokens, fc1_weight.T, fc2_weight, [tick(fold_send)])
    *parts, total = half_sums(there, shift(send, "c", 1), keep, [tick(fold_parts[0])])

    fold_parts = [shift(p, "y", step) for step, p in zip((1, -1, 2), fold_parts)]
    joined = join(fold_own, fold_parts, [tick(parts[0])])

    parts = [shift(p, "y", step) for step, p in zip((1, -1, 2), parts)]
    place_here = (ci * NY + yi).astype(I32)[None]
    piece = encoded_piece(place_here, total, parts, vision_tokens, [tick(joined)])
    pieces = place(jnp.zeros((NY,) + piece.shape, BF), piece, yi, 0)
    for step in (1, -1, 2):
        pieces = place(pieces, shift(piece, "y", step), (yi - step) % NY, 0)
    pieces = pieces.reshape(rows // 2, width)
    other = shift(pieces, "c", 1)
    encoded = jnp.concatenate(
        [jnp.where(ci == 0, pieces, other), jnp.where(ci == 0, other, pieces)], 0
    )

    block = [joined, *(shift(joined, "x", step) for step in (1, -1, 2))]
    block = in_order(column, block, [tick(late)]).reshape(NX * shard, -1)
    early = lax.all_gather(block, "z", axis=0, tiled=True)

    request_ids = jnp.arange(requests, dtype=I32)
    same_owner = owner_map[:, None] == owner_map[None, :]
    earlier = same_owner & (request_ids[None, :] < request_ids[:, None])
    slot_rank = jnp.sum(earlier.astype(I32), 1)
    slot_match = (owner_map[None, :] == img_index) & (
        slot_rank[None, :] == jnp.arange(CAP, dtype=I32)[:, None]
    )
    present = jnp.any(slot_match, 1)
    request_of = jnp.sum(jnp.where(slot_match, request_ids[None, :], 0), 1)
    count_of = jnp.where(
        present, jnp.sum(jnp.where(slot_match, tile_counts[None, :], 0), 1), 1
    )
    info = jnp.stack([request_of // BLOCK, present.astype(I32), count_of])

    slot_row = jnp.arange(NIMG * CAP, dtype=I32)
    slot_hot = (owner_map[None, :] == (slot_row // CAP)[:, None]) & (
        slot_rank[None, :] == (slot_row % CAP)[:, None]
    )
    partial = query_part(slot_hot.astype(BF), decode_hidden, query_weight, [tick(encoded)])
    queries = normed_queries(lax.all_to_all(partial, ("z", "x"), 0, 0, tiled=True))

    feats = regroup(encoded, inter_feats, shard)
    tile_here, block_here = img_index // NZ, img_index % NZ
    owners_here = lax.dynamic_slice_in_dim(owner_map, block_here * BLOCK, BLOCK)
    counts_here = lax.dynamic_slice_in_dim(tile_counts, block_here * BLOCK, BLOCK)
    targets = jnp.where(tile_here < counts_here, owners_here, -1)
    outgoing = relay_rows(
        targets, encoded, inter_feats, early, [tick(feats), queries]
    )
    arrived = lax.all_to_all(outgoing, ("z", "x"), 0, 0, tiled=True)
    kv_cache, attended = decode(info, arrived, queries)

    near = near_sum(column, feats, [late, left_first, right_second])
    vision_states = last_sum(column, near, feats, [left_second, right_first, *far])
    return (vision_states, kv_cache, attended)


def solution(mesh):
    img, tp = ("z", "x"), ("y", "c")
    fine = Mesh(mesh.devices.reshape(NZ, NX, NY, NC), img + tp)
    return jax.shard_map(
        per_device,
        mesh=fine,
        in_specs=(
            P(img, None),
            P(img, None),
            P(None, tp),
            P(tp, None),
            P(img, tp),
            P(tp, None),
            P(),
            P(),
            P(None, img),
            P(img, tp),
        ),
        out_specs=(P(img, tp), P(img, None, tp), P(img, tp)),
        check_vma=False,
    )
```

profile of v0, /device:TPU:2, one launch (start us, length us, event | category | flops | bytes accessed | tf_op | source)
XLA Modules:
  0.0 168.0 jit_solution(2726866144346291434)
XLA Ops:
  7.2 0.7 all-gather.3.cloned.1.call-update
  8.0 2.2 %copy-done.6 = bf16[1024,2048]{1,0:T(8,128)(2,1)S(1)} copy-done((bf16[1024,2048]{1,0:T(8,128)(2,1)S(1)}, bf16[1024,2048]{1,0:T(8,128)(2,1)}, u32[]{:S(2)}) %copy-start.6) | copy-done | bytes 4194328
  10.1 0.9 copy-done.9
  11.1 1.4 shard_map.121
  12.5 0.7 slice.38.refs_4_
  13.2 2.4 %shard_map.122 = (bf16[4,64,1280]{2,1,0:T(8,128)(2,1)}, f32[4,64,1280]{2,1,0:T(8,128)S(1)}) custom-call(s32[1]{0:T(128)} %bitcast.3.refs_0_, bf16[512,1280]{1,0:T(8,128)(2,1)S(1)} %copy-done.5, bf16[320,1280]{1,0:T(8,128)(2,1)S(1)} %bitcast.32, bf16[320,1280]{1,0:T(8,128)(2,1)S(1)} %copy-done.11, bf16[8,128]{1,0:T(8,128)(2,1)S(1)} %slice.38.refs_4_), custom_call_target="tpu_custom_call" | custom-call | flops 1 | bytes 1 | tf_op jit(solution)/shard_map/pallas_call | solution.py:68
  15.6 0.5 collective-permute-start.1
  16.1 2.1 %collective-permute-done.1.refs_1_ = bf16[4,120,256]{2,1,0:T(8,128)(2,1)S(1)} collective-permute-done((bf16[4,120,256]{2,1,0:T(8,128)(2,1)}, bf16[4,120,256]{2,1,0:T(8,128)(2,1)S(1)}, u32[]{:S(2)}, u32[]{:S(2)}) %collective-permute-start.1) | collective-permute-done | bytes 245792 | tf_op jit(solution)/shard_map/ppermute | solution.py:33
  18.3 1.0 copy-done.14
  19.3 0.7 shard_map.123
  20.0 0.8 shard_map.124
  20.9 0.7 copy-done.15
  21.6 1.6 collective-permute-start.2
  23.1 1.7 collective-permute-start.3
  24.8 2.0 %collective-permute-start.4 = (bf16[64,1280]{1,0:T(8,128)(2,1)}, bf16[64,1280]{1,0:T(8,128)(2,1)S(1)}, u32[]{:S(2)}, u32[]{:S(2)}) collective-permute-start(bf16[64,1280]{1,0:T(8,128)(2,1)} %get-tuple-element.25), channel_id=1, source_target_pairs={{0,4},{2,6},{4,0},{6,2},{1,5},{3,7},{5,1},{7,3},{8,12},{10,14},{12... | collective-permute-start | bytes 491528 | tf_op jit(solution)/shard_map/ppermute | solution.py:33
  26.8 0.7 collective-permute-start.5
  27.5 2.6 %collective-permute-start.6 = (bf16[120,256]{1,0:T(8,128)(2,1)}, bf16[120,256]{1,0:T(8,128)(2,1)S(1)}, u32[]{:S(2)}, u32[]{:S(2)}) collective-permute-start(bf16[120,256]{1,0:T(8,128)(2,1)} %get-tuple-element.27), channel_id=1, source_target_pairs={{0,6},{2,0},{4,2},{6,4},{1,7},{3,1},{5,3},{7,5},{8,14},{10,8},{12,... | collective-permute-start | bytes 184328 | tf_op jit(solution)/shard_map/ppermute | solution.py:33
  30.0 4.5 %collective-permute-done.5.refs_1_ = bf16[120,256]{1,0:T(8,128)(2,1)S(1)} collective-permute-done((bf16[120,256]{1,0:T(8,128)(2,1)S(1)}, bf16[120,256]{1,0:T(8,128)(2,1)S(1)}, u32[]{:S(2)}, u32[]{:S(2)}) %collective-permute-start.5) | collective-permute-done | bytes 61472 | tf_op jit(solution)/shard_map/ppermute | solution.py:33
  34.5 1.3 collective-permute-start.7
  35.8 4.6 %collective-permute-done.7.refs_3_ = bf16[120,256]{1,0:T(8,128)(2,1)S(1)} collective-permute-done((bf16[120,256]{1,0:T(8,128)(2,1)}, bf16[120,256]{1,0:T(8,128)(2,1)S(1)}, u32[]{:S(2)}, u32[]{:S(2)}) %collective-permute-start.7) | collective-permute-done | bytes 61472 | tf_op jit(solution)/shard_map/ppermute | solution.py:33
  40.4 0.9 copy-done.18
  41.4 1.6 collective-permute-start.18
  43.0 0.5 collective-permute-start.19
  43.5 2.1 %collective-permute-start.20 = (bf16[120,256]{1,0:T(8,128)(2,1)S(1)}, bf16[120,256]{1,0:T(8,128)(2,1)S(1)}, u32[]{:S(2)}, u32[]{:S(2)}) collective-permute-start(bf16[120,256]{1,0:T(8,128)(2,1)S(1)} %shard_map.125.refs_1_), channel_id=1, source_target_pairs={{0,16},{8,24},{16,0},{24,8},{1,17},{9,25},{17,1},{25,9},{2,18},{10... | collective-permute-start | bytes 184328 | tf_op jit(solution)/shard_map/ppermute | solution.py:33
  45.6 1.0 copy-done.16
  46.8 3.2 %collective-permute-start.9 = (bf16[64,1280]{1,0:T(8,128)(2,1)S(1)}, bf16[64,1280]{1,0:T(8,128)(2,1)S(1)}, u32[]{:S(2)}, u32[]{:S(2)}) collective-permute-start(bf16[64,1280]{1,0:T(8,128)(2,1)S(1)} %shard_map.126), channel_id=1, source_target_pairs={{0,6},{2,0},{4,2},{6,4},{1,7},{3,1},{5,3},{7,5},{8,14},{10,8},{12,... | collective-permute-start | bytes 491528 | tf_op jit(solution)/shard_map/ppermute | solution.py:33
  50.1 3.6 %all-gather.3.cloned.1.call-done.refs_2_ = bf16[960,1024]{1,0:T(8,128)(2,1)} async-done(((bf16[120,1024]{1,0:T(8,128)(2,1)}), bf16[960,1024]{1,0:T(8,128)(2,1)}) %all-gather.3.cloned.1.call-update) | async-done | bytes 1966096 | tf_op jit(solution)/shard_map/all_gather | solution.py:352
  53.7 0.7 slice.42.refs_5_
  54.4 3.0 %collective-permute-start.10 = (bf16[64,1280]{1,0:T(8,128)(2,1)S(1)}, bf16[64,1280]{1,0:T(8,128)(2,1)S(1)}, u32[]{:S(2)}, u32[]{:S(2)}) collective-permute-start(bf16[64,1280]{1,0:T(8,128)(2,1)S(1)} %shard_map.126), channel_id=1, source_target_pairs={{0,4},{2,6},{4,0},{6,2},{1,5},{3,7},{5,1},{7,3},{8,12},{10,14},{12... | collective-permute-start | bytes 491528 | tf_op jit(solution)/shard_map/ppermute | solution.py:33
  57.4 0.7 shard_map.130
  58.2 3.0 %collective-permute-done.10 = bf16[64,1280]{1,0:T(8,128)(2,1)S(1)} collective-permute-done((bf16[64,1280]{1,0:T(8,128)(2,1)S(1)}, bf16[64,1280]{1,0:T(8,128)(2,1)S(1)}, u32[]{:S(2)}, u32[]{:S(2)}) %collective-permute-start.10) | collective-permute-done | bytes 163872 | tf_op jit(solution)/shard_map/ppermute | solution.py:33
  61.4 0.2 convert_reduce_fusion
  61.5 0.1 and_convert_fusion.refs_0_
  61.7 1.9 %collective-permute-done.11 = bf16[256,1280]{1,0:T(8,128)(2,1)} collective-permute-done((bf16[256,1280]{1,0:T(8,128)(2,1)S(1)}, bf16[256,1280]{1,0:T(8,128)(2,1)}, u32[]{:S(2)}, u32[]{:S(2)}) %collective-permute-start.11) | collective-permute-done | bytes 655392 | tf_op jit(solution)/shard_map/ppermute | solution.py:33
  63.6 2.2 %broadcast_select_fusion.1 = (bf16[256,1280]{1,0:T(8,128)(2,1)}, bf16[256,1280]{1,0:T(8,128)(2,1)}) fusion(bf16[256,1280]{1,0:T(8,128)(2,1)} %collective-permute-done.11, pred[]{:T(512)S(6)} %eq.70, bf16[4,64,1280]{2,1,0:T(8,128)(2,1)S(1)} %bitcast_dynamic-update-slice_fusion), kind=kLoop, calls=%fused_computation.2 | loop fusion | flops 655360 | bytes 2621441 | tf_op jit(solution)/shard_map/jit(_where)/select_n | solution.py:376
  65.8 0.7 slice.44.refs_3_
  66.5 1.2 shard_map.131
  67.7 7.7 %all-to-all-start = ((bf16[32,8,1024]{2,1,0:T(8,128)(2,1)}), bf16[32,8,1024]{2,1,0:T(8,128)(2,1)}, u32[]{:S(2)}, u32[]{:S(2)}) async-start(bf16[32,8,1024]{2,1,0:T(8,128)(2,1)} %shard_map.131), calls=%async_computation | async-start | bytes 1048576 | tf_op jit(solution)/shard_map/all_to_all | solution.py:402
  75.4 1.4 fusion.5
  76.8 1.5 collective-permute-start.12
  78.3 0.6 collective-permute-start.13
  78.9 1.4 pad_maximum_fusion.refs_0_.refs_1_
  80.3 1.7 %copy-done.2 = bf16[512,2560]{1,0:T(8,128)(2,1)S(1)} copy-done((bf16[512,2560]{1,0:T(8,128)(2,1)S(1)}, bf16[512,2560]{1,0:T(8,128)(2,1)}, u32[]{:S(2)}) %copy-start.2) | copy-done | bytes 2621464
  82.0 1.8 %shard_map.127.refs_1_.feats = bf16[8,512,480]{2,1,0:T(8,128)(2,1)S(1)} custom-call(bf16[512,1280]{1,0:T(8,128)(2,1)S(1)} %pad_maximum_fusion.refs_0_.refs_1_, bf16[512,2560]{1,0:T(8,128)(2,1)S(1)} %copy-done.2), custom_call_target="tpu_custom_call" | custom-call | flops 1 | bytes 1 | tf_op jit(solution)/shard_map/pallas_call | solution.py:68
  83.9 1.9 %copy-done = bf16[8,512,480]{2,1,0:T(8,128)(2,1)} copy-done((bf16[8,512,480]{2,1,0:T(8,128)(2,1)}, bf16[8,512,480]{2,1,0:T(8,128)(2,1)S(1)}, u32[]{:S(2)}) %copy-start) | copy-done | bytes 3932184
  85.8 12.7 %all-to-all-done.refs_0_ = bf16[32,8,1024]{2,1,0:T(8,128)(2,1)} async-done(((bf16[32,8,1024]{2,1,0:T(8,128)(2,1)}), bf16[32,8,1024]{2,1,0:T(8,128)(2,1)}, u32[]{:S(2)}, u32[]{:S(2)}) %all-to-all-start) | async-done | bytes 524320 | tf_op jit(solution)/shard_map/all_to_all | solution.py:402
  98.5 1.2 shard_map.132.refs_5_.refs_2_
  99.7 1.4 collective-permute-start.14
  101.1 0.7 collective-permute-start.15
  101.8 4.3 %collective-permute-done.12.refs_3_ = bf16[480,1024]{1,0:T(8,128)(2,1)} collective-permute-done((bf16[480,1024]{1,0:T(8,128)(2,1)}, bf16[480,1024]{1,0:T(8,128)(2,1)}, u32[]{:S(2)}, u32[]{:S(2)}) %collective-permute-start.12) | collective-permute-done | bytes 983072 | tf_op jit(solution)/shard_map/ppermute | solution.py:33
  106.2 1.5 collective-permute-start.16
  107.6 0.6 collective-permute-start.17
  108.2 1.7 %copy-done.3 = bf16[512,2560]{1,0:T(8,128)(2,1)S(1)} copy-done((bf16[512,2560]{1,0:T(8,128)(2,1)S(1)}, bf16[512,2560]{1,0:T(8,128)(2,1)}, u32[]{:S(2)}) %copy-start.3) | copy-done | bytes 2621464
  109.9 1.5 copy-done.8
  111.5 3.7 %shard_map.133 = bf16[32,32,256]{2,1,0:T(8,128)(2,1)S(1)} custom-call(s32[16]{0:T(128)S(1)} %compare_select_fusion.refs_0_, bf16[512,1280]{1,0:T(8,128)(2,1)S(1)} %pad_maximum_fusion.refs_0_.refs_1_, bf16[512,2560]{1,0:T(8,128)(2,1)S(1)} %copy-done.3, bf16[3840,256]{1,0:T(8,128)(2,1)S(1)} %copy-done.8, bf16[8,128]{1,0:T(8,128)(2,1)S(1)} %slice.43.refs_4_, ...), custom_call_target="tpu_custom_call" | custom-call | flops 1 | bytes 1 | tf_op jit(solution)/shard_map/pallas_call | solution.py:68
  115.2 0.8 copy-done.7
  116.0 9.4 %all-to-all-start.1 = ((bf16[32,32,256]{2,1,0:T(8,128)(2,1)}), bf16[32,32,256]{2,1,0:T(8,128)(2,1)S(1)}, u32[]{:S(2)}, u32[]{:S(2)}) async-start(bf16[32,32,256]{2,1,0:T(8,128)(2,1)} %copy-done.7), calls=%async_computation.1 | async-start | bytes 1048576 | tf_op jit(solution)/shard_map/all_to_all | solution.py:412
  125.6 0.1 select_reduce_fusion.1
  125.8 2.2 %copy-done.1 = bf16[8,512,480]{2,1,0:T(8,128)(2,1)S(1)} copy-done((bf16[8,512,480]{2,1,0:T(8,128)(2,1)S(1)}, bf16[8,512,480]{2,1,0:T(8,128)(2,1)}, u32[]{:S(2)}) %copy-start.1) | copy-done | bytes 3932184
  128.0 3.8 %shard_map.128.near = f32[512,1024]{1,0:T(8,128)S(1)} custom-call(s32[1]{0:T(128)} %bitcast.refs_0_.x, bf16[8,512,480]{2,1,0:T(8,128)(2,1)S(1)} %copy-done.1, bf16[960,1024]{1,0:T(8,128)(2,1)S(1)} %copy-done.4, bf16[480,1024]{1,0:T(8,128)(2,1)} %collective-permute-done.12.refs_3_, bf16[480,1024]{1,0:T(8,128)(2,1)} %collective-permute-done.13.refs_4_), custom_call_target="tpu_custom_call" | custom-call | flops 1 | bytes 1 | tf_op jit(solution)/shard_map/pallas_call | solution.py:68
  131.8 20.4 %collective-permute-done.16.first = bf16[480,1024]{1,0:T(8,128)(2,1)} collective-permute-done((bf16[480,1024]{1,0:T(8,128)(2,1)}, bf16[480,1024]{1,0:T(8,128)(2,1)}, u32[]{:S(2)}, u32[]{:S(2)}) %collective-permute-start.16) | collective-permute-done | bytes 983072 | tf_op jit(solution)/shard_map/ppermute | solution.py:33
  152.2 1.7 collective-permute-done.17.second
  153.9 4.7 %shard_map.129 = bf16[512,1024]{1,0:T(8,128)(2,1)} custom-call(s32[1]{0:T(128)} %bitcast.refs_0_.x, f32[512,1024]{1,0:T(8,128)S(1)} %shard_map.128.near, bf16[8,512,480]{2,1,0:T(8,128)(2,1)S(1)} %copy-done.1, bf16[480,1024]{1,0:T(8,128)(2,1)} %collective-permute-done.14.left, bf16[480,1024]{1,0:T(8,128)(2,1)} %collective-permute-done.15.right, ...), custom_call_target="tpu_custom_call" | custom-call | flops 100000000 | bytes 100000000 | tf_op jit(solution)/shard_map/pallas_call | solution.py:313
  158.6 2.6 %shard_map.134 = (bf16[8,128,256]{2,1,0:T(8,128)(2,1)}, bf16[8,1024]{1,0:T(8,128)(2,1)}) custom-call(s32[3,8]{1,0:T(4,128)S(1)} %pad_add_fusion.refs_0_, bf16[32,32,256]{2,1,0:T(8,128)(2,1)S(1)} %all-to-all-done.1.refs_1_, f32[8,8,128]{2,1,0:T(8,128)S(1)} %shard_map.132.refs_5_.refs_2_), custom_call_target="tpu_custom_call" | custom-call | flops 1 | bytes 1 | tf_op jit(solution)/shard_map/pallas_call | solution.py:68
  (72 shorter events, 0.9 us)
Async XLA Ops:
  7.2 46.6 %all-gather.3.cloned.1.call-start = ((), (), s32[]{:S(2)}) async-start(), calls=%async_computation.2 | async-start | bytes 2211840 | tf_op jit(solution)/shard_map/all_gather | solution.py:352
  7.9 100.3 %all-gather.5.cloned.1.call-start = ((), (), s32[]{:S(2)}) async-start(), calls=%async_computation.3 | async-start | bytes 2211840 | tf_op jit(solution)/shard_map/all_gather | solution.py:381
  8.0 2.2 %copy-start.6 = (bf16[1024,2048]{1,0:T(8,128)(2,1)S(1)}, bf16[1024,2048]{1,0:T(8,128)(2,1)}, u32[]{:S(2)}) copy-start(bf16[1024,2048]{1,0:T(8,128)(2,1)} %refs_2_.3) | copy-start | bytes 12582916
  10.1 0.9 copy-start.9
  11.1 2.1 %copy-start.5 = (bf16[512,1280]{1,0:T(8,128)(2,1)S(1)}, bf16[512,1280]{1,0:T(8,128)(2,1)}, u32[]{:S(2)}) copy-start(bf16[512,1280]{1,0:T(8,128)(2,1)} %refs_5_.1) | copy-start | bytes 3932164
  11.1 2.1 %copy-start.10 = (bf16[1280,320]{0,1:T(8,128)(2,1)S(1)}, bf16[1280,320]{0,1:T(8,128)(2,1)}, u32[]{:S(2)}) copy-start(bf16[1280,320]{0,1:T(8,128)(2,1)} %param.12) | copy-start | bytes 2457604
  11.1 2.1 %copy-start.11 = (bf16[320,1280]{1,0:T(8,128)(2,1)S(1)}, bf16[320,1280]{1,0:T(8,128)(2,1)}, u32[]{:S(2)}) copy-start(bf16[320,1280]{1,0:T(8,128)(2,1)} %refs_3_.1) | copy-start | bytes 2457604
  12.5 3.1 %copy-start.13 = (f32[4,120,256]{2,1,0:T(8,128)}, f32[4,120,256]{2,1,0:T(8,128)S(1)}, u32[]{:S(2)}) copy-start(f32[4,120,256]{2,1,0:T(8,128)S(1)} %get-tuple-element.20.refs_2_) | copy-start | bytes 1474564
  15.6 4.4 %collective-permute-start = (bf16[4,64,1280]{2,1,0:T(8,128)(2,1)}, bf16[4,64,1280]{2,1,0:T(8,128)(2,1)S(1)}, u32[]{:S(2)}, u32[]{:S(2)}) collective-permute-start(bf16[4,64,1280]{2,1,0:T(8,128)(2,1)} %get-tuple-element.18), channel_id=1, source_target_pairs={{0,1},{1,0},{2,3},{3,2},{4,5},{5,4},{6,7},{7,6},{8,9},{9,8},{10,11... | collective-permute-start | bytes 1966088 | tf_op jit(solution)/shard_map/ppermute | solution.py:33
  15.6 2.7 %collective-permute-start.1 = (bf16[4,120,256]{2,1,0:T(8,128)(2,1)}, bf16[4,120,256]{2,1,0:T(8,128)(2,1)S(1)}, u32[]{:S(2)}, u32[]{:S(2)}) collective-permute-start(bf16[4,120,256]{2,1,0:T(8,128)(2,1)} %get-tuple-element.17), channel_id=1, source_target_pairs={{0,1},{1,0},{2,3},{3,2},{4,5},{5,4},{6,7},{7,6},{8,9},{9,8},{10,11... | collective-permute-start | bytes 737288 | tf_op jit(solution)/shard_map/ppermute | solution.py:33
  18.3 1.0 copy-start.14
  20.0 4.8 %copy-start.17 = (f32[120,256]{1,0:T(8,128)}, f32[120,256]{1,0:T(8,128)S(1)}, u32[]{:S(2)}) copy-start(f32[120,256]{1,0:T(8,128)S(1)} %get-tuple-element.26.refs_0_) | copy-start | bytes 368644
  20.9 0.7 copy-start.15
  21.6 21.9 %collective-permute-start.2 = (bf16[64,1280]{1,0:T(8,128)(2,1)S(1)}, bf16[64,1280]{1,0:T(8,128)(2,1)S(1)}, u32[]{:S(2)}, u32[]{:S(2)}) collective-permute-start(bf16[64,1280]{1,0:T(8,128)(2,1)S(1)} %get-tuple-element.23), channel_id=1, source_target_pairs={{0,2},{2,4},{4,6},{6,0},{1,3},{3,5},{5,7},{7,1},{8,10},{10,12},{12... | collective-permute-start | bytes 491528 | tf_op jit(solution)/shard_map/ppermute | solution.py:33
  23.1 22.5 %collective-permute-start.3 = (bf16[64,1280]{1,0:T(8,128)(2,1)}, bf16[64,1280]{1,0:T(8,128)(2,1)S(1)}, u32[]{:S(2)}, u32[]{:S(2)}) collective-permute-start(bf16[64,1280]{1,0:T(8,128)(2,1)} %get-tuple-element.24), channel_id=1, source_target_pairs={{0,6},{2,0},{4,2},{6,4},{1,7},{3,1},{5,3},{7,5},{8,14},{10,8},{12,... | collective-permute-start | bytes 491528 | tf_op jit(solution)/shard_map/ppermute | solution.py:33
  24.8 20.8 %collective-permute-start.4 = (bf16[64,1280]{1,0:T(8,128)(2,1)}, bf16[64,1280]{1,0:T(8,128)(2,1)S(1)}, u32[]{:S(2)}, u32[]{:S(2)}) collective-permute-start(bf16[64,1280]{1,0:T(8,128)(2,1)} %get-tuple-element.25), channel_id=1, source_target_pairs={{0,4},{2,6},{4,0},{6,2},{1,5},{3,7},{5,1},{7,3},{8,12},{10,14},{12... | collective-permute-start | bytes 491528 | tf_op jit(solution)/shard_map/ppermute | solution.py:33
  26.8 7.7 %collective-permute-start.5 = (bf16[120,256]{1,0:T(8,128)(2,1)S(1)}, bf16[120,256]{1,0:T(8,128)(2,1)S(1)}, u32[]{:S(2)}, u32[]{:S(2)}) collective-permute-start(bf16[120,256]{1,0:T(8,128)(2,1)S(1)} %get-tuple-element.21), channel_id=1, source_target_pairs={{0,2},{2,4},{4,6},{6,0},{1,3},{3,5},{5,7},{7,1},{8,10},{10,12},{12... | collective-permute-start | bytes 184328 | tf_op jit(solution)/shard_map/ppermute | solution.py:33
  27.5 8.4 %collective-permute-start.6 = (bf16[120,256]{1,0:T(8,128)(2,1)}, bf16[120,256]{1,0:T(8,128)(2,1)S(1)}, u32[]{:S(2)}, u32[]{:S(2)}) collective-permute-start(bf16[120,256]{1,0:T(8,128)(2,1)} %get-tuple-element.27), channel_id=1, source_target_pairs={{0,6},{2,0},{4,2},{6,4},{1,7},{3,1},{5,3},{7,5},{8,14},{10,8},{12,... | collective-permute-start | bytes 184328 | tf_op jit(solution)/shard_map/ppermute | solution.py:33
  34.5 5.9 %collective-permute-start.7 = (bf16[120,256]{1,0:T(8,128)(2,1)}, bf16[120,256]{1,0:T(8,128)(2,1)S(1)}, u32[]{:S(2)}, u32[]{:S(2)}) collective-permute-start(bf16[120,256]{1,0:T(8,128)(2,1)} %get-tuple-element.28), channel_id=1, source_target_pairs={{0,4},{2,6},{4,0},{6,2},{1,5},{3,7},{5,1},{7,3},{8,12},{10,14},{12... | collective-permute-start | bytes 184328 | tf_op jit(solution)/shard_map/ppermute | solution.py:33
  40.4 0.9 copy-start.18
  41.4 13.0 %collective-permute-start.18 = (bf16[120,256]{1,0:T(8,128)(2,1)S(1)}, bf16[120,256]{1,0:T(8,128)(2,1)S(1)}, u32[]{:S(2)}, u32[]{:S(2)}) collective-permute-start(bf16[120,256]{1,0:T(8,128)(2,1)S(1)} %shard_map.125.refs_1_), channel_id=1, source_target_pairs={{0,8},{8,16},{16,24},{24,0},{1,9},{9,17},{17,25},{25,1},{2,10},{10... | collective-permute-start | bytes 184328 | tf_op jit(solution)/shard_map/ppermute | solution.py:33
  43.0 14.5 %collective-permute-start.19 = (bf16[120,256]{1,0:T(8,128)(2,1)S(1)}, bf16[120,256]{1,0:T(8,128)(2,1)S(1)}, u32[]{:S(2)}, u32[]{:S(2)}) collective-permute-start(bf16[120,256]{1,0:T(8,128)(2,1)S(1)} %shard_map.125.refs_1_), channel_id=1, source_target_pairs={{0,24},{8,0},{16,8},{24,16},{1,25},{9,1},{17,9},{25,17},{2,26},{10... | collective-permute-start | bytes 184328 | tf_op jit(solution)/shard_map/ppermute | solution.py:33
  43.5 13.9 %collective-permute-start.20 = (bf16[120,256]{1,0:T(8,128)(2,1)S(1)}, bf16[120,256]{1,0:T(8,128)(2,1)S(1)}, u32[]{:S(2)}, u32[]{:S(2)}) collective-permute-start(bf16[120,256]{1,0:T(8,128)(2,1)S(1)} %shard_map.125.refs_1_), channel_id=1, source_target_pairs={{0,16},{8,24},{16,0},{24,8},{1,17},{9,25},{17,1},{25,9},{2,18},{10... | collective-permute-start | bytes 184328 | tf_op jit(solution)/shard_map/ppermute | solution.py:33
  45.6 1.0 copy-start.16
  46.6 14.8 %copy-start.20 = (s32[128]{0:T(128)S(1)}, s32[128]{0:T(128)}, u32[]{:S(2)}) copy-start(s32[128]{0:T(128)} %param.17) | copy-start | bytes 1540
  46.7 11.5 %collective-permute-start.8 = (bf16[64,1280]{1,0:T(8,128)(2,1)S(1)}, bf16[64,1280]{1,0:T(8,128)(2,1)S(1)}, u32[]{:S(2)}, u32[]{:S(2)}) collective-permute-start(bf16[64,1280]{1,0:T(8,128)(2,1)S(1)} %shard_map.126), channel_id=1, source_target_pairs={{0,2},{2,4},{4,6},{6,0},{1,3},{3,5},{5,7},{7,1},{8,10},{10,12},{12... | collective-permute-start | bytes 491528 | tf_op jit(solution)/shard_map/ppermute | solution.py:33
  46.8 11.4 %collective-permute-start.9 = (bf16[64,1280]{1,0:T(8,128)(2,1)S(1)}, bf16[64,1280]{1,0:T(8,128)(2,1)S(1)}, u32[]{:S(2)}, u32[]{:S(2)}) collective-permute-start(bf16[64,1280]{1,0:T(8,128)(2,1)S(1)} %shard_map.126), channel_id=1, source_target_pairs={{0,6},{2,0},{4,2},{6,4},{1,7},{3,1},{5,3},{7,5},{8,14},{10,8},{12,... | collective-permute-start | bytes 491528 | tf_op jit(solution)/shard_map/ppermute | solution.py:33
  54.4 6.8 %collective-permute-start.10 = (bf16[64,1280]{1,0:T(8,128)(2,1)S(1)}, bf16[64,1280]{1,0:T(8,128)(2,1)S(1)}, u32[]{:S(2)}, u32[]{:S(2)}) collective-permute-start(bf16[64,1280]{1,0:T(8,128)(2,1)S(1)} %shard_map.126), channel_id=1, source_target_pairs={{0,4},{2,6},{4,0},{6,2},{1,5},{3,7},{5,1},{7,3},{8,12},{10,14},{12... | collective-permute-start | bytes 491528 | tf_op jit(solution)/shard_map/ppermute | solution.py:33
  58.1 8.3 %copy-start.12 = (bf16[256,1024]{1,0:T(8,128)(2,1)S(1)}, bf16[256,1024]{1,0:T(8,128)(2,1)}, u32[]{:S(2)}) copy-start(bf16[256,1024]{1,0:T(8,128)(2,1)} %refs_2_.4) | copy-start | bytes 1572868
  58.1 8.3 %copy-start.19 = (bf16[128,256]{1,0:T(8,128)(2,1)S(1)}, bf16[128,256]{1,0:T(8,128)(2,1)}, u32[]{:S(2)}) copy-start(bf16[128,256]{1,0:T(8,128)(2,1)} %refs_1_.7) | copy-start | bytes 196612
  61.2 2.3 %collective-permute-start.11 = (bf16[256,1280]{1,0:T(8,128)(2,1)S(1)}, bf16[256,1280]{1,0:T(8,128)(2,1)}, u32[]{:S(2)}, u32[]{:S(2)}) collective-permute-start(bf16[256,1280]{1,0:T(8,128)(2,1)S(1)} %bitcast.33), channel_id=1, source_target_pairs={{0,1},{1,0},{2,3},{3,2},{4,5},{5,4},{6,7},{7,6},{8,9},{9,8},{10,11... | collective-permute-start | bytes 1966088 | tf_op jit(solution)/shard_map/ppermute | solution.py:33
  61.7 13.7 %copy-start.4 = (bf16[960,1024]{1,0:T(8,128)(2,1)S(1)}, bf16[960,1024]{1,0:T(8,128)(2,1)}, u32[]{:S(2)}) copy-start(bf16[960,1024]{1,0:T(8,128)(2,1)} %all-gather.3.cloned.1.call-done.refs_2_) | copy-start | bytes 5898244
  67.7 30.8 %all-to-all-start = ((bf16[32,8,1024]{2,1,0:T(8,128)(2,1)}), bf16[32,8,1024]{2,1,0:T(8,128)(2,1)}, u32[]{:S(2)}, u32[]{:S(2)}) async-start(bf16[32,8,1024]{2,1,0:T(8,128)(2,1)} %shard_map.131), calls=%async_computation | async-start | bytes 1048576 | tf_op jit(solution)/shard_map/all_to_all | solution.py:402
  75.4 3.5 %copy-start.21 = (s32[128]{0:T(128)S(1)}, s32[128]{0:T(128)}, u32[]{:S(2)}) copy-start(s32[128]{0:T(128)} %param.16) | copy-start | bytes 1540
  76.8 29.3 %collective-permute-start.12 = (bf16[480,1024]{1,0:T(8,128)(2,1)}, bf16[480,1024]{1,0:T(8,128)(2,1)}, u32[]{:S(2)}, u32[]{:S(2)}) collective-permute-start(bf16[480,1024]{1,0:T(8,128)(2,1)} %get-tuple-element.34), channel_id=1, source_target_pairs={{0,8},{8,16},{16,24},{24,0},{1,9},{9,17},{17,25},{25,1},{2,10},{10... | collective-permute-start | bytes 2949128 | tf_op jit(solution)/shard_map/ppermute | solution.py:33
  78.3 29.4 %collective-permute-start.13 = (bf16[480,1024]{1,0:T(8,128)(2,1)}, bf16[480,1024]{1,0:T(8,128)(2,1)}, u32[]{:S(2)}, u32[]{:S(2)}) collective-permute-start(bf16[480,1024]{1,0:T(8,128)(2,1)} %get-tuple-element.33), channel_id=1, source_target_pairs={{0,24},{8,0},{16,8},{24,16},{1,25},{9,1},{17,9},{25,17},{2,26},{10... | collective-permute-start | bytes 2949128 | tf_op jit(solution)/shard_map/ppermute | solution.py:33
  80.3 1.7 %copy-start.2 = (bf16[512,2560]{1,0:T(8,128)(2,1)S(1)}, bf16[512,2560]{1,0:T(8,128)(2,1)}, u32[]{:S(2)}) copy-start(bf16[512,2560]{1,0:T(8,128)(2,1)} %refs_2_.5) | copy-start | bytes 7864324
  83.9 2.0 %copy-start = (bf16[8,512,480]{2,1,0:T(8,128)(2,1)}, bf16[8,512,480]{2,1,0:T(8,128)(2,1)S(1)}, u32[]{:S(2)}) copy-start(bf16[8,512,480]{2,1,0:T(8,128)(2,1)S(1)} %shard_map.127.refs_1_.feats) | copy-start | bytes 11796484
  99.7 32.1 %collective-permute-start.14 = (bf16[480,1024]{1,0:T(8,128)(2,1)}, bf16[480,1024]{1,0:T(8,128)(2,1)}, u32[]{:S(2)}, u32[]{:S(2)}) collective-permute-start(bf16[480,1024]{1,0:T(8,128)(2,1)} %get-tuple-element.33), channel_id=1, source_target_pairs={{0,8},{8,16},{16,24},{24,0},{1,9},{9,17},{17,25},{25,1},{2,10},{10... | collective-permute-start | bytes 2949128 | tf_op jit(solution)/shard_map/ppermute | solution.py:33
  101.1 30.6 %collective-permute-start.15 = (bf16[480,1024]{1,0:T(8,128)(2,1)}, bf16[480,1024]{1,0:T(8,128)(2,1)}, u32[]{:S(2)}, u32[]{:S(2)}) collective-permute-start(bf16[480,1024]{1,0:T(8,128)(2,1)} %get-tuple-element.34), channel_id=1, source_target_pairs={{0,24},{8,0},{16,8},{24,16},{1,25},{9,1},{17,9},{25,17},{2,26},{10... | collective-permute-start | bytes 2949128 | tf_op jit(solution)/shard_map/ppermute | solution.py:33
  106.2 46.0 %collective-permute-start.16 = (bf16[480,1024]{1,0:T(8,128)(2,1)}, bf16[480,1024]{1,0:T(8,128)(2,1)}, u32[]{:S(2)}, u32[]{:S(2)}) collective-permute-start(bf16[480,1024]{1,0:T(8,128)(2,1)} %collective-permute-done.12.refs_3_), channel_id=1, source_target_pairs={{0,8},{8,16},{16,24},{24,0},{1,9},{9,17},{17,25},{25,1},{2,10},{10... | collective-permute-start | bytes 2949128 | tf_op jit(solution)/shard_map/ppermute | solution.py:33
  107.6 46.2 %collective-permute-start.17 = (bf16[480,1024]{1,0:T(8,128)(2,1)}, bf16[480,1024]{1,0:T(8,128)(2,1)}, u32[]{:S(2)}, u32[]{:S(2)}) collective-permute-start(bf16[480,1024]{1,0:T(8,128)(2,1)} %collective-permute-done.13.refs_4_), channel_id=1, source_target_pairs={{0,24},{8,0},{16,8},{24,16},{1,25},{9,1},{17,9},{25,17},{2,26},{10... | collective-permute-start | bytes 2949128 | tf_op jit(solution)/shard_map/ppermute | solution.py:33
  108.2 1.7 %copy-start.3 = (bf16[512,2560]{1,0:T(8,128)(2,1)S(1)}, bf16[512,2560]{1,0:T(8,128)(2,1)}, u32[]{:S(2)}) copy-start(bf16[512,2560]{1,0:T(8,128)(2,1)} %refs_2_.5) | copy-start | bytes 7864324
  109.9 1.5 copy-start.8
  115.2 0.8 copy-start.7
  116.0 42.5 %all-to-all-start.1 = ((bf16[32,32,256]{2,1,0:T(8,128)(2,1)}), bf16[32,32,256]{2,1,0:T(8,128)(2,1)S(1)}, u32[]{:S(2)}, u32[]{:S(2)}) async-start(bf16[32,32,256]{2,1,0:T(8,128)(2,1)} %copy-done.7), calls=%async_computation.1 | async-start | bytes 1048576 | tf_op jit(solution)/shard_map/all_to_all | solution.py:412
  125.8 2.2 %copy-start.1 = (bf16[8,512,480]{2,1,0:T(8,128)(2,1)S(1)}, bf16[8,512,480]{2,1,0:T(8,128)(2,1)}, u32[]{:S(2)}) copy-start(bf16[8,512,480]{2,1,0:T(8,128)(2,1)} %copy-done) | copy-start | bytes 11796484
Sparse Core Ops, SparseCore 0:
  9.8 43.8 all-gather.2
  58.3 45.8 all-gather.4
where the time goes:
time: 169 us; the launch traced here: 168 us
  waiting for transfers between devices  59.5 us (35%)
  starting transfers between devices  44.3 us (26%)
  Pallas kernels  25.2 us (15%)
  local copies, waits for them, and re-layouts  20.3 us (12%)
  between operations  14.4 us (9%)
  other arithmetic  4.3 us (3%)
    ppermute x21, waiting for transfers between devices, shift(): return lax.ppermute(value, axis, [(i, (i + step) % n) for i in range(n)])  42.5 us
    ppermute x21, starting transfers between devices, shift(): return lax.ppermute(value, axis, [(i, (i + step) % n) for i in range(n)])  27.1 us
    pallas_call x13, Pallas kernels, call(): pl.pallas_call(kernel, in_specs=[smem] * len(scalars) + [pl.BlockSpec(mem...  20.6 us
    unnamed x44, local copies, waits for them, and re-layouts  16.7 us
    all_to_all x1, waiting for transfers between devices, per_device(): lax.all_to_all(partial, ('z', 'x'), 0, 0, tiled=True)  12.7 us
    all_to_all x1, starting transfers between devices, per_device(): arrived = lax.all_to_all(outgoing, ('z', 'x'), 0, 0, tiled=True)  9.43 us
    all_to_all x1, starting transfers between devices, per_device(): lax.all_to_all(partial, ('z', 'x'), 0, 0, tiled=True)  7.67 us
    pallas_call x1, Pallas kernels, last_sum(): pl.pallas_call(last_body, in_specs=[smem, vmem, vmem] + [hbm] * 4, out_sp...  4.68 us
  transfers between devices with their start and end apart: 25, of which 10 were waited for; matrix products, arithmetic and copies ran while one was open for 5% of the time, Pallas kernels for 13%

commit v1 on v0

--- a/solution.py
+++ b/solution.py
@@ -23,7 +23,8 @@
 I32 = jnp.int32
 VMEM_LIMIT = 14 * 2**20
 COST = 1
-LAST_COST = 10**8
+FAR_COST = 10**9
+RELAY_LIMIT = 56 * 2**20
 HOPS = (0, -1, 1, 2)
 HOPS = (0, -1, 1, 2)
 
@@ -89,9 +90,9 @@
                 keep[y] = dot(proj[...], kv[:, mine : mine + KVW])
 
 
-def fold_weights(core, proj, kv):
+def fold_weights(core, proj, kv, after):
     dims = (NY, proj.shape[0], KVW)
-    return call(fold_body, [shape(dims), shape(dims, F32)], [core], [proj, kv])
+    return call(fold_body, [shape(dims), shape(dims, F32)], [core], [proj, kv], after)
 
 
 def half_body(y, swapped, keep, up, down, across, own):
@@ -143,20 +144,9 @@
     keep[...] = rows(core[0]).reshape(keep.shape)
 
 
-def layer(core, tokens, fc1, fc2, after):
+def layer(core, tokens, fc1, fc2):
     dims = (NY, tokens.shape[0] // (NC * NY), tokens.shape[1])
-    return call(layer_body, [shape(dims), shape(dims, F32)], [core], [tokens, fc1, fc2], after)
-
-
-def piece_body(place, own, up, down, across, tokens, out):
-    total = own[...] + up[...].astype(F32) + down[...].astype(F32) + across[...].astype(F32)
-    rows = own.shape[0]
-    here = tokens[pl.ds(pl.multiple_of(place[0] * rows, rows), rows), :]
-    out[...] = (here.astype(F32) + total).astype(BF)
-
-
-def encoded_piece(place, own, parts, tokens, after):
-    return call(piece_body, shape(own.shape), [place], [own, *parts, tokens], after)
+    return call(layer_body, [shape(dims), shape(dims, F32)], [core], [tokens, fc1, fc2])
 
 
 def regroup_body(shard, encoded, inter, out):
@@ -177,7 +167,7 @@
     return call(functools.partial(regroup_body, shard), shape(dims), [], [encoded, inter])
 
 
-def relay_body(tile_len, owners, encoded, inter, weight, out, features, table, total, sems):
+def relay_body(tile_len, owners, encoded, inter, weight, hot, hidden, query, out, features, table, total, sems):
     split = encoded.shape[1]
     steps = weight.shape[0] // split
     copies = []
@@ -188,7 +178,19 @@
         copies.append(pltpu.make_async_copy(weight.at[rows], table.at[k], sems.at[2 * k + 1]))
     for copy in copies:
         copy.start()
-    out[...] = jnp.zeros_like(out)
+    out[:, :tile_len, :] = jnp.zeros((NIMG, tile_len, KVW), BF)
+
+    slots = dot(hot[...], hidden[...]).astype(BF)
+    for p in range(GROUP * HD // (2 * KVW)):
+        pair = [
+            dot(slots, query[:, (2 * p + i) * KVW : (2 * p + i + 1) * KVW]).reshape(
+                NIMG, CAP, KVW
+            )
+            for i in range(2)
+        ]
+        start = tile_len + 2 * CAP * p
+        out[:, start : start + 2 * CAP, :] = jnp.concatenate(pair, 1).astype(BF)
+
     for k in range(steps):
         copies[2 * k].wait()
         copies[2 * k + 1].wait()
@@ -203,63 +205,54 @@
 
         @pl.when(owner >= 0)
         def _(q=q, owner=owner):
-            out[owner] = tokens[q * tile_len : (q + 1) * tile_len]
-
-
-def relay_rows(owners, encoded, inter, weight, after):
+            out[owner, :tile_len, :] = tokens[q * tile_len : (q + 1) * tile_len]
+
+
+def relay_rows(owners, encoded, inter, weight, hot, hidden, query, after):
     rows, split = encoded.shape
     tile_len = rows // BLOCK
-    width = weight.shape[1]
+    height = tile_len + CAP * GROUP * HD // KVW
     steps = weight.shape[0] // split
-    return call(
-        functools.partial(relay_body, tile_len),
-        shape((NIMG, tile_len, KVW)),
-        [owners],
-        [encoded, inter, weight],
-        after,
-        scratch=[
+    smem, vmem, hbm = (
+        pl.BlockSpec(memory_space=space) for space in (pltpu.SMEM, pltpu.VMEM, pl.ANY)
+    )
+
+    def body(*refs):
+        relay_body(tile_len, *refs[:7], *refs[7 + len(after) :])
+
+    return pl.pallas_call(
+        body,
+        in_specs=[smem] + [hbm] * 3 + [vmem] * 3 + [hbm] * len(after),
+        out_specs=vmem,
+        out_shape=shape((NIMG, height, KVW)),
+        scratch_shapes=[
             pltpu.VMEM((steps, rows, split), BF),
-            pltpu.VMEM((steps, split, width), BF),
-            pltpu.VMEM((rows, width), F32),
+            pltpu.VMEM((steps, split, KVW), BF),
+            pltpu.VMEM((rows, KVW), F32),
             pltpu.SemaphoreType.DMA((2 * steps,)),
         ],
-        space=pltpu.HBM,
-    )
-
-
-def query_body(hot, hidden, weight, out):
-    out[...] = dot(dot(hot[...], hidden[...]).astype(BF), weight[...]).astype(BF).reshape(out.shape)
-
-
-def query_part(hot, hidden, weight, after):
-    out = shape((NIMG, CAP, weight.shape[1]))
-    return call(query_body, out, [], [hot, hidden, weight], after)
-
-
-def normed_body(parts, out):
-    total = jnp.sum(parts[...].astype(F32), 0)
-    for g in range(GROUP):
-        out[g] = rms_scale(total[:, g * HD : (g + 1) * HD], 1e-06)
-
-
-def normed_queries(parts):
-    return call(normed_body, shape((GROUP, CAP, HD), F32), [], [parts])
-
-
-def decode_body(info, arrived, queries, cache, attended):
+        compiler_params=pltpu.CompilerParams(vmem_limit_bytes=RELAY_LIMIT),
+        cost_estimate=pl.CostEstimate(flops=COST, bytes_accessed=COST, transcendentals=0),
+    )(owners, encoded, inter, weight, hot, hidden, query, *after)
+
+
+def decode_body(tile_len, info, arrived, cache, attended):
     groups = NIMG // TILES
-    tile_len = arrived.shape[1]
     length = TILES * tile_len
+    sums = jnp.sum(arrived[:, tile_len:, :].astype(F32), 0)
+    queries = [
+        rms_scale(sums[:, h * HD : (h + 1) * HD], 1e-06).reshape(-1, CAP, HD) for h in range(2)
+    ]
     results = []
     for c in range(CAP):
         block, present, count = info[0, c], info[1, c] > 0, info[2, c]
         for j in range(TILES):
-            rows = arrived[j * groups + block]
+            rows = arrived[j * groups + block, :tile_len, :]
             cache[c, j * tile_len : (j + 1) * tile_len, :] = jnp.where(
                 present, rows, jnp.zeros_like(rows)
             )
         keys, values = cache[c, :, :HD], cache[c, :, HD:]
-        heads = jnp.concatenate([queries[g, c : c + 1] for g in range(GROUP)], 0).astype(BF)
+        heads = jnp.concatenate([q[:, c, :] for q in queries], 0).astype(BF)
         scores = lax.dot_general(
             heads, keys, (((1,), (1,)), ((), ())), preferred_element_type=F32
         ) / math.sqrt(HD)
@@ -268,21 +261,26 @@
         totals = jnp.sum(weights.astype(F32), -1, keepdims=True)
         result = dot(weights, values) / totals
         results.append(jnp.where(present, result, jnp.zeros_like(result)))
-    for g in range(GROUP):
-        column = jnp.concatenate([r[g : g + 1] for r in results], 0)
-        attended[:, g * HD : (g + 1) * HD] = column.astype(BF)
-
-
-def decode(info, arrived, queries):
-    outs = [shape((CAP, TILES * arrived.shape[1], KVW)), shape((CAP, GROUP * HD))]
-    return call(decode_body, outs, [info], [arrived, queries])
+    for row in range(GROUP):
+        head = row % (GROUP // 2) * 2 + row // (GROUP // 2)
+        column = jnp.concatenate([r[row : row + 1] for r in results], 0)
+        attended[:, head * HD : (head + 1) * HD] = column.astype(BF)
+
+
+def decode(info, arrived, tile_len):
+    outs = [shape((CAP, TILES * tile_len, KVW)), shape((CAP, GROUP * HD))]
+    return call(functools.partial(decode_body, tile_len), outs, [info], [arrived])
 
 
 def near_body(x, feats, own, left, right, out):
     mid = own.shape[0] // 2
-    here, before, after = ((x[0] + step) % NX * 2 for step in HOPS[:3])
-    out[...] = dot(feats[here], own[:mid]) + dot(feats[here + 1], own[mid:])
-    out[...] += dot(feats[before], left[...]) + dot(feats[after + 1], right[...])
+    for step, weight in zip(HOPS, (own, left, right)):
+        row = (x[0] + step) % NX * 2
+        term = dot(feats[row], weight[:mid]) + dot(feats[row + 1], weight[mid:])
+        if step == 0:
+            out[...] = term
+        else:
+            out[...] += term
 
 
 def near_sum(x, feats, weights):
@@ -290,40 +288,22 @@
     return call(near_body, shape(dims, F32), [x], [feats, *weights])
 
 
-def last_body(x, near, feats, left, right, first, second, out, places, sems):
-    copies = [
-        pltpu.make_async_copy(w, places.at[k], sems.at[k])
-        for k, w in enumerate((left, right, first, second))
-    ]
-    for copy in copies:
-        copy.start()
-    before, after, across = ((x[0] + step) % NX * 2 for step in HOPS[1:])
-    total = near[...]
-    for k, row in enumerate((before + 1, after, across, across + 1)):
-        copies[k].wait()
-        total = total + dot(feats[row], places[k])
-    out[...] = total.astype(BF)
-
-
-def last_sum(x, near, feats, weights):
-    dims = near.shape
-    smem, vmem, hbm = (
-        pl.BlockSpec(memory_space=space) for space in (pltpu.SMEM, pltpu.VMEM, pltpu.HBM)
-    )
-    return pl.pallas_call(
-        last_body,
-        in_specs=[smem, vmem, vmem] + [hbm] * 4,
-        out_specs=vmem,
-        out_shape=shape(dims),
-        scratch_shapes=[
-            pltpu.VMEM((4,) + weights[0].shape, BF),
-            pltpu.SemaphoreType.DMA((4,)),
-        ],
-        compiler_params=pltpu.CompilerParams(vmem_limit_bytes=VMEM_LIMIT),
-        cost_estimate=pl.CostEstimate(
-            flops=LAST_COST, bytes_accessed=LAST_COST, transcendentals=0
-        ),
-    )(x, near, feats, *weights)
+def far_body(x, feats, first, second, out):
+    row = (x[0] + HOPS[-1]) % NX * 2
+    out[...] = dot(feats[row], first[...]) + dot(feats[row + 1], second[...])
+
+
+def far_sum(x, feats, weights):
+    dims = (feats.shape[1], weights[0].shape[1])
+    return call(far_body, shape(dims, F32), [x], [feats, *weights], cost=FAR_COST)
+
+
+def last_body(near, rest, out):
+    out[...] = (near[...] + rest[...]).astype(BF)
+
+
+def last_sum(near, rest):
+    return call(last_body, shape(near.shape), [], [near, rest])
 
 
 def per_device(
@@ -350,35 +330,16 @@
     requests = tile_counts.shape[0]
 
     late = lax.all_gather(proj_weight, "z", axis=0, tiled=True)
+    left, right = shift(late, "x", 1), shift(late, "x", -1)
     mid = late.shape[0] // 2
-    left_first, right_second = shift(late[:mid], "x", 1), shift(late[mid:], "x", -1)
-    left_second, right_first = shift(late[mid:], "x", 1), shift(late[:mid], "x", -1)
-    far = [shift(left_first, "x", 1), shift(right_second, "x", -1)]
-
-    fold_send, fold_keep = fold_weights(core, proj_weight, kv_weight)
+    far = [shift(left[:mid], "x", 1), shift(right[mid:], "x", -1)]
+
+    send, keep = layer(core, vision_tokens, fc1_weight.T, fc2_weight)
+    swapped = shift(send, "c", 1)
+
+    fold_send, fold_keep = fold_weights(core, proj_weight, kv_weight, [send])
     *fold_parts, fold_own = half_sums(there, shift(fold_send, "c", 1), fold_keep)
-
-    send, keep = layer(core, vision_tokens, fc1_weight.T, fc2_weight, [tick(fold_send)])
-    *parts, total = half_sums(there, shift(send, "c", 1), keep, [tick(fold_parts[0])])
-
     fold_parts = [shift(p, "y", step) for step, p in zip((1, -1, 2), fold_parts)]
-    joined = join(fold_own, fold_parts, [tick(parts[0])])
-
-    parts = [shift(p, "y", step) for step, p in zip((1, -1, 2), parts)]
-    place_here = (ci * NY + yi).astype(I32)[None]
-    piece = encoded_piece(place_here, total, parts, vision_tokens, [tick(joined)])
-    pieces = place(jnp.zeros((NY,) + piece.shape, BF), piece, yi, 0)
-    for step in (1, -1, 2):
-        pieces = place(pieces, shift(piece, "y", step), (yi - step) % NY, 0)
-    pieces = pieces.reshape(rows // 2, width)
-    other = shift(pieces, "c", 1)
-    encoded = jnp.concatenate(
-        [jnp.where(ci == 0, pieces, other), jnp.where(ci == 0, other, pieces)], 0
-    )
-
-    block = [joined, *(shift(joined, "x", step) for step in (1, -1, 2))]
-    block = in_order(column, block, [tick(late)]).reshape(NX * shard, -1)
-    early = lax.all_gather(block, "z", axis=0, tiled=True)
 
     request_ids = jnp.arange(requests, dtype=I32)
     same_owner = owner_map[:, None] == owner_map[None, :]
@@ -394,26 +355,44 @@
     )
     info = jnp.stack([request_of // BLOCK, present.astype(I32), count_of])
 
+    *parts, total = half_sums(there, swapped, keep)
+    for step, part in zip((1, -1, 2), parts):
+        total = total + shift(part, "y", step).astype(F32)
+    quarter = rows // (NC * NY)
+    tokens_here = pick(vision_tokens.reshape(NC * NY, quarter, width), ci * NY + yi)
+    piece = (tokens_here.astype(F32) + total).astype(BF)
+    pieces = place(jnp.zeros((NY,) + piece.shape, BF), piece, yi, 0)
+    gathered = [shift(piece, "y", step) for step in (1, -1, 2)]
+    for step, value in zip((1, -1, 2), gathered):
+        pieces = place(pieces, value, (yi - step) % NY, 0)
+    pieces = pieces.reshape(rows // 2, width)
+    other = shift(pieces, "c", 1)
+    encoded = jnp.concatenate(
+        [jnp.where(ci == 0, pieces, other), jnp.where(ci == 0, other, pieces)], 0
+    )
+
+    joined = join(fold_own, fold_parts, [tick(v) for v in gathered])
+    block = [joined, *(shift(joined, "x", step) for step in (1, -1, 2))]
+    block = in_order(column, block, [tick(late)]).reshape(NX * shard, -1)
+    early = lax.all_gather(block, "z", axis=0, tiled=True)
+
     slot_row = jnp.arange(NIMG * CAP, dtype=I32)
     slot_hot = (owner_map[None, :] == (slot_row // CAP)[:, None]) & (
         slot_rank[None, :] == (slot_row % CAP)[:, None]
     )
-    partial = query_part(slot_hot.astype(BF), decode_hidden, query_weight, [tick(encoded)])
-    queries = normed_queries(lax.all_to_all(partial, ("z", "x"), 0, 0, tiled=True))
-
     feats = regroup(encoded, inter_feats, shard)
     tile_here, block_here = img_index // NZ, img_index % NZ
     owners_here = lax.dynamic_slice_in_dim(owner_map, block_here * BLOCK, BLOCK)
     counts_here = lax.dynamic_slice_in_dim(tile_counts, block_here * BLOCK, BLOCK)
     targets = jnp.where(tile_here < counts_here, owners_here, -1)
     outgoing = relay_rows(
-        targets, encoded, inter_feats, early, [tick(feats), queries]
+        targets, encoded, inter_feats, early, slot_hot.astype(BF), decode_hidden, query_weight, [tick(feats)]
     )
     arrived = lax.all_to_all(outgoing, ("z", "x"), 0, 0, tiled=True)
-    kv_cache, attended = decode(info, arrived, queries)
-
-    near = near_sum(column, feats, [late, left_first, right_second])
-    vision_states = last_sum(column, near, feats, [left_second, right_first, *far])
+    kv_cache, attended = decode(info, arrived, tile_len)
+
+    near = near_sum(column, feats, [late, left, right])
+    vision_states = last_sum(near, far_sum(column, feats, far))
     return (vision_states, kv_cache, attended)
 
 

time: 169 us -> 157 us (0.929)
  starting transfers between devices: 44.3 us -> 27.9 us
  waiting for transfers between devices: 59.5 us -> 70.2 us
  local copies, waits for them, and re-layouts: 20.3 us -> 17.1 us
  Pallas kernels: 25.2 us -> 22.2 us
    all_gather x1, waiting for transfers between devices: 0.01 us -> 28.4 us  [per_device(): early = lax.all_gather(block, 'z', axis=0, tiled=True)]
    all_to_all x1 -> x0, waiting for transfers between devices: 12.7 us -> none  [per_device(): lax.all_to_all(partial, ('z', 'x'), 0, 0, tiled=True)]
    all_to_all x1 -> x0, starting transfers between devices: 7.67 us -> none  [per_device(): lax.all_to_all(partial, ('z', 'x'), 0, 0, tiled=True)]
    ppermute x21 -> x19, starting transfers between devices: 27.1 us -> 20.4 us  [shift(): return lax.ppermute(value, axis, [(i, (i + step) % n) for i in range(n)])]
    unnamed x44 -> x24, local copies, waits for them, and re-layouts: 16.7 us -> 11.6 us
    pallas_call x13 -> x11, Pallas kernels: 20.6 us -> 16.3 us  [call(): pl.pallas_call(kernel, in_specs=[smem] * len(scalars) + [pl.BlockSpec(mem...]
    all_gather x1, waiting for transfers between devices: 3.61 us -> 0.59 us  [per_device(): late = lax.all_gather(proj_weight, 'z', axis=0, tiled=True)]
    all_to_all x1, starting transfers between devices: 9.43 us -> 7.38 us  [per_device(): arrived = lax.all_to_all(outgoing, ('z', 'x'), 0, 0, tiled=True)]
  transfers between devices with their start and end apart: 25 -> 22, of which waited for: 10 -> 12; matrix products, arithmetic and copies ran while one was open for 5% -> 7% of each run, Pallas kernels for 13% -> 12%
where the time goes in v1:
time: 157 us
  waiting for transfers between devices  70.2 us (45%)
  starting transfers between devices  27.9 us (18%)
  Pallas kernels  22.2 us (14%)
  local copies, waits for them, and re-layouts  17.1 us (11%)
  between operations  14.4 us (9%)
  other arithmetic  4.81 us (3%)
    ppermute x19, waiting for transfers between devices, shift(): return lax.ppermute(value, axis, [(i, (i + step) % n) for i in range(n)])  40.5 us
    all_gather x1, waiting for transfers between devices, per_device(): early = lax.all_gather(block, 'z', axis=0, tiled=True)  28.4 us
    ppermute x19, starting transfers between devices, shift(): return lax.ppermute(value, axis, [(i, (i + step) % n) for i in range(n)])  20.4 us
    pallas_call x11, Pallas kernels, call(): pl.pallas_call(kernel, in_specs=[smem] * len(scalars) + [pl.BlockSpec(mem...  16.3 us
    unnamed x24, local copies, waits for them, and re-layouts  11.6 us
    all_to_all x1, starting transfers between devices, per_device(): arrived = lax.all_to_all(outgoing, ('z', 'x'), 0, 0, tiled=True)  7.38 us
    pallas_call x1, Pallas kernels, relay_rows(): pl.pallas_call(body, in_specs=[smem] + [hbm] * 3 + [vmem] * 3 + [hbm] * l...  5.87 us
  transfers between devices with their start and end apart: 22, of which 12 were waited for; matrix products, arithmetic and copies ran while one was open for 7% of the time, Pallas kernels for 12%

profile of v1, /device:TPU:2, one launch (start us, length us, event | category | flops | bytes accessed | tf_op | source)
XLA Modules:
  0.0 156.5 jit_solution(12741255320735476059)
XLA Ops:
  7.2 0.7 all-gather.3.cloned.1.call-update
  8.0 1.3 copy-done.6
  9.3 1.1 copy-done.8
  10.4 1.1 copy-done.9
  11.6 2.2 %shard_map.121 = (bf16[4,64,1280]{2,1,0:T(8,128)(2,1)S(1)}, f32[4,64,1280]{2,1,0:T(8,128)S(1)}) custom-call(s32[1]{0:T(128)} %bitcast.4.refs_0_, bf16[512,1280]{1,0:T(8,128)(2,1)S(1)} %copy-done.6, bf16[320,1280]{1,0:T(8,128)(2,1)S(1)} %bitcast.36, bf16[320,1280]{1,0:T(8,128)(2,1)S(1)} %copy-done.9), custom_call_target="tpu_custom_call" | custom-call | flops 1 | bytes 1 | tf_op jit(solution)/shard_map/pallas_call | solution.py:69
  13.7 0.1 collective-permute-start
  13.9 2.1 %collective-permute-done.refs_1_ = bf16[4,64,1280]{2,1,0:T(8,128)(2,1)S(1)} collective-permute-done((bf16[4,64,1280]{2,1,0:T(8,128)(2,1)S(1)}, bf16[4,64,1280]{2,1,0:T(8,128)(2,1)S(1)}, u32[]{:S(2)}, u32[]{:S(2)}) %collective-permute-start) | collective-permute-done | bytes 655392 | tf_op jit(solution)/shard_map/ppermute | solution.py:34
  15.9 0.8 shard_map.122
  16.7 1.6 %collective-permute-start.1 = (bf16[64,1280]{1,0:T(8,128)(2,1)}, bf16[64,1280]{1,0:T(8,128)(2,1)S(1)}, u32[]{:S(2)}, u32[]{:S(2)}) collective-permute-start(bf16[64,1280]{1,0:T(8,128)(2,1)} %get-tuple-element.20), channel_id=1, source_target_pairs={{0,2},{2,4},{4,6},{6,0},{1,3},{3,5},{5,7},{7,1},{8,10},{10,12},{12... | collective-permute-start | bytes 491528 | tf_op jit(solution)/shard_map/ppermute | solution.py:34
  18.3 1.7 %collective-permute-start.2 = (bf16[64,1280]{1,0:T(8,128)(2,1)S(1)}, bf16[64,1280]{1,0:T(8,128)(2,1)S(1)}, u32[]{:S(2)}, u32[]{:S(2)}) collective-permute-start(bf16[64,1280]{1,0:T(8,128)(2,1)S(1)} %get-tuple-element.21), channel_id=1, source_target_pairs={{0,6},{2,0},{4,2},{6,4},{1,7},{3,1},{5,3},{7,5},{8,14},{10,8},{12,... | collective-permute-start | bytes 491528 | tf_op jit(solution)/shard_map/ppermute | solution.py:34
  19.9 2.0 %collective-permute-start.3 = (bf16[64,1280]{1,0:T(8,128)(2,1)S(1)}, bf16[64,1280]{1,0:T(8,128)(2,1)S(1)}, u32[]{:S(2)}, u32[]{:S(2)}) collective-permute-start(bf16[64,1280]{1,0:T(8,128)(2,1)S(1)} %get-tuple-element.22), channel_id=1, source_target_pairs={{0,4},{2,6},{4,0},{6,2},{1,5},{3,7},{5,1},{7,3},{8,12},{10,14},{12... | collective-permute-start | bytes 491528 | tf_op jit(solution)/shard_map/ppermute | solution.py:34
  21.9 2.2 %copy-done.4 = bf16[1024,2048]{1,0:T(8,128)(2,1)S(1)} copy-done((bf16[1024,2048]{1,0:T(8,128)(2,1)S(1)}, bf16[1024,2048]{1,0:T(8,128)(2,1)}, u32[]{:S(2)}) %copy-start.4) | copy-done | bytes 4194328
  24.1 0.7 shard_map.127
  24.8 0.1 collective-permute-start.12
  25.0 0.4 collective-permute-done.2
  25.4 3.8 %collective-permute-done.3 = bf16[64,1280]{1,0:T(8,128)(2,1)S(1)} collective-permute-done((bf16[64,1280]{1,0:T(8,128)(2,1)S(1)}, bf16[64,1280]{1,0:T(8,128)(2,1)S(1)}, u32[]{:S(2)}, u32[]{:S(2)}) %collective-permute-start.3) | collective-permute-done | bytes 163872 | tf_op jit(solution)/shard_map/ppermute | solution.py:34
  29.1 0.9 broadcast_in_dim.63
  30.0 1.7 %bitcast_dynamic-update-slice_fusion.3 = (bf16[4,64,1280]{2,1,0:T(8,128)(2,1)}, bf16[64,1280]{1,0:T(8,128)(2,1)S(1)}) fusion(bf16[4,64,1280]{2,1,0:T(8,128)(2,1)} %broadcast_in_dim.63, s32[]{:T(128)S(6)} %select_n.114, bf16[64,1280]{1,0:T(8,128)(2,1)S(1)} %collective-permute-done.3, bf16[64,1280]{1,0:T(8,128)(2,1)S(1)} %collective-permute-done.2, ...), kind=kLoop, calls=%fused_computation.8 | loop fusion | flops 737280 | bytes 1310728 | tf_op jit(solution)/shard_map/jit(dynamic_update_index_in_dim)/dynamic_update_slice | solution.py:50
  31.7 0.9 collective-permute-start.4
  32.6 2.3 %collective-permute-start.5 = (bf16[64,1280]{1,0:T(8,128)(2,1)S(1)}, bf16[64,1280]{1,0:T(8,128)(2,1)S(1)}, u32[]{:S(2)}, u32[]{:S(2)}) collective-permute-start(bf16[64,1280]{1,0:T(8,128)(2,1)S(1)} %get-tuple-element.34), channel_id=1, source_target_pairs={{0,6},{2,0},{4,2},{6,4},{1,7},{3,1},{5,3},{7,5},{8,14},{10,8},{12,... | collective-permute-start | bytes 491528 | tf_op jit(solution)/shard_map/ppermute | solution.py:34
  34.9 0.1 shard_map.128
  35.0 1.3 collective-permute-start.13
  36.3 2.0 %collective-permute-start.14 = (bf16[120,256]{1,0:T(8,128)(2,1)S(1)}, bf16[120,256]{1,0:T(8,128)(2,1)S(1)}, u32[]{:S(2)}, u32[]{:S(2)}) collective-permute-start(bf16[120,256]{1,0:T(8,128)(2,1)S(1)} %get-tuple-element.27), channel_id=1, source_target_pairs={{0,6},{2,0},{4,2},{6,4},{1,7},{3,1},{5,3},{7,5},{8,14},{10,8},{12,... | collective-permute-start | bytes 184328 | tf_op jit(solution)/shard_map/ppermute | solution.py:34
  38.3 4.8 %collective-permute-done.4 = bf16[64,1280]{1,0:T(8,128)(2,1)S(1)} collective-permute-done((bf16[64,1280]{1,0:T(8,128)(2,1)S(1)}, bf16[64,1280]{1,0:T(8,128)(2,1)S(1)}, u32[]{:S(2)}, u32[]{:S(2)}) %collective-permute-start.4) | collective-permute-done | bytes 163872 | tf_op jit(solution)/shard_map/ppermute | solution.py:34
  43.2 0.6 collective-permute-done.13.refs_1_
  43.8 5.1 %collective-permute-done.15.refs_3_ = bf16[120,256]{1,0:T(8,128)(2,1)S(1)} collective-permute-done((bf16[120,256]{1,0:T(8,128)(2,1)S(1)}, bf16[120,256]{1,0:T(8,128)(2,1)S(1)}, u32[]{:S(2)}, u32[]{:S(2)}) %collective-permute-start.15) | collective-permute-done | bytes 61472 | tf_op jit(solution)/shard_map/ppermute | solution.py:34
  48.9 1.6 %collective-permute-start.16 = (bf16[120,256]{1,0:T(8,128)(2,1)S(1)}, bf16[120,256]{1,0:T(8,128)(2,1)S(1)}, u32[]{:S(2)}, u32[]{:S(2)}) collective-permute-start(bf16[120,256]{1,0:T(8,128)(2,1)S(1)} %shard_map.129.refs_1_), channel_id=1, source_target_pairs={{0,8},{8,16},{16,24},{24,0},{1,9},{9,17},{17,25},{25,1},{2,10},{10... | collective-permute-start | bytes 184328 | tf_op jit(solution)/shard_map/ppermute | solution.py:34
  50.5 0.5 collective-permute-start.17
  51.0 2.1 %collective-permute-start.18 = (bf16[120,256]{1,0:T(8,128)(2,1)S(1)}, bf16[120,256]{1,0:T(8,128)(2,1)S(1)}, u32[]{:S(2)}, u32[]{:S(2)}) collective-permute-start(bf16[120,256]{1,0:T(8,128)(2,1)S(1)} %shard_map.129.refs_1_), channel_id=1, source_target_pairs={{0,16},{8,24},{16,0},{24,8},{1,17},{9,25},{17,1},{25,9},{2,18},{10... | collective-permute-start | bytes 184328 | tf_op jit(solution)/shard_map/ppermute | solution.py:34
  53.1 0.6 all-gather.3.cloned.1.call-done.refs_2_
  53.7 0.7 slice.33.refs_5_
  54.4 0.3 collective-permute-done.17.refs_3_
  54.7 2.0 %collective-permute-done.18.refs_4_ = bf16[120,256]{1,0:T(8,128)(2,1)S(1)} collective-permute-done((bf16[120,256]{1,0:T(8,128)(2,1)S(1)}, bf16[120,256]{1,0:T(8,128)(2,1)S(1)}, u32[]{:S(2)}, u32[]{:S(2)}) %collective-permute-start.18) | collective-permute-done | bytes 61472 | tf_op jit(solution)/shard_map/ppermute | solution.py:34
  56.7 0.7 shard_map.130
  57.5 0.7 bitcast_dynamic-update-slice_fusion.2
  58.2 0.7 bitcast_dynamic-update-slice_fusion.1
  58.9 0.7 bitcast_dynamic-update-slice_fusion
  59.6 1.5 collective-permute-start.8
  61.1 0.5 collective-permute-start.9
  61.6 0.6 compare_select_fusion.refs_0_
  62.2 0.2 convert_reduce_fusion
  62.4 0.8 and_convert_fusion.refs_4_
  63.2 1.2 broadcast_select_fusion.1
  64.4 0.1 pad_maximum_fusion.refs_0_.refs_1_
  64.5 1.6 %copy-done.3 = bf16[512,2560]{1,0:T(8,128)(2,1)S(1)} copy-done((bf16[512,2560]{1,0:T(8,128)(2,1)S(1)}, bf16[512,2560]{1,0:T(8,128)(2,1)}, u32[]{:S(2)}) %copy-start.3) | copy-done | bytes 2621464
  66.1 1.8 %shard_map.123.refs_1_ = bf16[8,512,480]{2,1,0:T(8,128)(2,1)S(1)} custom-call(bf16[512,1280]{1,0:T(8,128)(2,1)S(1)} %pad_maximum_fusion.refs_0_.refs_1_, bf16[512,2560]{1,0:T(8,128)(2,1)S(1)} %copy-done.3), custom_call_target="tpu_custom_call" | custom-call | flops 1 | bytes 1 | tf_op jit(solution)/shard_map/pallas_call | solution.py:69
  67.9 0.6 slice.34.refs_7_
  68.5 2.0 %copy-done = bf16[8,512,480]{2,1,0:T(8,128)(2,1)} copy-done((bf16[8,512,480]{2,1,0:T(8,128)(2,1)}, bf16[8,512,480]{2,1,0:T(8,128)(2,1)S(1)}, u32[]{:S(2)}) %copy-start) | copy-done | bytes 3932184
  70.5 28.4 %all-gather.5.cloned.1.call-done.refs_3_ = bf16[3840,256]{1,0:T(8,128)(2,1)} async-done(((bf16[480,256]{1,0:T(8,128)(2,1)}), bf16[3840,256]{1,0:T(8,128)(2,1)}) %all-gather.5.cloned.1.call-update) | async-done | bytes 1966096 | tf_op jit(solution)/shard_map/all_gather | solution.py:377
  98.9 5.9 %shard_map.131 = bf16[32,64,256]{2,1,0:T(8,128)(2,1)} custom-call(s32[16]{0:T(128)} %compare_select_fusion.refs_0_, bf16[512,1280]{1,0:T(8,128)(2,1)} %copy-done.2, bf16[512,2560]{1,0:T(8,128)(2,1)} %refs_2_.3, bf16[3840,256]{1,0:T(8,128)(2,1)} %all-gather.5.cloned.1.call-done.refs_3_, bf16[256,128]{1,0:T(8,128)(2,1)} %and_convert_fusion.refs_4_, ...), custom_call_target="tpu_custom_call" | custom-call | flops 1 | bytes 1 | tf_op jit(solution)/shard_map/pallas_call | solution.py:223
  104.8 7.4 %all-to-all-start = ((bf16[32,64,256]{2,1,0:T(8,128)(2,1)}), bf16[32,64,256]{2,1,0:T(8,128)(2,1)S(1)}, u32[]{:S(2)}, u32[]{:S(2)}) async-start(bf16[32,64,256]{2,1,0:T(8,128)(2,1)} %shard_map.131), calls=%async_computation | async-start | bytes 2097152 | tf_op jit(solution)/shard_map/all_to_all | solution.py:391
  112.2 0.1 slice.28
  112.3 1.5 collective-permute-start.10
  113.8 1.3 slice.29
  115.1 0.6 collective-permute-start.11
  115.7 0.1 fusion.3
  115.9 0.1 select_reduce_fusion.1
  116.1 2.2 %copy-done.1 = bf16[8,512,480]{2,1,0:T(8,128)(2,1)S(1)} copy-done((bf16[8,512,480]{2,1,0:T(8,128)(2,1)S(1)}, bf16[8,512,480]{2,1,0:T(8,128)(2,1)}, u32[]{:S(2)}) %copy-start.1) | copy-done | bytes 3932184
  118.3 4.9 %shard_map.124.refs_0_ = f32[512,1024]{1,0:T(8,128)S(1)} custom-call(s32[1]{0:T(128)} %bitcast.refs_0_, bf16[8,512,480]{2,1,0:T(8,128)(2,1)S(1)} %copy-done.1, bf16[960,1024]{1,0:T(8,128)(2,1)S(1)} %copy-done.5, bf16[960,1024]{1,0:T(8,128)(2,1)S(1)} %collective-permute-done.8.refs_3_, bf16[960,1024]{1,0:T(8,128)(2,1)} %collective-permute-done.9.refs_4_), custom_call_target="tpu_custom_call" | custom-call | flops 1 | bytes 1 | tf_op jit(solution)/shard_map/pallas_call | solution.py:69
  123.2 18.5 %collective-permute-done.10.refs_2_ = bf16[480,1024]{1,0:T(8,128)(2,1)S(1)} collective-permute-done((bf16[480,1024]{1,0:T(8,128)(2,1)S(1)}, bf16[480,1024]{1,0:T(8,128)(2,1)S(1)}, u32[]{:S(2)}, u32[]{:S(2)}) %collective-permute-start.10) | collective-permute-done | bytes 983072 | tf_op jit(solution)/shard_map/ppermute | solution.py:34
  141.7 2.9 %collective-permute-done.11.refs_3_ = bf16[480,1024]{1,0:T(8,128)(2,1)S(1)} collective-permute-done((bf16[480,1024]{1,0:T(8,128)(2,1)S(1)}, bf16[480,1024]{1,0:T(8,128)(2,1)S(1)}, u32[]{:S(2)}, u32[]{:S(2)}) %collective-permute-start.11) | collective-permute-done | bytes 983072 | tf_op jit(solution)/shard_map/ppermute | solution.py:34
  144.6 1.3 shard_map.125.refs_1_
  145.8 1.2 shard_map.126
  147.0 2.7 %shard_map.132 = (bf16[8,128,256]{2,1,0:T(8,128)(2,1)}, bf16[8,1024]{1,0:T(8,128)(2,1)}) custom-call(s32[3,8]{1,0:T(4,128)S(1)} %pad_add_fusion.refs_0_, bf16[32,64,256]{2,1,0:T(8,128)(2,1)S(1)} %all-to-all-done.refs_1_), custom_call_target="tpu_custom_call" | custom-call | flops 1 | bytes 1 | tf_op jit(solution)/shard_map/pallas_call | solution.py:69
  (43 shorter events, 0.2 us)
Async XLA Ops:
  7.2 46.6 %all-gather.3.cloned.1.call-start = ((), (), s32[]{:S(2)}) async-start(), calls=%async_computation.1 | async-start | bytes 2211840 | tf_op jit(solution)/shard_map/all_gather | solution.py:332
  7.9 91.0 %all-gather.5.cloned.1.call-start = ((), (), s32[]{:S(2)}) async-start(), calls=%async_computation.2 | async-start | bytes 2211840 | tf_op jit(solution)/shard_map/all_gather | solution.py:377
  8.0 1.3 copy-start.6
  9.3 1.1 copy-start.8
  10.4 1.1 copy-start.9
  11.6 10.4 %copy-start.7 = (bf16[120,1024]{1,0:T(8,128)(2,1)S(1)}, bf16[120,1024]{1,0:T(8,128)(2,1)}, u32[]{:S(2)}) copy-start(bf16[120,1024]{1,0:T(8,128)(2,1)} %refs_1_.5) | copy-start | bytes 737284
  13.7 2.2 %collective-permute-start = (bf16[4,64,1280]{2,1,0:T(8,128)(2,1)S(1)}, bf16[4,64,1280]{2,1,0:T(8,128)(2,1)S(1)}, u32[]{:S(2)}, u32[]{:S(2)}) collective-permute-start(bf16[4,64,1280]{2,1,0:T(8,128)(2,1)S(1)} %get-tuple-element.17.refs_3_), channel_id=1, source_target_pairs={{0,1},{1,0},{2,3},{3,2},{4,5},{5,4},{6,7},{7,6},{8,9},{9,8},{10,11... | collective-permute-start | bytes 1966088 | tf_op jit(solution)/shard_map/ppermute | solution.py:34
  16.7 8.3 %collective-permute-start.1 = (bf16[64,1280]{1,0:T(8,128)(2,1)}, bf16[64,1280]{1,0:T(8,128)(2,1)S(1)}, u32[]{:S(2)}, u32[]{:S(2)}) collective-permute-start(bf16[64,1280]{1,0:T(8,128)(2,1)} %get-tuple-element.20), channel_id=1, source_target_pairs={{0,2},{2,4},{4,6},{6,0},{1,3},{3,5},{5,7},{7,1},{8,10},{10,12},{12... | collective-permute-start | bytes 491528 | tf_op jit(solution)/shard_map/ppermute | solution.py:34
  18.3 7.1 %collective-permute-start.2 = (bf16[64,1280]{1,0:T(8,128)(2,1)S(1)}, bf16[64,1280]{1,0:T(8,128)(2,1)S(1)}, u32[]{:S(2)}, u32[]{:S(2)}) collective-permute-start(bf16[64,1280]{1,0:T(8,128)(2,1)S(1)} %get-tuple-element.21), channel_id=1, source_target_pairs={{0,6},{2,0},{4,2},{6,4},{1,7},{3,1},{5,3},{7,5},{8,14},{10,8},{12,... | collective-permute-start | bytes 491528 | tf_op jit(solution)/shard_map/ppermute | solution.py:34
  19.9 9.2 %collective-permute-start.3 = (bf16[64,1280]{1,0:T(8,128)(2,1)S(1)}, bf16[64,1280]{1,0:T(8,128)(2,1)S(1)}, u32[]{:S(2)}, u32[]{:S(2)}) collective-permute-start(bf16[64,1280]{1,0:T(8,128)(2,1)S(1)} %get-tuple-element.22), channel_id=1, source_target_pairs={{0,4},{2,6},{4,0},{6,2},{1,5},{3,7},{5,1},{7,3},{8,12},{10,14},{12... | collective-permute-start | bytes 491528 | tf_op jit(solution)/shard_map/ppermute | solution.py:34
  21.9 2.2 %copy-start.4 = (bf16[1024,2048]{1,0:T(8,128)(2,1)S(1)}, bf16[1024,2048]{1,0:T(8,128)(2,1)}, u32[]{:S(2)}) copy-start(bf16[1024,2048]{1,0:T(8,128)(2,1)} %refs_2_.2) | copy-start | bytes 12582916
  24.8 10.1 %collective-permute-start.12 = (bf16[4,120,256]{2,1,0:T(8,128)(2,1)S(1)}, bf16[4,120,256]{2,1,0:T(8,128)(2,1)S(1)}, u32[]{:S(2)}, u32[]{:S(2)}) collective-permute-start(bf16[4,120,256]{2,1,0:T(8,128)(2,1)S(1)} %get-tuple-element.23), channel_id=1, source_target_pairs={{0,1},{1,0},{2,3},{3,2},{4,5},{5,4},{6,7},{7,6},{8,9},{9,8},{10,11... | collective-permute-start | bytes 737288 | tf_op jit(solution)/shard_map/ppermute | solution.py:34
  30.0 31.6 %copy-start.10 = (s32[128]{0:T(128)S(1)}, s32[128]{0:T(128)}, u32[]{:S(2)}) copy-start(s32[128]{0:T(128)} %param.17) | copy-start | bytes 1540
  30.0 31.6 %copy-start.11 = (s32[128]{0:T(128)S(1)}, s32[128]{0:T(128)}, u32[]{:S(2)}) copy-start(s32[128]{0:T(128)} %param.16) | copy-start | bytes 1540
  31.7 11.5 %collective-permute-start.4 = (bf16[64,1280]{1,0:T(8,128)(2,1)S(1)}, bf16[64,1280]{1,0:T(8,128)(2,1)S(1)}, u32[]{:S(2)}, u32[]{:S(2)}) collective-permute-start(bf16[64,1280]{1,0:T(8,128)(2,1)S(1)} %get-tuple-element.34), channel_id=1, source_target_pairs={{0,2},{2,4},{4,6},{6,0},{1,3},{3,5},{5,7},{7,1},{8,10},{10,12},{12... | collective-permute-start | bytes 491528 | tf_op jit(solution)/shard_map/ppermute | solution.py:34
  32.6 10.5 %collective-permute-start.5 = (bf16[64,1280]{1,0:T(8,128)(2,1)S(1)}, bf16[64,1280]{1,0:T(8,128)(2,1)S(1)}, u32[]{:S(2)}, u32[]{:S(2)}) collective-permute-start(bf16[64,1280]{1,0:T(8,128)(2,1)S(1)} %get-tuple-element.34), channel_id=1, source_target_pairs={{0,6},{2,0},{4,2},{6,4},{1,7},{3,1},{5,3},{7,5},{8,14},{10,8},{12,... | collective-permute-start | bytes 491528 | tf_op jit(solution)/shard_map/ppermute | solution.py:34
  34.9 8.2 %collective-permute-start.6 = (bf16[64,1280]{1,0:T(8,128)(2,1)S(1)}, bf16[64,1280]{1,0:T(8,128)(2,1)S(1)}, u32[]{:S(2)}, u32[]{:S(2)}) collective-permute-start(bf16[64,1280]{1,0:T(8,128)(2,1)S(1)} %get-tuple-element.34), channel_id=1, source_target_pairs={{0,4},{2,6},{4,0},{6,2},{1,5},{3,7},{5,1},{7,3},{8,12},{10,14},{12... | collective-permute-start | bytes 491528 | tf_op jit(solution)/shard_map/ppermute | solution.py:34
  35.0 8.8 %collective-permute-start.13 = (bf16[120,256]{1,0:T(8,128)(2,1)S(1)}, bf16[120,256]{1,0:T(8,128)(2,1)S(1)}, u32[]{:S(2)}, u32[]{:S(2)}) collective-permute-start(bf16[120,256]{1,0:T(8,128)(2,1)S(1)} %get-tuple-element.26), channel_id=1, source_target_pairs={{0,2},{2,4},{4,6},{6,0},{1,3},{3,5},{5,7},{7,1},{8,10},{10,12},{12... | collective-permute-start | bytes 184328 | tf_op jit(solution)/shard_map/ppermute | solution.py:34
  36.3 7.5 %collective-permute-start.14 = (bf16[120,256]{1,0:T(8,128)(2,1)S(1)}, bf16[120,256]{1,0:T(8,128)(2,1)S(1)}, u32[]{:S(2)}, u32[]{:S(2)}) collective-permute-start(bf16[120,256]{1,0:T(8,128)(2,1)S(1)} %get-tuple-element.27), channel_id=1, source_target_pairs={{0,6},{2,0},{4,2},{6,4},{1,7},{3,1},{5,3},{7,5},{8,14},{10,8},{12,... | collective-permute-start | bytes 184328 | tf_op jit(solution)/shard_map/ppermute | solution.py:34
  43.1 5.7 %collective-permute-start.15 = (bf16[120,256]{1,0:T(8,128)(2,1)S(1)}, bf16[120,256]{1,0:T(8,128)(2,1)S(1)}, u32[]{:S(2)}, u32[]{:S(2)}) collective-permute-start(bf16[120,256]{1,0:T(8,128)(2,1)S(1)} %get-tuple-element.28), channel_id=1, source_target_pairs={{0,4},{2,6},{4,0},{6,2},{1,5},{3,7},{5,1},{7,3},{8,12},{10,14},{12... | collective-permute-start | bytes 184328 | tf_op jit(solution)/shard_map/ppermute | solution.py:34
  48.9 5.5 %collective-permute-start.16 = (bf16[120,256]{1,0:T(8,128)(2,1)S(1)}, bf16[120,256]{1,0:T(8,128)(2,1)S(1)}, u32[]{:S(2)}, u32[]{:S(2)}) collective-permute-start(bf16[120,256]{1,0:T(8,128)(2,1)S(1)} %shard_map.129.refs_1_), channel_id=1, source_target_pairs={{0,8},{8,16},{16,24},{24,0},{1,9},{9,17},{17,25},{25,1},{2,10},{10... | collective-permute-start | bytes 184328 | tf_op jit(solution)/shard_map/ppermute | solution.py:34
  50.5 4.2 %collective-permute-start.17 = (bf16[120,256]{1,0:T(8,128)(2,1)S(1)}, bf16[120,256]{1,0:T(8,128)(2,1)S(1)}, u32[]{:S(2)}, u32[]{:S(2)}) collective-permute-start(bf16[120,256]{1,0:T(8,128)(2,1)S(1)} %shard_map.129.refs_1_), channel_id=1, source_target_pairs={{0,24},{8,0},{16,8},{24,16},{1,25},{9,1},{17,9},{25,17},{2,26},{10... | collective-permute-start | bytes 184328 | tf_op jit(solution)/shard_map/ppermute | solution.py:34
  51.0 5.7 %collective-permute-start.18 = (bf16[120,256]{1,0:T(8,128)(2,1)S(1)}, bf16[120,256]{1,0:T(8,128)(2,1)S(1)}, u32[]{:S(2)}, u32[]{:S(2)}) collective-permute-start(bf16[120,256]{1,0:T(8,128)(2,1)S(1)} %shard_map.129.refs_1_), channel_id=1, source_target_pairs={{0,16},{8,24},{16,0},{24,8},{1,17},{9,25},{17,1},{25,9},{2,18},{10... | collective-permute-start | bytes 184328 | tf_op jit(solution)/shard_map/ppermute | solution.py:34
  59.6 3.6 %collective-permute-start.7 = (bf16[256,1280]{1,0:T(8,128)(2,1)}, bf16[256,1280]{1,0:T(8,128)(2,1)S(1)}, u32[]{:S(2)}, u32[]{:S(2)}) collective-permute-start(bf16[256,1280]{1,0:T(8,128)(2,1)} %bitcast.10), channel_id=1, source_target_pairs={{0,1},{1,0},{2,3},{3,2},{4,5},{5,4},{6,7},{7,6},{8,9},{9,8},{10,11... | collective-permute-start | bytes 1966088 | tf_op jit(solution)/shard_map/ppermute | solution.py:34
  59.6 52.6 %collective-permute-start.8 = (bf16[960,1024]{1,0:T(8,128)(2,1)}, bf16[960,1024]{1,0:T(8,128)(2,1)S(1)}, u32[]{:S(2)}, u32[]{:S(2)}) collective-permute-start(bf16[960,1024]{1,0:T(8,128)(2,1)} %all-gather.3.cloned.1.call-done.refs_2_), channel_id=1, source_target_pairs={{0,8},{8,16},{16,24},{24,0},{1,9},{9,17},{17,25},{25,1},{2,10},{10... | collective-permute-start | bytes 5898248 | tf_op jit(solution)/shard_map/ppermute | solution.py:34
  61.1 52.8 %collective-permute-start.9 = (bf16[960,1024]{1,0:T(8,128)(2,1)}, bf16[960,1024]{1,0:T(8,128)(2,1)}, u32[]{:S(2)}, u32[]{:S(2)}) collective-permute-start(bf16[960,1024]{1,0:T(8,128)(2,1)} %all-gather.3.cloned.1.call-done.refs_2_), channel_id=1, source_target_pairs={{0,24},{8,0},{16,8},{24,16},{1,25},{9,1},{17,9},{25,17},{2,26},{10... | collective-permute-start | bytes 5898248 | tf_op jit(solution)/shard_map/ppermute | solution.py:34
  64.4 1.7 %copy-start.3 = (bf16[512,2560]{1,0:T(8,128)(2,1)S(1)}, bf16[512,2560]{1,0:T(8,128)(2,1)}, u32[]{:S(2)}) copy-start(bf16[512,2560]{1,0:T(8,128)(2,1)} %refs_2_.3) | copy-start | bytes 7864324
  66.1 1.8 %copy-start.2 = (bf16[512,1280]{1,0:T(8,128)(2,1)}, bf16[512,1280]{1,0:T(8,128)(2,1)S(1)}, u32[]{:S(2)}) copy-start(bf16[512,1280]{1,0:T(8,128)(2,1)S(1)} %pad_maximum_fusion.refs_0_.refs_1_) | copy-start | bytes 3932164
  68.5 2.0 %copy-start = (bf16[8,512,480]{2,1,0:T(8,128)(2,1)}, bf16[8,512,480]{2,1,0:T(8,128)(2,1)S(1)}, u32[]{:S(2)}) copy-start(bf16[8,512,480]{2,1,0:T(8,128)(2,1)S(1)} %shard_map.123.refs_1_) | copy-start | bytes 11796484
  104.8 42.2 %all-to-all-start = ((bf16[32,64,256]{2,1,0:T(8,128)(2,1)}), bf16[32,64,256]{2,1,0:T(8,128)(2,1)S(1)}, u32[]{:S(2)}, u32[]{:S(2)}) async-start(bf16[32,64,256]{2,1,0:T(8,128)(2,1)} %shard_map.131), calls=%async_computation | async-start | bytes 2097152 | tf_op jit(solution)/shard_map/all_to_all | solution.py:391
  112.2 3.9 %copy-start.5 = (bf16[960,1024]{1,0:T(8,128)(2,1)S(1)}, bf16[960,1024]{1,0:T(8,128)(2,1)}, u32[]{:S(2)}) copy-start(bf16[960,1024]{1,0:T(8,128)(2,1)} %all-gather.3.cloned.1.call-done.refs_2_) | copy-start | bytes 5898244
  112.3 29.4 %collective-permute-start.10 = (bf16[480,1024]{1,0:T(8,128)(2,1)S(1)}, bf16[480,1024]{1,0:T(8,128)(2,1)S(1)}, u32[]{:S(2)}, u32[]{:S(2)}) collective-permute-start(bf16[480,1024]{1,0:T(8,128)(2,1)S(1)} %slice.28), channel_id=1, source_target_pairs={{0,8},{8,16},{16,24},{24,0},{1,9},{9,17},{17,25},{25,1},{2,10},{10... | collective-permute-start | bytes 2949128 | tf_op jit(solution)/shard_map/ppermute | solution.py:34
  115.1 29.5 %collective-permute-start.11 = (bf16[480,1024]{1,0:T(8,128)(2,1)S(1)}, bf16[480,1024]{1,0:T(8,128)(2,1)S(1)}, u32[]{:S(2)}, u32[]{:S(2)}) collective-permute-start(bf16[480,1024]{1,0:T(8,128)(2,1)S(1)} %slice.29), channel_id=1, source_target_pairs={{0,24},{8,0},{16,8},{24,16},{1,25},{9,1},{17,9},{25,17},{2,26},{10... | collective-permute-start | bytes 2949128 | tf_op jit(solution)/shard_map/ppermute | solution.py:34
  116.1 2.2 %copy-start.1 = (bf16[8,512,480]{2,1,0:T(8,128)(2,1)S(1)}, bf16[8,512,480]{2,1,0:T(8,128)(2,1)}, u32[]{:S(2)}) copy-start(bf16[8,512,480]{2,1,0:T(8,128)(2,1)} %copy-done) | copy-start | bytes 11796484
Sparse Core Ops, SparseCore 0:
  9.8 43.9 all-gather.2
  57.6 41.2 all-gather.4

commit v2 on v1

--- a/solution.py
+++ b/solution.py
@@ -23,7 +23,7 @@
 I32 = jnp.int32
 VMEM_LIMIT = 14 * 2**20
 COST = 1
-FAR_COST = 10**9
+LAST_COST = 10**9
 RELAY_LIMIT = 56 * 2**20
 HOPS = (0, -1, 1, 2)
 HOPS = (0, -1, 1, 2)
@@ -122,11 +122,33 @@
         out[(x[0] + step) % NX] = value[...]
 
 
+def pair_body(which, own, other, out):
+    out[which[0]] = own[...]
+    out[1 - which[0]] = other[...]
+
+
+def pair(which, own, other):
+    return call(pair_body, shape((NC,) + own.shape), [which], [own, other])
+
+
 def in_order(x, parts, after):
     return call(block_body, shape((NX,) + parts[0].shape), [x], parts, after)
 
 
-def layer_body(core, tokens, fc1, fc2, send, keep):
+def layer_body(core, source, first, second, send, keep, tokens, fc1, fc2, sems):
+    parts = 4
+    pairs = []
+    for ref, place in ((source, tokens), (first, fc1), (second, fc2)):
+        rows = ref.shape[0] // parts
+        pairs += [
+            (ref.at[k * rows : (k + 1) * rows], place.at[k * rows : (k + 1) * rows])
+            for k in range(parts)
+        ]
+    copies = [pltpu.make_async_copy(s, d, sems.at[i]) for i, (s, d) in enumerate(pairs)]
+    for copy in copies:
+        copy.start()
+    for copy in copies:
+        copy.wait()
     half = tokens.shape[0] // NC
 
     def rows(which):
@@ -146,7 +168,23 @@
 
 def layer(core, tokens, fc1, fc2):
     dims = (NY, tokens.shape[0] // (NC * NY), tokens.shape[1])
-    return call(layer_body, [shape(dims), shape(dims, F32)], [core], [tokens, fc1, fc2])
+    smem, vmem, anywhere = (
+        pl.BlockSpec(memory_space=space) for space in (pltpu.SMEM, pltpu.VMEM, pl.ANY)
+    )
+    return pl.pallas_call(
+        layer_body,
+        in_specs=[smem] + [anywhere] * 3,
+        out_specs=[vmem] * 2,
+        out_shape=[shape(dims), shape(dims, F32)],
+        scratch_shapes=[
+            pltpu.VMEM(tokens.shape, BF),
+            pltpu.VMEM(fc1.shape, BF),
+            pltpu.VMEM(fc2.shape, BF),
+            pltpu.SemaphoreType.DMA((12,)),
+        ],
+        compiler_params=pltpu.CompilerParams(vmem_limit_bytes=RELAY_LIMIT),
+        cost_estimate=pl.CostEstimate(flops=COST, bytes_accessed=COST, transcendentals=0),
+    )(core, tokens, fc1, fc2)
 
 
 def regroup_body(shard, encoded, inter, out):
@@ -272,7 +310,9 @@
     return call(functools.partial(decode_body, tile_len), outs, [info], [arrived])
 
 
-def near_body(x, feats, own, left, right, out):
+def near_body(x, feats, own, left, right, out, across):
+    for half in range(2):
+        across[half] = feats[(x[0] + HOPS[-1]) % NX * 2 + half]
     mid = own.shape[0] // 2
     for step, weight in zip(HOPS, (own, left, right)):
         row = (x[0] + step) % NX * 2
@@ -284,26 +324,17 @@
 
 
 def near_sum(x, feats, weights):
-    dims = (feats.shape[1], weights[0].shape[1])
-    return call(near_body, shape(dims, F32), [x], [feats, *weights])
-
-
-def far_body(x, feats, first, second, out):
-    row = (x[0] + HOPS[-1]) % NX * 2
-    out[...] = dot(feats[row], first[...]) + dot(feats[row + 1], second[...])
-
-
-def far_sum(x, feats, weights):
-    dims = (feats.shape[1], weights[0].shape[1])
-    return call(far_body, shape(dims, F32), [x], [feats, *weights], cost=FAR_COST)
-
-
-def last_body(near, rest, out):
-    out[...] = (near[...] + rest[...]).astype(BF)
-
-
-def last_sum(near, rest):
-    return call(last_body, shape(near.shape), [], [near, rest])
+    outs = [shape((feats.shape[1], weights[0].shape[1]), F32), shape((2,) + feats.shape[1:])]
+    return call(near_body, outs, [x], [feats, *weights])
+
+
+def last_body(near, across, first, second, out):
+    total = dot(across[0], first[...]) + dot(across[1], second[...])
+    out[...] = (near[...] + total).astype(BF)
+
+
+def last_sum(near, across, far, after):
+    return call(last_body, shape(near.shape), [], [near, across, *far], after, cost=LAST_COST)
 
 
 def per_device(
@@ -361,15 +392,9 @@
     quarter = rows // (NC * NY)
     tokens_here = pick(vision_tokens.reshape(NC * NY, quarter, width), ci * NY + yi)
     piece = (tokens_here.astype(F32) + total).astype(BF)
-    pieces = place(jnp.zeros((NY,) + piece.shape, BF), piece, yi, 0)
     gathered = [shift(piece, "y", step) for step in (1, -1, 2)]
-    for step, value in zip((1, -1, 2), gathered):
-        pieces = place(pieces, value, (yi - step) % NY, 0)
-    pieces = pieces.reshape(rows // 2, width)
-    other = shift(pieces, "c", 1)
-    encoded = jnp.concatenate(
-        [jnp.where(ci == 0, pieces, other), jnp.where(ci == 0, other, pieces)], 0
-    )
+    pieces = in_order(there, [piece, *gathered], []).reshape(rows // 2, width)
+    encoded = pair(core, pieces, shift(pieces, "c", 1)).reshape(rows, width)
 
     joined = join(fold_own, fold_parts, [tick(v) for v in gathered])
     block = [joined, *(shift(joined, "x", step) for step in (1, -1, 2))]
@@ -391,8 +416,8 @@
     arrived = lax.all_to_all(outgoing, ("z", "x"), 0, 0, tiled=True)
     kv_cache, attended = decode(info, arrived, tile_len)
 
-    near = near_sum(column, feats, [late, left, right])
-    vision_states = last_sum(near, far_sum(column, feats, far))
+    near, across = near_sum(column, feats, [late, left, right])
+    vision_states = last_sum(near, across, far, [])
     return (vision_states, kv_cache, attended)
 
 

time: 157 us -> 154 us (0.981)
  local copies, waits for them, and re-layouts: 17.1 us -> 14.4 us
  Pallas kernels: 22.2 us -> 24.5 us
  other arithmetic: 4.81 us -> 2.89 us
    pallas_call x0 -> x1, Pallas kernels: none -> 5.06 us  [layer(): pl.pallas_call(layer_body, in_specs=[smem] + [anywhere] * 3, out_specs=[v...]
    ppermute x19, waiting for transfers between devices: 40.5 us -> 36.2 us  [shift(): return lax.ppermute(value, axis, [(i, (i + step) % n) for i in range(n)])]
    all_gather x1, waiting for transfers between devices: 0.59 us -> 3.78 us  [per_device(): late = lax.all_gather(proj_weight, 'z', axis=0, tiled=True)]
    pallas_call x11, Pallas kernels: 16.3 us -> 13.5 us  [call(): pl.pallas_call(kernel, in_specs=[smem] * len(scalars) + [pl.BlockSpec(mem...]
    dynamic_update_slice x3 -> x0, local copies, waits for them, and re-layouts: 2.04 us -> none  [place(): return lax.dynamic_update_index_in_dim(buffer, value, index, axis)]
    dynamic_update_slice x1 -> x0, other arithmetic: 1.7 us -> none  [place(): return lax.dynamic_update_index_in_dim(buffer, value, index, axis)]
    unnamed x24 -> x26, local copies, waits for them, and re-layouts: 11.6 us -> 11.8 us
  transfers between devices with their start and end apart: 22 -> 22, of which waited for: 12 -> 12; matrix products, arithmetic and copies ran while one was open for 7% -> 4% of each run, Pallas kernels for 12% -> 14%
where the time goes in v2:
time: 154 us
  waiting for transfers between devices  69.6 us (45%)
  starting transfers between devices  28.3 us (18%)
  Pallas kernels  24.5 us (16%)
  local copies, waits for them, and re-layouts  14.4 us (9%)
  between operations  14.3 us (9%)
  other arithmetic  2.89 us (2%)
    ppermute x19, waiting for transfers between devices, shift(): return lax.ppermute(value, axis, [(i, (i + step) % n) for i in range(n)])  36.2 us
    all_gather x1, waiting for transfers between devices, per_device(): early = lax.all_gather(block, 'z', axis=0, tiled=True)  28.9 us
    ppermute x19, starting transfers between devices, shift(): return lax.ppermute(value, axis, [(i, (i + step) % n) for i in range(n)])  20.8 us
    pallas_call x11, Pallas kernels, call(): pl.pallas_call(kernel, in_specs=[smem] * len(scalars) + [pl.BlockSpec(mem...  13.5 us
    unnamed x26, local copies, waits for them, and re-layouts  11.8 us
    all_to_all x1, starting transfers between devices, per_device(): arrived = lax.all_to_all(outgoing, ('z', 'x'), 0, 0, tiled=True)  7.37 us
    pallas_call x1, Pallas kernels, relay_rows(): pl.pallas_call(body, in_specs=[smem] + [hbm] * 3 + [vmem] * 3 + [hbm] * l...  5.88 us
    pallas_call x1, Pallas kernels, layer(): pl.pallas_call(layer_body, in_specs=[smem] + [anywhere] * 3, out_specs=[v...  5.06 us
  transfers between devices with their start and end apart: 22, of which 12 were waited for; matrix products, arithmetic and copies ran while one was open for 4% of the time, Pallas kernels for 14%

profile of v2, /device:TPU:2, one launch (start us, length us, event | category | flops | bytes accessed | tf_op | source)
XLA Modules:
  0.0 153.9 jit_solution(1733759504351748354)
XLA Ops:
  7.2 0.0 all-gather.3.cloned.1.call-start
  7.2 0.7 all-gather.3.cloned.1.call-update
  7.9 0.0 all-gather.5.cloned.1.call-start
  8.0 5.1 %shard_map.121 = (bf16[4,64,1280]{2,1,0:T(8,128)(2,1)}, f32[4,64,1280]{2,1,0:T(8,128)}) custom-call(s32[1]{0:T(128)} %bitcast.1.core.refs_0_, bf16[512,1280]{1,0:T(8,128)(2,1)} %source.1, bf16[320,1280]{1,0:T(8,128)(2,1)} %bitcast.30, bf16[320,1280]{1,0:T(8,128)(2,1)} %second.1), custom_call_target="tpu_custom_call" | custom-call | flops 1 | bytes 1 | tf_op jit(solution)/shard_map/pallas_call | solution.py:174
  13.0 0.1 collective-permute-start
  13.1 2.3 %collective-permute-done.refs_1_ = bf16[4,64,1280]{2,1,0:T(8,128)(2,1)S(1)} collective-permute-done((bf16[4,64,1280]{2,1,0:T(8,128)(2,1)}, bf16[4,64,1280]{2,1,0:T(8,128)(2,1)S(1)}, u32[]{:S(2)}, u32[]{:S(2)}) %collective-permute-start) | collective-permute-done | bytes 655392 | tf_op jit(solution)/shard_map/ppermute | solution.py:34
  15.4 1.3 copy-done.8
  16.7 0.1 shard_map.122
  16.9 1.7 %collective-permute-start.1 = (bf16[64,1280]{1,0:T(8,128)(2,1)S(1)}, bf16[64,1280]{1,0:T(8,128)(2,1)S(1)}, u32[]{:S(2)}, u32[]{:S(2)}) collective-permute-start(bf16[64,1280]{1,0:T(8,128)(2,1)S(1)} %get-tuple-element.22), channel_id=1, source_target_pairs={{0,2},{2,4},{4,6},{6,0},{1,3},{3,5},{5,7},{7,1},{8,10},{10,12},{12... | collective-permute-start | bytes 491528 | tf_op jit(solution)/shard_map/ppermute | solution.py:34
  18.5 1.7 %collective-permute-start.2 = (bf16[64,1280]{1,0:T(8,128)(2,1)S(1)}, bf16[64,1280]{1,0:T(8,128)(2,1)S(1)}, u32[]{:S(2)}, u32[]{:S(2)}) collective-permute-start(bf16[64,1280]{1,0:T(8,128)(2,1)S(1)} %get-tuple-element.23), channel_id=1, source_target_pairs={{0,6},{2,0},{4,2},{6,4},{1,7},{3,1},{5,3},{7,5},{8,14},{10,8},{12,... | collective-permute-start | bytes 491528 | tf_op jit(solution)/shard_map/ppermute | solution.py:34
  20.2 2.0 %collective-permute-start.3 = (bf16[64,1280]{1,0:T(8,128)(2,1)S(1)}, bf16[64,1280]{1,0:T(8,128)(2,1)S(1)}, u32[]{:S(2)}, u32[]{:S(2)}) collective-permute-start(bf16[64,1280]{1,0:T(8,128)(2,1)S(1)} %get-tuple-element.24), channel_id=1, source_target_pairs={{0,4},{2,6},{4,0},{6,2},{1,5},{3,7},{5,1},{7,3},{8,12},{10,14},{12... | collective-permute-start | bytes 491528 | tf_op jit(solution)/shard_map/ppermute | solution.py:34
  22.2 2.2 %copy-done.4 = bf16[1024,2048]{1,0:T(8,128)(2,1)S(1)} copy-done((bf16[1024,2048]{1,0:T(8,128)(2,1)S(1)}, bf16[1024,2048]{1,0:T(8,128)(2,1)}, u32[]{:S(2)}) %copy-start.4) | copy-done | bytes 4194328
  24.4 0.7 shard_map.128
  25.1 0.1 collective-permute-start.12
  25.2 2.1 %collective-permute-done.2 = bf16[64,1280]{1,0:T(8,128)(2,1)S(1)} collective-permute-done((bf16[64,1280]{1,0:T(8,128)(2,1)S(1)}, bf16[64,1280]{1,0:T(8,128)(2,1)S(1)}, u32[]{:S(2)}, u32[]{:S(2)}) %collective-permute-start.2) | collective-permute-done | bytes 163872 | tf_op jit(solution)/shard_map/ppermute | solution.py:34
  27.3 1.8 %collective-permute-done.3 = bf16[64,1280]{1,0:T(8,128)(2,1)S(1)} collective-permute-done((bf16[64,1280]{1,0:T(8,128)(2,1)S(1)}, bf16[64,1280]{1,0:T(8,128)(2,1)S(1)}, u32[]{:S(2)}, u32[]{:S(2)}) %collective-permute-start.3) | collective-permute-done | bytes 163872 | tf_op jit(solution)/shard_map/ppermute | solution.py:34
  29.1 1.0 fusion.refs_1_
  30.2 1.2 collective-permute-start.4
  31.4 2.1 %collective-permute-start.5 = (bf16[64,1280]{1,0:T(8,128)(2,1)S(1)}, bf16[64,1280]{1,0:T(8,128)(2,1)S(1)}, u32[]{:S(2)}, u32[]{:S(2)}) collective-permute-start(bf16[64,1280]{1,0:T(8,128)(2,1)S(1)} %fusion.refs_1_), channel_id=1, source_target_pairs={{0,6},{2,0},{4,2},{6,4},{1,7},{3,1},{5,3},{7,5},{8,14},{10,8},{12,... | collective-permute-start | bytes 491528 | tf_op jit(solution)/shard_map/ppermute | solution.py:34
  33.5 0.1 collective-permute-start.6
  33.6 0.1 shard_map.129
  33.7 1.5 collective-permute-start.13
  35.2 1.8 %collective-permute-start.14 = (bf16[120,256]{1,0:T(8,128)(2,1)S(1)}, bf16[120,256]{1,0:T(8,128)(2,1)S(1)}, u32[]{:S(2)}, u32[]{:S(2)}) collective-permute-start(bf16[120,256]{1,0:T(8,128)(2,1)S(1)} %get-tuple-element.31), channel_id=1, source_target_pairs={{0,6},{2,0},{4,2},{6,4},{1,7},{3,1},{5,3},{7,5},{8,14},{10,8},{12,... | collective-permute-start | bytes 184328 | tf_op jit(solution)/shard_map/ppermute | solution.py:34
  37.0 3.0 %collective-permute-done.4.refs_2_ = bf16[64,1280]{1,0:T(8,128)(2,1)S(1)} collective-permute-done((bf16[64,1280]{1,0:T(8,128)(2,1)S(1)}, bf16[64,1280]{1,0:T(8,128)(2,1)S(1)}, u32[]{:S(2)}, u32[]{:S(2)}) %collective-permute-start.4) | collective-permute-done | bytes 163872 | tf_op jit(solution)/shard_map/ppermute | solution.py:34
  40.0 1.7 %collective-permute-done.5.refs_3_ = bf16[64,1280]{1,0:T(8,128)(2,1)S(1)} collective-permute-done((bf16[64,1280]{1,0:T(8,128)(2,1)S(1)}, bf16[64,1280]{1,0:T(8,128)(2,1)S(1)}, u32[]{:S(2)}, u32[]{:S(2)}) %collective-permute-start.5) | collective-permute-done | bytes 163872 | tf_op jit(solution)/shard_map/ppermute | solution.py:34
  41.7 0.1 collective-permute-done.6.refs_4_
  41.8 0.6 collective-permute-done.13.refs_1_
  42.4 3.3 %collective-permute-done.15.refs_3_ = bf16[120,256]{1,0:T(8,128)(2,1)S(1)} collective-permute-done((bf16[120,256]{1,0:T(8,128)(2,1)S(1)}, bf16[120,256]{1,0:T(8,128)(2,1)S(1)}, u32[]{:S(2)}, u32[]{:S(2)}) %collective-permute-start.15) | collective-permute-done | bytes 61472 | tf_op jit(solution)/shard_map/ppermute | solution.py:34
  45.7 1.6 %collective-permute-start.16 = (bf16[120,256]{1,0:T(8,128)(2,1)S(1)}, bf16[120,256]{1,0:T(8,128)(2,1)S(1)}, u32[]{:S(2)}, u32[]{:S(2)}) collective-permute-start(bf16[120,256]{1,0:T(8,128)(2,1)S(1)} %shard_map.130.refs_1_), channel_id=1, source_target_pairs={{0,8},{8,16},{16,24},{24,0},{1,9},{9,17},{17,25},{25,1},{2,10},{10... | collective-permute-start | bytes 184328 | tf_op jit(solution)/shard_map/ppermute | solution.py:34
  47.3 0.5 collective-permute-start.17
  47.8 2.1 %collective-permute-start.18 = (bf16[120,256]{1,0:T(8,128)(2,1)S(1)}, bf16[120,256]{1,0:T(8,128)(2,1)S(1)}, u32[]{:S(2)}, u32[]{:S(2)}) collective-permute-start(bf16[120,256]{1,0:T(8,128)(2,1)S(1)} %shard_map.130.refs_1_), channel_id=1, source_target_pairs={{0,16},{8,24},{16,0},{24,8},{1,17},{9,25},{17,1},{25,9},{2,18},{10... | collective-permute-start | bytes 184328 | tf_op jit(solution)/shard_map/ppermute | solution.py:34
  50.0 3.8 %all-gather.3.cloned.1.call-done.refs_2_ = bf16[960,1024]{1,0:T(8,128)(2,1)} async-done(((bf16[120,1024]{1,0:T(8,128)(2,1)}), bf16[960,1024]{1,0:T(8,128)(2,1)}) %all-gather.3.cloned.1.call-update) | async-done | bytes 1966096 | tf_op jit(solution)/shard_map/all_gather | solution.py:363
  53.7 0.7 slice.33.refs_5_
  54.4 0.7 shard_map.131
  55.1 0.0 all-gather.5.cloned.1.call-update
  55.2 1.5 %collective-permute-start.8 = (bf16[960,1024]{1,0:T(8,128)(2,1)}, bf16[960,1024]{1,0:T(8,128)(2,1)S(1)}, u32[]{:S(2)}, u32[]{:S(2)}) collective-permute-start(bf16[960,1024]{1,0:T(8,128)(2,1)} %all-gather.3.cloned.1.call-done.refs_2_), channel_id=1, source_target_pairs={{0,8},{8,16},{16,24},{24,0},{1,9},{9,17},{17,25},{25,1},{2,10},{10... | collective-permute-start | bytes 5898248 | tf_op jit(solution)/shard_map/ppermute | solution.py:34
  56.7 0.6 collective-permute-start.9
  57.3 0.1 collective-permute-start.7
  57.4 0.0 copy-start.5
  57.4 0.8 copy-done.5
  58.3 0.6 compare_select_fusion.refs_0_
  58.9 0.2 convert_reduce_fusion
  59.0 0.8 and_convert_fusion.refs_4_
  59.8 1.1 copy-done.6
  60.9 0.1 shard_map.124
  61.0 2.2 %copy-done.3 = bf16[512,2560]{1,0:T(8,128)(2,1)S(1)} copy-done((bf16[512,2560]{1,0:T(8,128)(2,1)S(1)}, bf16[512,2560]{1,0:T(8,128)(2,1)}, u32[]{:S(2)}) %copy-start.3) | copy-done | bytes 2621464
  63.2 1.8 %shard_map.125.refs_1_ = bf16[8,512,480]{2,1,0:T(8,128)(2,1)S(1)} custom-call(bf16[512,1280]{1,0:T(8,128)(2,1)S(1)} %bitcast.25, bf16[512,2560]{1,0:T(8,128)(2,1)S(1)} %copy-done.3), custom_call_target="tpu_custom_call" | custom-call | flops 1 | bytes 1 | tf_op jit(solution)/shard_map/pallas_call | solution.py:69
  65.1 0.6 slice.34.refs_7_
  65.7 2.0 %copy-done = bf16[8,512,480]{2,1,0:T(8,128)(2,1)} copy-done((bf16[8,512,480]{2,1,0:T(8,128)(2,1)}, bf16[8,512,480]{2,1,0:T(8,128)(2,1)S(1)}, u32[]{:S(2)}) %copy-start) | copy-done | bytes 3932184
  67.6 28.9 %all-gather.5.cloned.1.call-done.refs_3_ = bf16[3840,256]{1,0:T(8,128)(2,1)} async-done(((bf16[480,256]{1,0:T(8,128)(2,1)}), bf16[3840,256]{1,0:T(8,128)(2,1)}) %all-gather.5.cloned.1.call-update) | async-done | bytes 1966096 | tf_op jit(solution)/shard_map/all_gather | solution.py:402
  96.5 5.9 %shard_map.132 = bf16[32,64,256]{2,1,0:T(8,128)(2,1)} custom-call(s32[16]{0:T(128)} %compare_select_fusion.refs_0_, bf16[512,1280]{1,0:T(8,128)(2,1)} %bitcast.26, bf16[512,2560]{1,0:T(8,128)(2,1)} %refs_2_.3, bf16[3840,256]{1,0:T(8,128)(2,1)} %all-gather.5.cloned.1.call-done.refs_3_, bf16[256,128]{1,0:T(8,128)(2,1)} %and_convert_fusion.refs_4_, ...), custom_call_target="tpu_custom_call" | custom-call | flops 1 | bytes 1 | tf_op jit(solution)/shard_map/pallas_call | solution.py:261
  102.4 7.4 %all-to-all-start = ((bf16[32,64,256]{2,1,0:T(8,128)(2,1)}), bf16[32,64,256]{2,1,0:T(8,128)(2,1)S(1)}, u32[]{:S(2)}, u32[]{:S(2)}) async-start(bf16[32,64,256]{2,1,0:T(8,128)(2,1)} %shard_map.132), calls=%async_computation | async-start | bytes 2097152 | tf_op jit(solution)/shard_map/all_to_all | solution.py:416
  109.8 0.1 slice.28
  109.9 1.5 %collective-permute-start.10 = (bf16[480,1024]{1,0:T(8,128)(2,1)S(1)}, bf16[480,1024]{1,0:T(8,128)(2,1)S(1)}, u32[]{:S(2)}, u32[]{:S(2)}) collective-permute-start(bf16[480,1024]{1,0:T(8,128)(2,1)S(1)} %slice.28), channel_id=1, source_target_pairs={{0,8},{8,16},{16,24},{24,0},{1,9},{9,17},{17,25},{25,1},{2,10},{10... | collective-permute-start | bytes 2949128 | tf_op jit(solution)/shard_map/ppermute | solution.py:34
  111.4 1.3 slice.29
  112.7 0.6 collective-permute-start.11
  113.3 0.1 fusion.3
  113.4 0.1 select_reduce_fusion.1
  113.7 2.2 %copy-done.1 = bf16[8,512,480]{2,1,0:T(8,128)(2,1)S(1)} copy-done((bf16[8,512,480]{2,1,0:T(8,128)(2,1)S(1)}, bf16[8,512,480]{2,1,0:T(8,128)(2,1)}, u32[]{:S(2)}) %copy-start.1) | copy-done | bytes 3932184
  115.8 5.0 %shard_map.126 = (f32[512,1024]{1,0:T(8,128)S(1)}, bf16[2,512,480]{2,1,0:T(8,128)(2,1)S(1)}) custom-call(s32[1]{0:T(128)} %bitcast.refs_0_, bf16[8,512,480]{2,1,0:T(8,128)(2,1)S(1)} %copy-done.1, bf16[960,1024]{1,0:T(8,128)(2,1)S(1)} %copy-done.7, bf16[960,1024]{1,0:T(8,128)(2,1)S(1)} %collective-permute-done.8.refs_3_, ...), custom_call_target="tpu_custom_call" | custom-call | flops 1 | bytes 1 | tf_op jit(solution)/shard_map/pallas_call | solution.py:69
  120.8 18.4 %collective-permute-done.10.refs_2_ = bf16[480,1024]{1,0:T(8,128)(2,1)S(1)} collective-permute-done((bf16[480,1024]{1,0:T(8,128)(2,1)S(1)}, bf16[480,1024]{1,0:T(8,128)(2,1)S(1)}, u32[]{:S(2)}, u32[]{:S(2)}) %collective-permute-start.10) | collective-permute-done | bytes 983072 | tf_op jit(solution)/shard_map/ppermute | solution.py:34
  139.3 2.9 %collective-permute-done.11.refs_3_ = bf16[480,1024]{1,0:T(8,128)(2,1)S(1)} collective-permute-done((bf16[480,1024]{1,0:T(8,128)(2,1)S(1)}, bf16[480,1024]{1,0:T(8,128)(2,1)S(1)}, u32[]{:S(2)}, u32[]{:S(2)}) %collective-permute-start.11) | collective-permute-done | bytes 983072 | tf_op jit(solution)/shard_map/ppermute | solution.py:34
  142.1 2.2 %shard_map.127 = bf16[512,1024]{1,0:T(8,128)(2,1)} custom-call(f32[512,1024]{1,0:T(8,128)S(1)} %get-tuple-element.25.refs_0_, bf16[2,512,480]{2,1,0:T(8,128)(2,1)S(1)} %get-tuple-element.26.refs_1_, bf16[480,1024]{1,0:T(8,128)(2,1)S(1)} %collective-permute-done.10.refs_2_, bf16[480,1024]{1,0:T(8,128)(2,1)S(1)} %collective-permute-done.11.refs_3_), custom_call_target="tpu_custom_call" | custom-call | flops 1000000000 | bytes 1000000000 | tf_op jit(solution)/shard_map/pallas_call | solution.py:69
  144.4 2.7 %shard_map.133 = (bf16[8,128,256]{2,1,0:T(8,128)(2,1)}, bf16[8,1024]{1,0:T(8,128)(2,1)}) custom-call(s32[3,8]{1,0:T(4,128)S(1)} %pad_add_fusion.refs_0_, bf16[32,64,256]{2,1,0:T(8,128)(2,1)S(1)} %all-to-all-done.refs_1_), custom_call_target="tpu_custom_call" | custom-call | flops 1 | bytes 1 | tf_op jit(solution)/shard_map/pallas_call | solution.py:69
  (40 shorter events, 0.2 us)
Async XLA Ops:
  7.2 46.6 %all-gather.3.cloned.1.call-start = ((), (), s32[]{:S(2)}) async-start(), calls=%async_computation.1 | async-start | bytes 2211840 | tf_op jit(solution)/shard_map/all_gather | solution.py:363
  7.9 88.6 %all-gather.5.cloned.1.call-start = ((), (), s32[]{:S(2)}) async-start(), calls=%async_computation.2 | async-start | bytes 2211840 | tf_op jit(solution)/shard_map/all_gather | solution.py:402
  8.0 14.2 %copy-start.9 = (bf16[120,1024]{1,0:T(8,128)(2,1)S(1)}, bf16[120,1024]{1,0:T(8,128)(2,1)}, u32[]{:S(2)}) copy-start(bf16[120,1024]{1,0:T(8,128)(2,1)} %refs_1_.3) | copy-start | bytes 737284
  13.0 2.4 %collective-permute-start = (bf16[4,64,1280]{2,1,0:T(8,128)(2,1)}, bf16[4,64,1280]{2,1,0:T(8,128)(2,1)S(1)}, u32[]{:S(2)}, u32[]{:S(2)}) collective-permute-start(bf16[4,64,1280]{2,1,0:T(8,128)(2,1)} %get-tuple-element.19.refs_3_), channel_id=1, source_target_pairs={{0,1},{1,0},{2,3},{3,2},{4,5},{5,4},{6,7},{7,6},{8,9},{9,8},{10,11... | collective-permute-start | bytes 1966088 | tf_op jit(solution)/shard_map/ppermute | solution.py:34
  15.4 1.3 copy-start.8
  16.7 5.4 %copy-start.10 = (bf16[4,64,1280]{2,1,0:T(8,128)(2,1)S(1)}, bf16[4,64,1280]{2,1,0:T(8,128)(2,1)}, u32[]{:S(2)}) copy-start(bf16[4,64,1280]{2,1,0:T(8,128)(2,1)} %get-tuple-element.19.refs_3_) | copy-start | bytes 1966084
  16.9 8.4 %collective-permute-start.1 = (bf16[64,1280]{1,0:T(8,128)(2,1)S(1)}, bf16[64,1280]{1,0:T(8,128)(2,1)S(1)}, u32[]{:S(2)}, u32[]{:S(2)}) collective-permute-start(bf16[64,1280]{1,0:T(8,128)(2,1)S(1)} %get-tuple-element.22), channel_id=1, source_target_pairs={{0,2},{2,4},{4,6},{6,0},{1,3},{3,5},{5,7},{7,1},{8,10},{10,12},{12... | collective-permute-start | bytes 491528 | tf_op jit(solution)/shard_map/ppermute | solution.py:34
  18.5 8.8 %collective-permute-start.2 = (bf16[64,1280]{1,0:T(8,128)(2,1)S(1)}, bf16[64,1280]{1,0:T(8,128)(2,1)S(1)}, u32[]{:S(2)}, u32[]{:S(2)}) collective-permute-start(bf16[64,1280]{1,0:T(8,128)(2,1)S(1)} %get-tuple-element.23), channel_id=1, source_target_pairs={{0,6},{2,0},{4,2},{6,4},{1,7},{3,1},{5,3},{7,5},{8,14},{10,8},{12,... | collective-permute-start | bytes 491528 | tf_op jit(solution)/shard_map/ppermute | solution.py:34
  20.2 9.0 %collective-permute-start.3 = (bf16[64,1280]{1,0:T(8,128)(2,1)S(1)}, bf16[64,1280]{1,0:T(8,128)(2,1)S(1)}, u32[]{:S(2)}, u32[]{:S(2)}) collective-permute-start(bf16[64,1280]{1,0:T(8,128)(2,1)S(1)} %get-tuple-element.24), channel_id=1, source_target_pairs={{0,4},{2,6},{4,0},{6,2},{1,5},{3,7},{5,1},{7,3},{8,12},{10,14},{12... | collective-permute-start | bytes 491528 | tf_op jit(solution)/shard_map/ppermute | solution.py:34
  22.2 2.2 %copy-start.4 = (bf16[1024,2048]{1,0:T(8,128)(2,1)S(1)}, bf16[1024,2048]{1,0:T(8,128)(2,1)}, u32[]{:S(2)}) copy-start(bf16[1024,2048]{1,0:T(8,128)(2,1)} %refs_2_.2) | copy-start | bytes 12582916
  25.1 8.5 %collective-permute-start.12 = (bf16[4,120,256]{2,1,0:T(8,128)(2,1)S(1)}, bf16[4,120,256]{2,1,0:T(8,128)(2,1)S(1)}, u32[]{:S(2)}, u32[]{:S(2)}) collective-permute-start(bf16[4,120,256]{2,1,0:T(8,128)(2,1)S(1)} %get-tuple-element.27), channel_id=1, source_target_pairs={{0,1},{1,0},{2,3},{3,2},{4,5},{5,4},{6,7},{7,6},{8,9},{9,8},{10,11... | collective-permute-start | bytes 737288 | tf_op jit(solution)/shard_map/ppermute | solution.py:34
  29.1 29.1 %copy-start.11 = (s32[128]{0:T(128)S(1)}, s32[128]{0:T(128)}, u32[]{:S(2)}) copy-start(s32[128]{0:T(128)} %param.17) | copy-start | bytes 1540
  29.1 29.1 %copy-start.12 = (s32[128]{0:T(128)S(1)}, s32[128]{0:T(128)}, u32[]{:S(2)}) copy-start(s32[128]{0:T(128)} %param.16) | copy-start | bytes 1540
  30.2 9.8 %collective-permute-start.4 = (bf16[64,1280]{1,0:T(8,128)(2,1)S(1)}, bf16[64,1280]{1,0:T(8,128)(2,1)S(1)}, u32[]{:S(2)}, u32[]{:S(2)}) collective-permute-start(bf16[64,1280]{1,0:T(8,128)(2,1)S(1)} %fusion.refs_1_), channel_id=1, source_target_pairs={{0,2},{2,4},{4,6},{6,0},{1,3},{3,5},{5,7},{7,1},{8,10},{10,12},{12... | collective-permute-start | bytes 491528 | tf_op jit(solution)/shard_map/ppermute | solution.py:34
  31.4 10.3 %collective-permute-start.5 = (bf16[64,1280]{1,0:T(8,128)(2,1)S(1)}, bf16[64,1280]{1,0:T(8,128)(2,1)S(1)}, u32[]{:S(2)}, u32[]{:S(2)}) collective-permute-start(bf16[64,1280]{1,0:T(8,128)(2,1)S(1)} %fusion.refs_1_), channel_id=1, source_target_pairs={{0,6},{2,0},{4,2},{6,4},{1,7},{3,1},{5,3},{7,5},{8,14},{10,8},{12,... | collective-permute-start | bytes 491528 | tf_op jit(solution)/shard_map/ppermute | solution.py:34
  33.5 8.3 %collective-permute-start.6 = (bf16[64,1280]{1,0:T(8,128)(2,1)S(1)}, bf16[64,1280]{1,0:T(8,128)(2,1)S(1)}, u32[]{:S(2)}, u32[]{:S(2)}) collective-permute-start(bf16[64,1280]{1,0:T(8,128)(2,1)S(1)} %fusion.refs_1_), channel_id=1, source_target_pairs={{0,4},{2,6},{4,0},{6,2},{1,5},{3,7},{5,1},{7,3},{8,12},{10,14},{12... | collective-permute-start | bytes 491528 | tf_op jit(solution)/shard_map/ppermute | solution.py:34
  33.7 8.7 %collective-permute-start.13 = (bf16[120,256]{1,0:T(8,128)(2,1)S(1)}, bf16[120,256]{1,0:T(8,128)(2,1)S(1)}, u32[]{:S(2)}, u32[]{:S(2)}) collective-permute-start(bf16[120,256]{1,0:T(8,128)(2,1)S(1)} %get-tuple-element.30), channel_id=1, source_target_pairs={{0,2},{2,4},{4,6},{6,0},{1,3},{3,5},{5,7},{7,1},{8,10},{10,12},{12... | collective-permute-start | bytes 184328 | tf_op jit(solution)/shard_map/ppermute | solution.py:34
  35.2 7.2 %collective-permute-start.14 = (bf16[120,256]{1,0:T(8,128)(2,1)S(1)}, bf16[120,256]{1,0:T(8,128)(2,1)S(1)}, u32[]{:S(2)}, u32[]{:S(2)}) collective-permute-start(bf16[120,256]{1,0:T(8,128)(2,1)S(1)} %get-tuple-element.31), channel_id=1, source_target_pairs={{0,6},{2,0},{4,2},{6,4},{1,7},{3,1},{5,3},{7,5},{8,14},{10,8},{12,... | collective-permute-start | bytes 184328 | tf_op jit(solution)/shard_map/ppermute | solution.py:34
  40.0 5.7 %collective-permute-start.15 = (bf16[120,256]{1,0:T(8,128)(2,1)S(1)}, bf16[120,256]{1,0:T(8,128)(2,1)S(1)}, u32[]{:S(2)}, u32[]{:S(2)}) collective-permute-start(bf16[120,256]{1,0:T(8,128)(2,1)S(1)} %get-tuple-element.32), channel_id=1, source_target_pairs={{0,4},{2,6},{4,0},{6,2},{1,5},{3,7},{5,1},{7,3},{8,12},{10,14},{12... | collective-permute-start | bytes 184328 | tf_op jit(solution)/shard_map/ppermute | solution.py:34
  45.7 8.7 %collective-permute-start.16 = (bf16[120,256]{1,0:T(8,128)(2,1)S(1)}, bf16[120,256]{1,0:T(8,128)(2,1)S(1)}, u32[]{:S(2)}, u32[]{:S(2)}) collective-permute-start(bf16[120,256]{1,0:T(8,128)(2,1)S(1)} %shard_map.130.refs_1_), channel_id=1, source_target_pairs={{0,8},{8,16},{16,24},{24,0},{1,9},{9,17},{17,25},{25,1},{2,10},{10... | collective-permute-start | bytes 184328 | tf_op jit(solution)/shard_map/ppermute | solution.py:34
  47.3 7.1 %collective-permute-start.17 = (bf16[120,256]{1,0:T(8,128)(2,1)S(1)}, bf16[120,256]{1,0:T(8,128)(2,1)S(1)}, u32[]{:S(2)}, u32[]{:S(2)}) collective-permute-start(bf16[120,256]{1,0:T(8,128)(2,1)S(1)} %shard_map.130.refs_1_), channel_id=1, source_target_pairs={{0,24},{8,0},{16,8},{24,16},{1,25},{9,1},{17,9},{25,17},{2,26},{10... | collective-permute-start | bytes 184328 | tf_op jit(solution)/shard_map/ppermute | solution.py:34
  47.8 6.6 %collective-permute-start.18 = (bf16[120,256]{1,0:T(8,128)(2,1)S(1)}, bf16[120,256]{1,0:T(8,128)(2,1)S(1)}, u32[]{:S(2)}, u32[]{:S(2)}) collective-permute-start(bf16[120,256]{1,0:T(8,128)(2,1)S(1)} %shard_map.130.refs_1_), channel_id=1, source_target_pairs={{0,16},{8,24},{16,0},{24,8},{1,17},{9,25},{17,1},{25,9},{2,18},{10... | collective-permute-start | bytes 184328 | tf_op jit(solution)/shard_map/ppermute | solution.py:34
  55.2 54.6 %collective-permute-start.8 = (bf16[960,1024]{1,0:T(8,128)(2,1)}, bf16[960,1024]{1,0:T(8,128)(2,1)S(1)}, u32[]{:S(2)}, u32[]{:S(2)}) collective-permute-start(bf16[960,1024]{1,0:T(8,128)(2,1)} %all-gather.3.cloned.1.call-done.refs_2_), channel_id=1, source_target_pairs={{0,8},{8,16},{16,24},{24,0},{1,9},{9,17},{17,25},{25,1},{2,10},{10... | collective-permute-start | bytes 5898248 | tf_op jit(solution)/shard_map/ppermute | solution.py:34
  56.7 54.7 %collective-permute-start.9 = (bf16[960,1024]{1,0:T(8,128)(2,1)}, bf16[960,1024]{1,0:T(8,128)(2,1)}, u32[]{:S(2)}, u32[]{:S(2)}) collective-permute-start(bf16[960,1024]{1,0:T(8,128)(2,1)} %all-gather.3.cloned.1.call-done.refs_2_), channel_id=1, source_target_pairs={{0,24},{8,0},{16,8},{24,16},{1,25},{9,1},{17,9},{25,17},{2,26},{10... | collective-permute-start | bytes 5898248 | tf_op jit(solution)/shard_map/ppermute | solution.py:34
  57.3 2.5 %collective-permute-start.7 = (bf16[256,1280]{1,0:T(8,128)(2,1)S(1)}, bf16[256,1280]{1,0:T(8,128)(2,1)S(1)}, u32[]{:S(2)}, u32[]{:S(2)}) collective-permute-start(bf16[256,1280]{1,0:T(8,128)(2,1)S(1)} %bitcast.27), channel_id=1, source_target_pairs={{0,1},{1,0},{2,3},{3,2},{4,5},{5,4},{6,7},{7,6},{8,9},{9,8},{10,11... | collective-permute-start | bytes 1966088 | tf_op jit(solution)/shard_map/ppermute | solution.py:34
  57.4 0.8 copy-start.5
  59.8 1.1 copy-start.6
  61.0 4.1 %copy-start.2 = (bf16[2,256,1280]{2,1,0:T(8,128)(2,1)}, bf16[2,256,1280]{2,1,0:T(8,128)(2,1)S(1)}, u32[]{:S(2)}) copy-start(bf16[2,256,1280]{2,1,0:T(8,128)(2,1)S(1)} %shard_map.124) | copy-start | bytes 3932164
  61.0 2.2 %copy-start.3 = (bf16[512,2560]{1,0:T(8,128)(2,1)S(1)}, bf16[512,2560]{1,0:T(8,128)(2,1)}, u32[]{:S(2)}) copy-start(bf16[512,2560]{1,0:T(8,128)(2,1)} %refs_2_.3) | copy-start | bytes 7864324
  65.7 2.0 %copy-start = (bf16[8,512,480]{2,1,0:T(8,128)(2,1)}, bf16[8,512,480]{2,1,0:T(8,128)(2,1)S(1)}, u32[]{:S(2)}) copy-start(bf16[8,512,480]{2,1,0:T(8,128)(2,1)S(1)} %shard_map.125.refs_1_) | copy-start | bytes 11796484
  102.4 42.0 %all-to-all-start = ((bf16[32,64,256]{2,1,0:T(8,128)(2,1)}), bf16[32,64,256]{2,1,0:T(8,128)(2,1)S(1)}, u32[]{:S(2)}, u32[]{:S(2)}) async-start(bf16[32,64,256]{2,1,0:T(8,128)(2,1)} %shard_map.132), calls=%async_computation | async-start | bytes 2097152 | tf_op jit(solution)/shard_map/all_to_all | solution.py:416
  109.8 3.9 %copy-start.7 = (bf16[960,1024]{1,0:T(8,128)(2,1)S(1)}, bf16[960,1024]{1,0:T(8,128)(2,1)}, u32[]{:S(2)}) copy-start(bf16[960,1024]{1,0:T(8,128)(2,1)} %all-gather.3.cloned.1.call-done.refs_2_) | copy-start | bytes 5898244
  109.9 29.4 %collective-permute-start.10 = (bf16[480,1024]{1,0:T(8,128)(2,1)S(1)}, bf16[480,1024]{1,0:T(8,128)(2,1)S(1)}, u32[]{:S(2)}, u32[]{:S(2)}) collective-permute-start(bf16[480,1024]{1,0:T(8,128)(2,1)S(1)} %slice.28), channel_id=1, source_target_pairs={{0,8},{8,16},{16,24},{24,0},{1,9},{9,17},{17,25},{25,1},{2,10},{10... | collective-permute-start | bytes 2949128 | tf_op jit(solution)/shard_map/ppermute | solution.py:34
  112.7 29.5 %collective-permute-start.11 = (bf16[480,1024]{1,0:T(8,128)(2,1)S(1)}, bf16[480,1024]{1,0:T(8,128)(2,1)S(1)}, u32[]{:S(2)}, u32[]{:S(2)}) collective-permute-start(bf16[480,1024]{1,0:T(8,128)(2,1)S(1)} %slice.29), channel_id=1, source_target_pairs={{0,24},{8,0},{16,8},{24,16},{1,25},{9,1},{17,9},{25,17},{2,26},{10... | collective-permute-start | bytes 2949128 | tf_op jit(solution)/shard_map/ppermute | solution.py:34
  113.6 2.2 %copy-start.1 = (bf16[8,512,480]{2,1,0:T(8,128)(2,1)S(1)}, bf16[8,512,480]{2,1,0:T(8,128)(2,1)}, u32[]{:S(2)}) copy-start(bf16[8,512,480]{2,1,0:T(8,128)(2,1)} %copy-done) | copy-start | bytes 11796484
Sparse Core Ops, SparseCore 0:
  9.8 43.9 all-gather.2
  56.1 40.3 all-gather.4

commit v3 on v2

--- a/solution.py
+++ b/solution.py
@@ -210,10 +210,16 @@
     steps = weight.shape[0] // split
     copies = []
     for k in range(steps):
-        rows = pl.ds(k * split, split)
-        source = encoded if k == 0 else inter.at[:, pl.ds((k - 1) * split, split)]
-        copies.append(pltpu.make_async_copy(source, features.at[k], sems.at[2 * k]))
-        copies.append(pltpu.make_async_copy(weight.at[rows], table.at[k], sems.at[2 * k + 1]))
+        for part in range(2):
+            tall, deep = encoded.shape[0] // 2, split // 2
+            rows = pl.ds(part * tall, tall)
+            columns = pl.ds(0 if k == 0 else (k - 1) * split, split)
+            source = (encoded if k == 0 else inter).at[rows, columns]
+            here = weight.at[pl.ds(k * split + part * deep, deep)]
+            there = table.at[k, pl.ds(part * deep, deep)]
+            sem = 4 * k + 2 * part
+            copies.append(pltpu.make_async_copy(source, features.at[k, rows], sems.at[sem]))
+            copies.append(pltpu.make_async_copy(here, there, sems.at[sem + 1]))
     for copy in copies:
         copy.start()
     out[:, :tile_len, :] = jnp.zeros((NIMG, tile_len, KVW), BF)
@@ -230,8 +236,8 @@
         out[:, start : start + 2 * CAP, :] = jnp.concatenate(pair, 1).astype(BF)
 
     for k in range(steps):
-        copies[2 * k].wait()
-        copies[2 * k + 1].wait()
+        for copy in copies[4 * k : 4 * k + 4]:
+            copy.wait()
         if k == 0:
             total[...] = dot(features[k], table[k])
         else:
@@ -267,7 +273,7 @@
             pltpu.VMEM((steps, rows, split), BF),
             pltpu.VMEM((steps, split, KVW), BF),
             pltpu.VMEM((rows, KVW), F32),
-            pltpu.SemaphoreType.DMA((2 * steps,)),
+            pltpu.SemaphoreType.DMA((4 * steps,)),
         ],
         compiler_params=pltpu.CompilerParams(vmem_limit_bytes=RELAY_LIMIT),
         cost_estimate=pl.CostEstimate(flops=COST, bytes_accessed=COST, transcendentals=0),
@@ -281,24 +287,33 @@
     queries = [
         rms_scale(sums[:, h * HD : (h + 1) * HD], 1e-06).reshape(-1, CAP, HD) for h in range(2)
     ]
+    stored, lives = [], []
+    for c in range(CAP):
+        block, present = info[0, c], info[1, c] > 0
+        rows = [arrived[j * groups + block, :tile_len, :] for j in range(TILES)]
+        rows = jnp.concatenate(rows, 0)
+        rows = jnp.where(present, rows, jnp.zeros_like(rows))
+        cache[c] = rows
+        stored.append(rows)
+        lives.append(present)
+    scores = []
+    for c in range(CAP):
+        heads = jnp.concatenate([q[:, c, :] for q in queries], 0).astype(BF)
+        scores.append(
+            lax.dot_general(
+                heads, stored[c][:, :HD], (((1,), (1,)), ((), ())), preferred_element_type=F32
+            )
+            / math.sqrt(HD)
+        )
+    tile = lax.broadcasted_iota(I32, (GROUP, length), 1) // tile_len
+    weights = [
+        jnp.where(tile < info[2, c], jnp.exp(scores[c]), 0.0).astype(BF) for c in range(CAP)
+    ]
     results = []
     for c in range(CAP):
-        block, present, count = info[0, c], info[1, c] > 0, info[2, c]
-        for j in range(TILES):
-            rows = arrived[j * groups + block, :tile_len, :]
-            cache[c, j * tile_len : (j + 1) * tile_len, :] = jnp.where(
-                present, rows, jnp.zeros_like(rows)
-            )
-        keys, values = cache[c, :, :HD], cache[c, :, HD:]
-        heads = jnp.concatenate([q[:, c, :] for q in queries], 0).astype(BF)
-        scores = lax.dot_general(
-            heads, keys, (((1,), (1,)), ((), ())), preferred_element_type=F32
-        ) / math.sqrt(HD)
-        tile = lax.broadcasted_iota(I32, (GROUP, length), 1) // tile_len
-        weights = jnp.where(tile < count, jnp.exp(scores), 0.0).astype(BF)
-        totals = jnp.sum(weights.astype(F32), -1, keepdims=True)
-        result = dot(weights, values) / totals
-        results.append(jnp.where(present, result, jnp.zeros_like(result)))
+        totals = jnp.sum(weights[c].astype(F32), -1, keepdims=True)
+        result = dot(weights[c], stored[c][:, HD:]) / totals
+        results.append(jnp.where(lives[c], result, jnp.zeros_like(result)))
     for row in range(GROUP):
         head = row % (GROUP // 2) * 2 + row // (GROUP // 2)
         column = jnp.concatenate([r[row : row + 1] for r in results], 0)

time: 154 us -> 154 us (level)
  no operation moved by 1% of the time
where the time goes in v3:
time: 154 us; the launch traced here: 153 us
  waiting for transfers between devices  69.6 us (45%)
  starting transfers between devices  28.3 us (18%)
  Pallas kernels  23.6 us (15%)
  local copies, waits for them, and re-layouts  14.4 us (9%)
  between operations  14.3 us (9%)
  other arithmetic  2.89 us (2%)
    ppermute x19, waiting for transfers between devices, shift(): return lax.ppermute(value, axis, [(i, (i + step) % n) for i in range(n)])  36.2 us
    all_gather x1, waiting for transfers between devices, per_device(): early = lax.all_gather(block, 'z', axis=0, tiled=True)  28.9 us
    ppermute x19, starting transfers between devices, shift(): return lax.ppermute(value, axis, [(i, (i + step) % n) for i in range(n)])  20.8 us
    pallas_call x11, Pallas kernels, call(): pl.pallas_call(kernel, in_specs=[smem] * len(scalars) + [pl.BlockSpec(mem...  12.6 us
    unnamed x26, local copies, waits for them, and re-layouts  11.8 us
    all_to_all x1, starting transfers between devices, per_device(): arrived = lax.all_to_all(outgoing, ('z', 'x'), 0, 0, tiled=True)  7.37 us
    pallas_call x1, Pallas kernels, relay_rows(): pl.pallas_call(body, in_specs=[smem] + [hbm] * 3 + [vmem] * 3 + [hbm] * l...  5.92 us
    pallas_call x1, Pallas kernels, layer(): pl.pallas_call(layer_body, in_specs=[smem] + [anywhere] * 3, out_specs=[v...  5.06 us
  transfers between devices with their start and end apart: 22, of which 12 were waited for; matrix products, arithmetic and copies ran while one was open for 4% of the time, Pallas kernels for 14%

profile of v3, /device:TPU:2, one launch (start us, length us, event | category | flops | bytes accessed | tf_op | source)
XLA Modules:
  0.0 153.0 jit_solution(13975312333163159325)
XLA Ops:
  7.2 0.0 all-gather.3.cloned.1.call-start
  7.2 0.7 all-gather.3.cloned.1.call-update
  7.9 0.0 all-gather.5.cloned.1.call-start
  8.0 5.1 %shard_map.121 = (bf16[4,64,1280]{2,1,0:T(8,128)(2,1)}, f32[4,64,1280]{2,1,0:T(8,128)}) custom-call(s32[1]{0:T(128)} %bitcast.1.core.refs_0_, bf16[512,1280]{1,0:T(8,128)(2,1)} %source.1, bf16[320,1280]{1,0:T(8,128)(2,1)} %bitcast.30, bf16[320,1280]{1,0:T(8,128)(2,1)} %second.1), custom_call_target="tpu_custom_call" | custom-call | flops 1 | bytes 1 | tf_op jit(solution)/shard_map/pallas_call | solution.py:174
  13.0 0.1 collective-permute-start
  13.1 2.3 %collective-permute-done.refs_1_ = bf16[4,64,1280]{2,1,0:T(8,128)(2,1)S(1)} collective-permute-done((bf16[4,64,1280]{2,1,0:T(8,128)(2,1)}, bf16[4,64,1280]{2,1,0:T(8,128)(2,1)S(1)}, u32[]{:S(2)}, u32[]{:S(2)}) %collective-permute-start) | collective-permute-done | bytes 655392 | tf_op jit(solution)/shard_map/ppermute | solution.py:34
  15.4 1.3 copy-done.8
  16.7 0.1 shard_map.122
  16.9 1.7 %collective-permute-start.1 = (bf16[64,1280]{1,0:T(8,128)(2,1)S(1)}, bf16[64,1280]{1,0:T(8,128)(2,1)S(1)}, u32[]{:S(2)}, u32[]{:S(2)}) collective-permute-start(bf16[64,1280]{1,0:T(8,128)(2,1)S(1)} %get-tuple-element.22), channel_id=1, source_target_pairs={{0,2},{2,4},{4,6},{6,0},{1,3},{3,5},{5,7},{7,1},{8,10},{10,12},{12... | collective-permute-start | bytes 491528 | tf_op jit(solution)/shard_map/ppermute | solution.py:34
  18.5 1.7 %collective-permute-start.2 = (bf16[64,1280]{1,0:T(8,128)(2,1)S(1)}, bf16[64,1280]{1,0:T(8,128)(2,1)S(1)}, u32[]{:S(2)}, u32[]{:S(2)}) collective-permute-start(bf16[64,1280]{1,0:T(8,128)(2,1)S(1)} %get-tuple-element.23), channel_id=1, source_target_pairs={{0,6},{2,0},{4,2},{6,4},{1,7},{3,1},{5,3},{7,5},{8,14},{10,8},{12,... | collective-permute-start | bytes 491528 | tf_op jit(solution)/shard_map/ppermute | solution.py:34
  20.2 2.0 %collective-permute-start.3 = (bf16[64,1280]{1,0:T(8,128)(2,1)S(1)}, bf16[64,1280]{1,0:T(8,128)(2,1)S(1)}, u32[]{:S(2)}, u32[]{:S(2)}) collective-permute-start(bf16[64,1280]{1,0:T(8,128)(2,1)S(1)} %get-tuple-element.24), channel_id=1, source_target_pairs={{0,4},{2,6},{4,0},{6,2},{1,5},{3,7},{5,1},{7,3},{8,12},{10,14},{12... | collective-permute-start | bytes 491528 | tf_op jit(solution)/shard_map/ppermute | solution.py:34
  22.2 2.2 %copy-done.4 = bf16[1024,2048]{1,0:T(8,128)(2,1)S(1)} copy-done((bf16[1024,2048]{1,0:T(8,128)(2,1)S(1)}, bf16[1024,2048]{1,0:T(8,128)(2,1)}, u32[]{:S(2)}) %copy-start.4) | copy-done | bytes 4194328
  24.4 0.7 shard_map.128
  25.1 0.1 collective-permute-start.12
  25.2 2.1 %collective-permute-done.2 = bf16[64,1280]{1,0:T(8,128)(2,1)S(1)} collective-permute-done((bf16[64,1280]{1,0:T(8,128)(2,1)S(1)}, bf16[64,1280]{1,0:T(8,128)(2,1)S(1)}, u32[]{:S(2)}, u32[]{:S(2)}) %collective-permute-start.2) | collective-permute-done | bytes 163872 | tf_op jit(solution)/shard_map/ppermute | solution.py:34
  27.3 1.8 %collective-permute-done.3 = bf16[64,1280]{1,0:T(8,128)(2,1)S(1)} collective-permute-done((bf16[64,1280]{1,0:T(8,128)(2,1)S(1)}, bf16[64,1280]{1,0:T(8,128)(2,1)S(1)}, u32[]{:S(2)}, u32[]{:S(2)}) %collective-permute-start.3) | collective-permute-done | bytes 163872 | tf_op jit(solution)/shard_map/ppermute | solution.py:34
  29.1 1.0 fusion.refs_1_
  30.2 1.2 collective-permute-start.4
  31.4 2.1 %collective-permute-start.5 = (bf16[64,1280]{1,0:T(8,128)(2,1)S(1)}, bf16[64,1280]{1,0:T(8,128)(2,1)S(1)}, u32[]{:S(2)}, u32[]{:S(2)}) collective-permute-start(bf16[64,1280]{1,0:T(8,128)(2,1)S(1)} %fusion.refs_1_), channel_id=1, source_target_pairs={{0,6},{2,0},{4,2},{6,4},{1,7},{3,1},{5,3},{7,5},{8,14},{10,8},{12,... | collective-permute-start | bytes 491528 | tf_op jit(solution)/shard_map/ppermute | solution.py:34
  33.5 0.1 collective-permute-start.6
  33.6 0.1 shard_map.129
  33.7 1.5 collective-permute-start.13
  35.2 1.8 %collective-permute-start.14 = (bf16[120,256]{1,0:T(8,128)(2,1)S(1)}, bf16[120,256]{1,0:T(8,128)(2,1)S(1)}, u32[]{:S(2)}, u32[]{:S(2)}) collective-permute-start(bf16[120,256]{1,0:T(8,128)(2,1)S(1)} %get-tuple-element.31), channel_id=1, source_target_pairs={{0,6},{2,0},{4,2},{6,4},{1,7},{3,1},{5,3},{7,5},{8,14},{10,8},{12,... | collective-permute-start | bytes 184328 | tf_op jit(solution)/shard_map/ppermute | solution.py:34
  37.0 3.0 %collective-permute-done.4.refs_2_ = bf16[64,1280]{1,0:T(8,128)(2,1)S(1)} collective-permute-done((bf16[64,1280]{1,0:T(8,128)(2,1)S(1)}, bf16[64,1280]{1,0:T(8,128)(2,1)S(1)}, u32[]{:S(2)}, u32[]{:S(2)}) %collective-permute-start.4) | collective-permute-done | bytes 163872 | tf_op jit(solution)/shard_map/ppermute | solution.py:34
  40.0 1.7 %collective-permute-done.5.refs_3_ = bf16[64,1280]{1,0:T(8,128)(2,1)S(1)} collective-permute-done((bf16[64,1280]{1,0:T(8,128)(2,1)S(1)}, bf16[64,1280]{1,0:T(8,128)(2,1)S(1)}, u32[]{:S(2)}, u32[]{:S(2)}) %collective-permute-start.5) | collective-permute-done | bytes 163872 | tf_op jit(solution)/shard_map/ppermute | solution.py:34
  41.7 0.1 collective-permute-done.6.refs_4_
  41.8 0.6 collective-permute-done.13.refs_1_
  42.4 3.3 %collective-permute-done.15.refs_3_ = bf16[120,256]{1,0:T(8,128)(2,1)S(1)} collective-permute-done((bf16[120,256]{1,0:T(8,128)(2,1)S(1)}, bf16[120,256]{1,0:T(8,128)(2,1)S(1)}, u32[]{:S(2)}, u32[]{:S(2)}) %collective-permute-start.15) | collective-permute-done | bytes 61472 | tf_op jit(solution)/shard_map/ppermute | solution.py:34
  45.7 1.6 %collective-permute-start.16 = (bf16[120,256]{1,0:T(8,128)(2,1)S(1)}, bf16[120,256]{1,0:T(8,128)(2,1)S(1)}, u32[]{:S(2)}, u32[]{:S(2)}) collective-permute-start(bf16[120,256]{1,0:T(8,128)(2,1)S(1)} %shard_map.130.refs_1_), channel_id=1, source_target_pairs={{0,8},{8,16},{16,24},{24,0},{1,9},{9,17},{17,25},{25,1},{2,10},{10... | collective-permute-start | bytes 184328 | tf_op jit(solution)/shard_map/ppermute | solution.py:34
  47.3 0.5 collective-permute-start.17
  47.8 2.1 %collective-permute-start.18 = (bf16[120,256]{1,0:T(8,128)(2,1)S(1)}, bf16[120,256]{1,0:T(8,128)(2,1)S(1)}, u32[]{:S(2)}, u32[]{:S(2)}) collective-permute-start(bf16[120,256]{1,0:T(8,128)(2,1)S(1)} %shard_map.130.refs_1_), channel_id=1, source_target_pairs={{0,16},{8,24},{16,0},{24,8},{1,17},{9,25},{17,1},{25,9},{2,18},{10... | collective-permute-start | bytes 184328 | tf_op jit(solution)/shard_map/ppermute | solution.py:34
  50.0 3.8 %all-gather.3.cloned.1.call-done.refs_2_ = bf16[960,1024]{1,0:T(8,128)(2,1)} async-done(((bf16[120,1024]{1,0:T(8,128)(2,1)}), bf16[960,1024]{1,0:T(8,128)(2,1)}) %all-gather.3.cloned.1.call-update) | async-done | bytes 1966096 | tf_op jit(solution)/shard_map/all_gather | solution.py:378
  53.7 0.7 slice.33.refs_5_
  54.4 0.7 shard_map.131
  55.1 0.0 all-gather.5.cloned.1.call-update
  55.2 1.5 %collective-permute-start.8 = (bf16[960,1024]{1,0:T(8,128)(2,1)}, bf16[960,1024]{1,0:T(8,128)(2,1)S(1)}, u32[]{:S(2)}, u32[]{:S(2)}) collective-permute-start(bf16[960,1024]{1,0:T(8,128)(2,1)} %all-gather.3.cloned.1.call-done.refs_2_), channel_id=1, source_target_pairs={{0,8},{8,16},{16,24},{24,0},{1,9},{9,17},{17,25},{25,1},{2,10},{10... | collective-permute-start | bytes 5898248 | tf_op jit(solution)/shard_map/ppermute | solution.py:34
  56.7 0.6 collective-permute-start.9
  57.3 0.1 collective-permute-start.7
  57.4 0.8 copy-done.5
  58.3 0.6 compare_select_fusion.refs_0_
  58.9 0.2 convert_reduce_fusion
  59.0 0.8 and_convert_fusion.refs_4_
  59.8 1.1 copy-done.6
  60.9 0.1 shard_map.124
  61.0 0.0 copy-start.3
  61.0 2.2 %copy-done.3 = bf16[512,2560]{1,0:T(8,128)(2,1)S(1)} copy-done((bf16[512,2560]{1,0:T(8,128)(2,1)S(1)}, bf16[512,2560]{1,0:T(8,128)(2,1)}, u32[]{:S(2)}) %copy-start.3) | copy-done | bytes 2621464
  63.2 1.8 %shard_map.125.refs_1_ = bf16[8,512,480]{2,1,0:T(8,128)(2,1)S(1)} custom-call(bf16[512,1280]{1,0:T(8,128)(2,1)S(1)} %bitcast.25, bf16[512,2560]{1,0:T(8,128)(2,1)S(1)} %copy-done.3), custom_call_target="tpu_custom_call" | custom-call | flops 1 | bytes 1 | tf_op jit(solution)/shard_map/pallas_call | solution.py:69
  65.1 0.6 slice.34.refs_7_
  65.7 2.0 %copy-done = bf16[8,512,480]{2,1,0:T(8,128)(2,1)} copy-done((bf16[8,512,480]{2,1,0:T(8,128)(2,1)}, bf16[8,512,480]{2,1,0:T(8,128)(2,1)S(1)}, u32[]{:S(2)}) %copy-start) | copy-done | bytes 3932184
  67.6 28.9 %all-gather.5.cloned.1.call-done.refs_3_ = bf16[3840,256]{1,0:T(8,128)(2,1)} async-done(((bf16[480,256]{1,0:T(8,128)(2,1)}), bf16[3840,256]{1,0:T(8,128)(2,1)}) %all-gather.5.cloned.1.call-update) | async-done | bytes 1966096 | tf_op jit(solution)/shard_map/all_gather | solution.py:417
  96.5 5.9 %shard_map.132 = bf16[32,64,256]{2,1,0:T(8,128)(2,1)} custom-call(s32[16]{0:T(128)} %compare_select_fusion.refs_0_, bf16[512,1280]{1,0:T(8,128)(2,1)} %bitcast.26, bf16[512,2560]{1,0:T(8,128)(2,1)} %refs_2_.3, bf16[3840,256]{1,0:T(8,128)(2,1)} %all-gather.5.cloned.1.call-done.refs_3_, bf16[256,128]{1,0:T(8,128)(2,1)} %and_convert_fusion.refs_4_, ...), custom_call_target="tpu_custom_call" | custom-call | flops 1 | bytes 1 | tf_op jit(solution)/shard_map/pallas_call | solution.py:267
  102.4 7.4 %all-to-all-start = ((bf16[32,64,256]{2,1,0:T(8,128)(2,1)}), bf16[32,64,256]{2,1,0:T(8,128)(2,1)S(1)}, u32[]{:S(2)}, u32[]{:S(2)}) async-start(bf16[32,64,256]{2,1,0:T(8,128)(2,1)} %shard_map.132), calls=%async_computation | async-start | bytes 2097152 | tf_op jit(solution)/shard_map/all_to_all | solution.py:431
  109.8 0.1 slice.28
  109.9 1.5 %collective-permute-start.10 = (bf16[480,1024]{1,0:T(8,128)(2,1)S(1)}, bf16[480,1024]{1,0:T(8,128)(2,1)S(1)}, u32[]{:S(2)}, u32[]{:S(2)}) collective-permute-start(bf16[480,1024]{1,0:T(8,128)(2,1)S(1)} %slice.28), channel_id=1, source_target_pairs={{0,8},{8,16},{16,24},{24,0},{1,9},{9,17},{17,25},{25,1},{2,10},{10... | collective-permute-start | bytes 2949128 | tf_op jit(solution)/shard_map/ppermute | solution.py:34
  111.4 1.3 slice.29
  112.7 0.6 collective-permute-start.11
  113.4 0.1 fusion.3
  113.5 0.1 select_reduce_fusion.1
  113.7 2.2 %copy-done.1 = bf16[8,512,480]{2,1,0:T(8,128)(2,1)S(1)} copy-done((bf16[8,512,480]{2,1,0:T(8,128)(2,1)S(1)}, bf16[8,512,480]{2,1,0:T(8,128)(2,1)}, u32[]{:S(2)}) %copy-start.1) | copy-done | bytes 3932184
  115.9 5.0 %shard_map.126 = (f32[512,1024]{1,0:T(8,128)S(1)}, bf16[2,512,480]{2,1,0:T(8,128)(2,1)S(1)}) custom-call(s32[1]{0:T(128)} %bitcast.refs_0_, bf16[8,512,480]{2,1,0:T(8,128)(2,1)S(1)} %copy-done.1, bf16[960,1024]{1,0:T(8,128)(2,1)S(1)} %copy-done.7, bf16[960,1024]{1,0:T(8,128)(2,1)S(1)} %collective-permute-done.8.refs_3_, ...), custom_call_target="tpu_custom_call" | custom-call | flops 1 | bytes 1 | tf_op jit(solution)/shard_map/pallas_call | solution.py:69
  120.9 18.4 %collective-permute-done.10.refs_2_ = bf16[480,1024]{1,0:T(8,128)(2,1)S(1)} collective-permute-done((bf16[480,1024]{1,0:T(8,128)(2,1)S(1)}, bf16[480,1024]{1,0:T(8,128)(2,1)S(1)}, u32[]{:S(2)}, u32[]{:S(2)}) %collective-permute-start.10) | collective-permute-done | bytes 983072 | tf_op jit(solution)/shard_map/ppermute | solution.py:34
  139.3 2.9 %collective-permute-done.11.refs_3_ = bf16[480,1024]{1,0:T(8,128)(2,1)S(1)} collective-permute-done((bf16[480,1024]{1,0:T(8,128)(2,1)S(1)}, bf16[480,1024]{1,0:T(8,128)(2,1)S(1)}, u32[]{:S(2)}, u32[]{:S(2)}) %collective-permute-start.11) | collective-permute-done | bytes 983072 | tf_op jit(solution)/shard_map/ppermute | solution.py:34
  142.2 2.2 %shard_map.127 = bf16[512,1024]{1,0:T(8,128)(2,1)} custom-call(f32[512,1024]{1,0:T(8,128)S(1)} %get-tuple-element.25.refs_0_, bf16[2,512,480]{2,1,0:T(8,128)(2,1)S(1)} %get-tuple-element.26.refs_1_, bf16[480,1024]{1,0:T(8,128)(2,1)S(1)} %collective-permute-done.10.refs_2_, bf16[480,1024]{1,0:T(8,128)(2,1)S(1)} %collective-permute-done.11.refs_3_), custom_call_target="tpu_custom_call" | custom-call | flops 1000000000 | bytes 1000000000 | tf_op jit(solution)/shard_map/pallas_call | solution.py:69
  144.4 1.8 %shard_map.133 = (bf16[8,128,256]{2,1,0:T(8,128)(2,1)}, bf16[8,1024]{1,0:T(8,128)(2,1)}) custom-call(s32[3,8]{1,0:T(4,128)S(1)} %pad_add_fusion.refs_0_, bf16[32,64,256]{2,1,0:T(8,128)(2,1)S(1)} %all-to-all-done.refs_1_), custom_call_target="tpu_custom_call" | custom-call | flops 1 | bytes 1 | tf_op jit(solution)/shard_map/pallas_call | solution.py:69
  (40 shorter events, 0.2 us)
Async XLA Ops:
  7.2 46.6 %all-gather.3.cloned.1.call-start = ((), (), s32[]{:S(2)}) async-start(), calls=%async_computation.1 | async-start | bytes 2211840 | tf_op jit(solution)/shard_map/all_gather | solution.py:378
  7.9 88.6 %all-gather.5.cloned.1.call-start = ((), (), s32[]{:S(2)}) async-start(), calls=%async_computation.2 | async-start | bytes 2211840 | tf_op jit(solution)/shard_map/all_gather | solution.py:417
  8.0 14.2 %copy-start.9 = (bf16[120,1024]{1,0:T(8,128)(2,1)S(1)}, bf16[120,1024]{1,0:T(8,128)(2,1)}, u32[]{:S(2)}) copy-start(bf16[120,1024]{1,0:T(8,128)(2,1)} %refs_1_.3) | copy-start | bytes 737284
  13.0 2.4 %collective-permute-start = (bf16[4,64,1280]{2,1,0:T(8,128)(2,1)}, bf16[4,64,1280]{2,1,0:T(8,128)(2,1)S(1)}, u32[]{:S(2)}, u32[]{:S(2)}) collective-permute-start(bf16[4,64,1280]{2,1,0:T(8,128)(2,1)} %get-tuple-element.19.refs_3_), channel_id=1, source_target_pairs={{0,1},{1,0},{2,3},{3,2},{4,5},{5,4},{6,7},{7,6},{8,9},{9,8},{10,11... | collective-permute-start | bytes 1966088 | tf_op jit(solution)/shard_map/ppermute | solution.py:34
  15.4 1.3 copy-start.8
  16.7 5.4 %copy-start.10 = (bf16[4,64,1280]{2,1,0:T(8,128)(2,1)S(1)}, bf16[4,64,1280]{2,1,0:T(8,128)(2,1)}, u32[]{:S(2)}) copy-start(bf16[4,64,1280]{2,1,0:T(8,128)(2,1)} %get-tuple-element.19.refs_3_) | copy-start | bytes 1966084
  16.9 8.4 %collective-permute-start.1 = (bf16[64,1280]{1,0:T(8,128)(2,1)S(1)}, bf16[64,1280]{1,0:T(8,128)(2,1)S(1)}, u32[]{:S(2)}, u32[]{:S(2)}) collective-permute-start(bf16[64,1280]{1,0:T(8,128)(2,1)S(1)} %get-tuple-element.22), channel_id=1, source_target_pairs={{0,2},{2,4},{4,6},{6,0},{1,3},{3,5},{5,7},{7,1},{8,10},{10,12},{12... | collective-permute-start | bytes 491528 | tf_op jit(solution)/shard_map/ppermute | solution.py:34
  18.5 8.8 %collective-permute-start.2 = (bf16[64,1280]{1,0:T(8,128)(2,1)S(1)}, bf16[64,1280]{1,0:T(8,128)(2,1)S(1)}, u32[]{:S(2)}, u32[]{:S(2)}) collective-permute-start(bf16[64,1280]{1,0:T(8,128)(2,1)S(1)} %get-tuple-element.23), channel_id=1, source_target_pairs={{0,6},{2,0},{4,2},{6,4},{1,7},{3,1},{5,3},{7,5},{8,14},{10,8},{12,... | collective-permute-start | bytes 491528 | tf_op jit(solution)/shard_map/ppermute | solution.py:34
  20.2 9.0 %collective-permute-start.3 = (bf16[64,1280]{1,0:T(8,128)(2,1)S(1)}, bf16[64,1280]{1,0:T(8,128)(2,1)S(1)}, u32[]{:S(2)}, u32[]{:S(2)}) collective-permute-start(bf16[64,1280]{1,0:T(8,128)(2,1)S(1)} %get-tuple-element.24), channel_id=1, source_target_pairs={{0,4},{2,6},{4,0},{6,2},{1,5},{3,7},{5,1},{7,3},{8,12},{10,14},{12... | collective-permute-start | bytes 491528 | tf_op jit(solution)/shard_map/ppermute | solution.py:34
  22.2 2.2 %copy-start.4 = (bf16[1024,2048]{1,0:T(8,128)(2,1)S(1)}, bf16[1024,2048]{1,0:T(8,128)(2,1)}, u32[]{:S(2)}) copy-start(bf16[1024,2048]{1,0:T(8,128)(2,1)} %refs_2_.2) | copy-start | bytes 12582916
  25.1 8.5 %collective-permute-start.12 = (bf16[4,120,256]{2,1,0:T(8,128)(2,1)S(1)}, bf16[4,120,256]{2,1,0:T(8,128)(2,1)S(1)}, u32[]{:S(2)}, u32[]{:S(2)}) collective-permute-start(bf16[4,120,256]{2,1,0:T(8,128)(2,1)S(1)} %get-tuple-element.27), channel_id=1, source_target_pairs={{0,1},{1,0},{2,3},{3,2},{4,5},{5,4},{6,7},{7,6},{8,9},{9,8},{10,11... | collective-permute-start | bytes 737288 | tf_op jit(solution)/shard_map/ppermute | solution.py:34
  29.1 29.1 %copy-start.11 = (s32[128]{0:T(128)S(1)}, s32[128]{0:T(128)}, u32[]{:S(2)}) copy-start(s32[128]{0:T(128)} %param.17) | copy-start | bytes 1540
  29.1 29.1 %copy-start.12 = (s32[128]{0:T(128)S(1)}, s32[128]{0:T(128)}, u32[]{:S(2)}) copy-start(s32[128]{0:T(128)} %param.16) | copy-start | bytes 1540
  30.2 9.8 %collective-permute-start.4 = (bf16[64,1280]{1,0:T(8,128)(2,1)S(1)}, bf16[64,1280]{1,0:T(8,128)(2,1)S(1)}, u32[]{:S(2)}, u32[]{:S(2)}) collective-permute-start(bf16[64,1280]{1,0:T(8,128)(2,1)S(1)} %fusion.refs_1_), channel_id=1, source_target_pairs={{0,2},{2,4},{4,6},{6,0},{1,3},{3,5},{5,7},{7,1},{8,10},{10,12},{12... | collective-permute-start | bytes 491528 | tf_op jit(solution)/shard_map/ppermute | solution.py:34
  31.4 10.3 %collective-permute-start.5 = (bf16[64,1280]{1,0:T(8,128)(2,1)S(1)}, bf16[64,1280]{1,0:T(8,128)(2,1)S(1)}, u32[]{:S(2)}, u32[]{:S(2)}) collective-permute-start(bf16[64,1280]{1,0:T(8,128)(2,1)S(1)} %fusion.refs_1_), channel_id=1, source_target_pairs={{0,6},{2,0},{4,2},{6,4},{1,7},{3,1},{5,3},{7,5},{8,14},{10,8},{12,... | collective-permute-start | bytes 491528 | tf_op jit(solution)/shard_map/ppermute | solution.py:34
  33.5 8.3 %collective-permute-start.6 = (bf16[64,1280]{1,0:T(8,128)(2,1)S(1)}, bf16[64,1280]{1,0:T(8,128)(2,1)S(1)}, u32[]{:S(2)}, u32[]{:S(2)}) collective-permute-start(bf16[64,1280]{1,0:T(8,128)(2,1)S(1)} %fusion.refs_1_), channel_id=1, source_target_pairs={{0,4},{2,6},{4,0},{6,2},{1,5},{3,7},{5,1},{7,3},{8,12},{10,14},{12... | collective-permute-start | bytes 491528 | tf_op jit(solution)/shard_map/ppermute | solution.py:34
  33.7 8.7 %collective-permute-start.13 = (bf16[120,256]{1,0:T(8,128)(2,1)S(1)}, bf16[120,256]{1,0:T(8,128)(2,1)S(1)}, u32[]{:S(2)}, u32[]{:S(2)}) collective-permute-start(bf16[120,256]{1,0:T(8,128)(2,1)S(1)} %get-tuple-element.30), channel_id=1, source_target_pairs={{0,2},{2,4},{4,6},{6,0},{1,3},{3,5},{5,7},{7,1},{8,10},{10,12},{12... | collective-permute-start | bytes 184328 | tf_op jit(solution)/shard_map/ppermute | solution.py:34
  35.2 7.2 %collective-permute-start.14 = (bf16[120,256]{1,0:T(8,128)(2,1)S(1)}, bf16[120,256]{1,0:T(8,128)(2,1)S(1)}, u32[]{:S(2)}, u32[]{:S(2)}) collective-permute-start(bf16[120,256]{1,0:T(8,128)(2,1)S(1)} %get-tuple-element.31), channel_id=1, source_target_pairs={{0,6},{2,0},{4,2},{6,4},{1,7},{3,1},{5,3},{7,5},{8,14},{10,8},{12,... | collective-permute-start | bytes 184328 | tf_op jit(solution)/shard_map/ppermute | solution.py:34
  40.0 5.7 %collective-permute-start.15 = (bf16[120,256]{1,0:T(8,128)(2,1)S(1)}, bf16[120,256]{1,0:T(8,128)(2,1)S(1)}, u32[]{:S(2)}, u32[]{:S(2)}) collective-permute-start(bf16[120,256]{1,0:T(8,128)(2,1)S(1)} %get-tuple-element.32), channel_id=1, source_target_pairs={{0,4},{2,6},{4,0},{6,2},{1,5},{3,7},{5,1},{7,3},{8,12},{10,14},{12... | collective-permute-start | bytes 184328 | tf_op jit(solution)/shard_map/ppermute | solution.py:34
  45.7 8.7 %collective-permute-start.16 = (bf16[120,256]{1,0:T(8,128)(2,1)S(1)}, bf16[120,256]{1,0:T(8,128)(2,1)S(1)}, u32[]{:S(2)}, u32[]{:S(2)}) collective-permute-start(bf16[120,256]{1,0:T(8,128)(2,1)S(1)} %shard_map.130.refs_1_), channel_id=1, source_target_pairs={{0,8},{8,16},{16,24},{24,0},{1,9},{9,17},{17,25},{25,1},{2,10},{10... | collective-permute-start | bytes 184328 | tf_op jit(solution)/shard_map/ppermute | solution.py:34
  47.3 7.1 %collective-permute-start.17 = (bf16[120,256]{1,0:T(8,128)(2,1)S(1)}, bf16[120,256]{1,0:T(8,128)(2,1)S(1)}, u32[]{:S(2)}, u32[]{:S(2)}) collective-permute-start(bf16[120,256]{1,0:T(8,128)(2,1)S(1)} %shard_map.130.refs_1_), channel_id=1, source_target_pairs={{0,24},{8,0},{16,8},{24,16},{1,25},{9,1},{17,9},{25,17},{2,26},{10... | collective-permute-start | bytes 184328 | tf_op jit(solution)/shard_map/ppermute | solution.py:34
  47.8 6.6 %collective-permute-start.18 = (bf16[120,256]{1,0:T(8,128)(2,1)S(1)}, bf16[120,256]{1,0:T(8,128)(2,1)S(1)}, u32[]{:S(2)}, u32[]{:S(2)}) collective-permute-start(bf16[120,256]{1,0:T(8,128)(2,1)S(1)} %shard_map.130.refs_1_), channel_id=1, source_target_pairs={{0,16},{8,24},{16,0},{24,8},{1,17},{9,25},{17,1},{25,9},{2,18},{10... | collective-permute-start | bytes 184328 | tf_op jit(solution)/shard_map/ppermute | solution.py:34
  55.2 54.6 %collective-permute-start.8 = (bf16[960,1024]{1,0:T(8,128)(2,1)}, bf16[960,1024]{1,0:T(8,128)(2,1)S(1)}, u32[]{:S(2)}, u32[]{:S(2)}) collective-permute-start(bf16[960,1024]{1,0:T(8,128)(2,1)} %all-gather.3.cloned.1.call-done.refs_2_), channel_id=1, source_target_pairs={{0,8},{8,16},{16,24},{24,0},{1,9},{9,17},{17,25},{25,1},{2,10},{10... | collective-permute-start | bytes 5898248 | tf_op jit(solution)/shard_map/ppermute | solution.py:34
  56.7 54.7 %collective-permute-start.9 = (bf16[960,1024]{1,0:T(8,128)(2,1)}, bf16[960,1024]{1,0:T(8,128)(2,1)}, u32[]{:S(2)}, u32[]{:S(2)}) collective-permute-start(bf16[960,1024]{1,0:T(8,128)(2,1)} %all-gather.3.cloned.1.call-done.refs_2_), channel_id=1, source_target_pairs={{0,24},{8,0},{16,8},{24,16},{1,25},{9,1},{17,9},{25,17},{2,26},{10... | collective-permute-start | bytes 5898248 | tf_op jit(solution)/shard_map/ppermute | solution.py:34
  57.3 2.5 %collective-permute-start.7 = (bf16[256,1280]{1,0:T(8,128)(2,1)S(1)}, bf16[256,1280]{1,0:T(8,128)(2,1)S(1)}, u32[]{:S(2)}, u32[]{:S(2)}) collective-permute-start(bf16[256,1280]{1,0:T(8,128)(2,1)S(1)} %bitcast.27), channel_id=1, source_target_pairs={{0,1},{1,0},{2,3},{3,2},{4,5},{5,4},{6,7},{7,6},{8,9},{9,8},{10,11... | collective-permute-start | bytes 1966088 | tf_op jit(solution)/shard_map/ppermute | solution.py:34
  57.4 0.8 copy-start.5
  59.8 1.1 copy-start.6
  61.0 4.1 %copy-start.2 = (bf16[2,256,1280]{2,1,0:T(8,128)(2,1)}, bf16[2,256,1280]{2,1,0:T(8,128)(2,1)S(1)}, u32[]{:S(2)}) copy-start(bf16[2,256,1280]{2,1,0:T(8,128)(2,1)S(1)} %shard_map.124) | copy-start | bytes 3932164
  61.0 2.2 %copy-start.3 = (bf16[512,2560]{1,0:T(8,128)(2,1)S(1)}, bf16[512,2560]{1,0:T(8,128)(2,1)}, u32[]{:S(2)}) copy-start(bf16[512,2560]{1,0:T(8,128)(2,1)} %refs_2_.3) | copy-start | bytes 7864324
  65.7 2.0 %copy-start = (bf16[8,512,480]{2,1,0:T(8,128)(2,1)}, bf16[8,512,480]{2,1,0:T(8,128)(2,1)S(1)}, u32[]{:S(2)}) copy-start(bf16[8,512,480]{2,1,0:T(8,128)(2,1)S(1)} %shard_map.125.refs_1_) | copy-start | bytes 11796484
  102.4 42.0 %all-to-all-start = ((bf16[32,64,256]{2,1,0:T(8,128)(2,1)}), bf16[32,64,256]{2,1,0:T(8,128)(2,1)S(1)}, u32[]{:S(2)}, u32[]{:S(2)}) async-start(bf16[32,64,256]{2,1,0:T(8,128)(2,1)} %shard_map.132), calls=%async_computation | async-start | bytes 2097152 | tf_op jit(solution)/shard_map/all_to_all | solution.py:431
  109.8 3.9 %copy-start.7 = (bf16[960,1024]{1,0:T(8,128)(2,1)S(1)}, bf16[960,1024]{1,0:T(8,128)(2,1)}, u32[]{:S(2)}) copy-start(bf16[960,1024]{1,0:T(8,128)(2,1)} %all-gather.3.cloned.1.call-done.refs_2_) | copy-start | bytes 5898244
  109.9 29.4 %collective-permute-start.10 = (bf16[480,1024]{1,0:T(8,128)(2,1)S(1)}, bf16[480,1024]{1,0:T(8,128)(2,1)S(1)}, u32[]{:S(2)}, u32[]{:S(2)}) collective-permute-start(bf16[480,1024]{1,0:T(8,128)(2,1)S(1)} %slice.28), channel_id=1, source_target_pairs={{0,8},{8,16},{16,24},{24,0},{1,9},{9,17},{17,25},{25,1},{2,10},{10... | collective-permute-start | bytes 2949128 | tf_op jit(solution)/shard_map/ppermute | solution.py:34
  112.7 29.5 %collective-permute-start.11 = (bf16[480,1024]{1,0:T(8,128)(2,1)S(1)}, bf16[480,1024]{1,0:T(8,128)(2,1)S(1)}, u32[]{:S(2)}, u32[]{:S(2)}) collective-permute-start(bf16[480,1024]{1,0:T(8,128)(2,1)S(1)} %slice.29), channel_id=1, source_target_pairs={{0,24},{8,0},{16,8},{24,16},{1,25},{9,1},{17,9},{25,17},{2,26},{10... | collective-permute-start | bytes 2949128 | tf_op jit(solution)/shard_map/ppermute | solution.py:34
  113.7 2.2 %copy-start.1 = (bf16[8,512,480]{2,1,0:T(8,128)(2,1)S(1)}, bf16[8,512,480]{2,1,0:T(8,128)(2,1)}, u32[]{:S(2)}) copy-start(bf16[8,512,480]{2,1,0:T(8,128)(2,1)} %copy-done) | copy-start | bytes 11796484
Sparse Core Ops, SparseCore 0:
  9.8 43.9 all-gather.2
  56.1 40.3 all-gather.4

commit v4 on v3

--- a/solution.py
+++ b/solution.py
@@ -343,13 +343,47 @@
     return call(near_body, outs, [x], [feats, *weights])
 
 
-def last_body(near, across, first, second, out):
-    total = dot(across[0], first[...]) + dot(across[1], second[...])
-    out[...] = (near[...] + total).astype(BF)
-
-
-def last_sum(near, across, far, after):
-    return call(last_body, shape(near.shape), [], [near, across, *far], after, cost=LAST_COST)
+def last_body(near, across, first, second, out, places, total, done, sems):
+    copies = [
+        pltpu.make_async_copy(w, places.at[k], sems.at[k]) for k, w in enumerate((first, second))
+    ]
+    for copy in copies:
+        copy.start()
+    copies[0].wait()
+    total[...] = near[...] + dot(across[0], places[0])
+    copies[1].wait()
+    width = done.shape[1] // 2
+    writes = []
+    for k in range(2):
+        columns = slice(k * width, (k + 1) * width)
+        term = dot(across[1], places[1, :, columns])
+        done[:, columns] = (total[:, columns] + term).astype(BF)
+        writes.append(
+            pltpu.make_async_copy(done.at[:, columns], out.at[:, columns], sems.at[2 + k])
+        )
+        writes[k].start()
+    for write in writes:
+        write.wait()
+
+
+def last_sum(near, across, far):
+    vmem, anywhere = (pl.BlockSpec(memory_space=space) for space in (pltpu.VMEM, pl.ANY))
+    return pl.pallas_call(
+        last_body,
+        in_specs=[vmem] * 2 + [anywhere] * 2,
+        out_specs=anywhere,
+        out_shape=shape(near.shape),
+        scratch_shapes=[
+            pltpu.VMEM((2,) + far[0].shape, BF),
+            pltpu.VMEM(near.shape, F32),
+            pltpu.VMEM(near.shape, BF),
+            pltpu.SemaphoreType.DMA((4,)),
+        ],
+        compiler_params=pltpu.CompilerParams(vmem_limit_bytes=VMEM_LIMIT),
+        cost_estimate=pl.CostEstimate(
+            flops=LAST_COST, bytes_accessed=LAST_COST, transcendentals=0
+        ),
+    )(near, across, *far)
 
 
 def per_device(
@@ -432,7 +466,7 @@
     kv_cache, attended = decode(info, arrived, tile_len)
 
     near, across = near_sum(column, feats, [late, left, right])
-    vision_states = last_sum(near, across, far, [])
+    vision_states = last_sum(near, across, far)
     return (vision_states, kv_cache, attended)
 
 

time: 154 us -> 154 us (level)
    pallas_call x0 -> x1, Pallas kernels: none -> 2.87 us  [last_sum(): pl.pallas_call(last_body, in_specs=[vmem] * 2 + [anywhere] * 2, out_specs...]
    pallas_call x11 -> x10, Pallas kernels: 12.6 us -> 10.4 us  [call(): pl.pallas_call(kernel, in_specs=[smem] * len(scalars) + [pl.BlockSpec(mem...]
where the time goes in v4:
time: 154 us
  waiting for transfers between devices  69.4 us (45%)
  starting transfers between devices  28.5 us (19%)
  Pallas kernels  24.2 us (16%)
  local copies, waits for them, and re-layouts  14.4 us (9%)
  between operations  14.3 us (9%)
  other arithmetic  2.89 us (2%)
    ppermute x19, waiting for transfers between devices, shift(): return lax.ppermute(value, axis, [(i, (i + step) % n) for i in range(n)])  36.1 us
    all_gather x1, waiting for transfers between devices, per_device(): early = lax.all_gather(block, 'z', axis=0, tiled=True)  28.9 us
    ppermute x19, starting transfers between devices, shift(): return lax.ppermute(value, axis, [(i, (i + step) % n) for i in range(n)])  21 us
    unnamed x26, local copies, waits for them, and re-layouts  11.8 us
    pallas_call x10, Pallas kernels, call(): pl.pallas_call(kernel, in_specs=[smem] * len(scalars) + [pl.BlockSpec(mem...  10.4 us
    all_to_all x1, starting transfers between devices, per_device(): arrived = lax.all_to_all(outgoing, ('z', 'x'), 0, 0, tiled=True)  7.37 us
    pallas_call x1, Pallas kernels, relay_rows(): pl.pallas_call(body, in_specs=[smem] + [hbm] * 3 + [vmem] * 3 + [hbm] * l...  5.92 us
    pallas_call x1, Pallas kernels, layer(): pl.pallas_call(layer_body, in_specs=[smem] + [anywhere] * 3, out_specs=[v...  5.06 us
  transfers between devices with their start and end apart: 22, of which 12 were waited for; matrix products, arithmetic and copies ran while one was open for 4% of the time, Pallas kernels for 14%

profile of v4, /device:TPU:2, one launch (start us, length us, event | category | flops | bytes accessed | tf_op | source)
XLA Modules:
  0.0 153.8 jit_solution(11709636561735290197)
XLA Ops:
  7.2 0.0 all-gather.3.cloned.1.call-start
  7.2 0.7 all-gather.3.cloned.1.call-update
  7.9 0.0 all-gather.5.cloned.1.call-start
  8.0 5.1 %shard_map.121 = (bf16[4,64,1280]{2,1,0:T(8,128)(2,1)}, f32[4,64,1280]{2,1,0:T(8,128)}) custom-call(s32[1]{0:T(128)} %bitcast.1.core.refs_0_, bf16[512,1280]{1,0:T(8,128)(2,1)} %source.1, bf16[320,1280]{1,0:T(8,128)(2,1)} %bitcast.30, bf16[320,1280]{1,0:T(8,128)(2,1)} %second.1), custom_call_target="tpu_custom_call" | custom-call | flops 1 | bytes 1 | tf_op jit(solution)/shard_map/pallas_call | solution.py:174
  13.0 0.1 collective-permute-start
  13.1 2.3 %collective-permute-done.refs_1_ = bf16[4,64,1280]{2,1,0:T(8,128)(2,1)S(1)} collective-permute-done((bf16[4,64,1280]{2,1,0:T(8,128)(2,1)}, bf16[4,64,1280]{2,1,0:T(8,128)(2,1)S(1)}, u32[]{:S(2)}, u32[]{:S(2)}) %collective-permute-start) | collective-permute-done | bytes 655392 | tf_op jit(solution)/shard_map/ppermute | solution.py:34
  15.4 1.3 copy-done.8
  16.7 0.1 shard_map.122
  16.9 1.7 %collective-permute-start.1 = (bf16[64,1280]{1,0:T(8,128)(2,1)S(1)}, bf16[64,1280]{1,0:T(8,128)(2,1)S(1)}, u32[]{:S(2)}, u32[]{:S(2)}) collective-permute-start(bf16[64,1280]{1,0:T(8,128)(2,1)S(1)} %get-tuple-element.22), channel_id=1, source_target_pairs={{0,2},{2,4},{4,6},{6,0},{1,3},{3,5},{5,7},{7,1},{8,10},{10,12},{12... | collective-permute-start | bytes 491528 | tf_op jit(solution)/shard_map/ppermute | solution.py:34
  18.5 1.7 %collective-permute-start.2 = (bf16[64,1280]{1,0:T(8,128)(2,1)S(1)}, bf16[64,1280]{1,0:T(8,128)(2,1)S(1)}, u32[]{:S(2)}, u32[]{:S(2)}) collective-permute-start(bf16[64,1280]{1,0:T(8,128)(2,1)S(1)} %get-tuple-element.23), channel_id=1, source_target_pairs={{0,6},{2,0},{4,2},{6,4},{1,7},{3,1},{5,3},{7,5},{8,14},{10,8},{12,... | collective-permute-start | bytes 491528 | tf_op jit(solution)/shard_map/ppermute | solution.py:34
  20.2 2.0 %collective-permute-start.3 = (bf16[64,1280]{1,0:T(8,128)(2,1)S(1)}, bf16[64,1280]{1,0:T(8,128)(2,1)S(1)}, u32[]{:S(2)}, u32[]{:S(2)}) collective-permute-start(bf16[64,1280]{1,0:T(8,128)(2,1)S(1)} %get-tuple-element.24), channel_id=1, source_target_pairs={{0,4},{2,6},{4,0},{6,2},{1,5},{3,7},{5,1},{7,3},{8,12},{10,14},{12... | collective-permute-start | bytes 491528 | tf_op jit(solution)/shard_map/ppermute | solution.py:34
  22.2 2.2 %copy-done.4 = bf16[1024,2048]{1,0:T(8,128)(2,1)S(1)} copy-done((bf16[1024,2048]{1,0:T(8,128)(2,1)S(1)}, bf16[1024,2048]{1,0:T(8,128)(2,1)}, u32[]{:S(2)}) %copy-start.4) | copy-done | bytes 4194328
  24.4 0.7 shard_map.128
  25.1 0.1 collective-permute-start.12
  25.2 2.1 %collective-permute-done.2 = bf16[64,1280]{1,0:T(8,128)(2,1)S(1)} collective-permute-done((bf16[64,1280]{1,0:T(8,128)(2,1)S(1)}, bf16[64,1280]{1,0:T(8,128)(2,1)S(1)}, u32[]{:S(2)}, u32[]{:S(2)}) %collective-permute-start.2) | collective-permute-done | bytes 163872 | tf_op jit(solution)/shard_map/ppermute | solution.py:34
  27.3 1.8 %collective-permute-done.3 = bf16[64,1280]{1,0:T(8,128)(2,1)S(1)} collective-permute-done((bf16[64,1280]{1,0:T(8,128)(2,1)S(1)}, bf16[64,1280]{1,0:T(8,128)(2,1)S(1)}, u32[]{:S(2)}, u32[]{:S(2)}) %collective-permute-start.3) | collective-permute-done | bytes 163872 | tf_op jit(solution)/shard_map/ppermute | solution.py:34
  29.1 1.0 fusion.refs_1_
  30.2 1.2 collective-permute-start.4
  31.4 2.1 %collective-permute-start.5 = (bf16[64,1280]{1,0:T(8,128)(2,1)S(1)}, bf16[64,1280]{1,0:T(8,128)(2,1)S(1)}, u32[]{:S(2)}, u32[]{:S(2)}) collective-permute-start(bf16[64,1280]{1,0:T(8,128)(2,1)S(1)} %fusion.refs_1_), channel_id=1, source_target_pairs={{0,6},{2,0},{4,2},{6,4},{1,7},{3,1},{5,3},{7,5},{8,14},{10,8},{12,... | collective-permute-start | bytes 491528 | tf_op jit(solution)/shard_map/ppermute | solution.py:34
  33.5 0.1 collective-permute-start.6
  33.6 0.1 shard_map.129
  33.7 1.5 collective-permute-start.13
  35.2 1.8 %collective-permute-start.14 = (bf16[120,256]{1,0:T(8,128)(2,1)S(1)}, bf16[120,256]{1,0:T(8,128)(2,1)S(1)}, u32[]{:S(2)}, u32[]{:S(2)}) collective-permute-start(bf16[120,256]{1,0:T(8,128)(2,1)S(1)} %get-tuple-element.31), channel_id=1, source_target_pairs={{0,6},{2,0},{4,2},{6,4},{1,7},{3,1},{5,3},{7,5},{8,14},{10,8},{12,... | collective-permute-start | bytes 184328 | tf_op jit(solution)/shard_map/ppermute | solution.py:34
  37.0 3.0 %collective-permute-done.4.refs_2_ = bf16[64,1280]{1,0:T(8,128)(2,1)S(1)} collective-permute-done((bf16[64,1280]{1,0:T(8,128)(2,1)S(1)}, bf16[64,1280]{1,0:T(8,128)(2,1)S(1)}, u32[]{:S(2)}, u32[]{:S(2)}) %collective-permute-start.4) | collective-permute-done | bytes 163872 | tf_op jit(solution)/shard_map/ppermute | solution.py:34
  40.0 1.7 %collective-permute-done.5.refs_3_ = bf16[64,1280]{1,0:T(8,128)(2,1)S(1)} collective-permute-done((bf16[64,1280]{1,0:T(8,128)(2,1)S(1)}, bf16[64,1280]{1,0:T(8,128)(2,1)S(1)}, u32[]{:S(2)}, u32[]{:S(2)}) %collective-permute-start.5) | collective-permute-done | bytes 163872 | tf_op jit(solution)/shard_map/ppermute | solution.py:34
  41.7 0.1 collective-permute-done.6.refs_4_
  41.8 0.6 collective-permute-done.13.refs_1_
  42.4 3.3 %collective-permute-done.15.refs_3_ = bf16[120,256]{1,0:T(8,128)(2,1)S(1)} collective-permute-done((bf16[120,256]{1,0:T(8,128)(2,1)S(1)}, bf16[120,256]{1,0:T(8,128)(2,1)S(1)}, u32[]{:S(2)}, u32[]{:S(2)}) %collective-permute-start.15) | collective-permute-done | bytes 61472 | tf_op jit(solution)/shard_map/ppermute | solution.py:34
  45.7 1.6 %collective-permute-start.16 = (bf16[120,256]{1,0:T(8,128)(2,1)S(1)}, bf16[120,256]{1,0:T(8,128)(2,1)S(1)}, u32[]{:S(2)}, u32[]{:S(2)}) collective-permute-start(bf16[120,256]{1,0:T(8,128)(2,1)S(1)} %shard_map.130.refs_1_), channel_id=1, source_target_pairs={{0,8},{8,16},{16,24},{24,0},{1,9},{9,17},{17,25},{25,1},{2,10},{10... | collective-permute-start | bytes 184328 | tf_op jit(solution)/shard_map/ppermute | solution.py:34
  47.3 0.5 collective-permute-start.17
  47.8 2.1 %collective-permute-start.18 = (bf16[120,256]{1,0:T(8,128)(2,1)S(1)}, bf16[120,256]{1,0:T(8,128)(2,1)S(1)}, u32[]{:S(2)}, u32[]{:S(2)}) collective-permute-start(bf16[120,256]{1,0:T(8,128)(2,1)S(1)} %shard_map.130.refs_1_), channel_id=1, source_target_pairs={{0,16},{8,24},{16,0},{24,8},{1,17},{9,25},{17,1},{25,9},{2,18},{10... | collective-permute-start | bytes 184328 | tf_op jit(solution)/shard_map/ppermute | solution.py:34
  50.0 3.8 %all-gather.3.cloned.1.call-done.refs_2_ = bf16[960,1024]{1,0:T(8,128)(2,1)} async-done(((bf16[120,1024]{1,0:T(8,128)(2,1)}), bf16[960,1024]{1,0:T(8,128)(2,1)}) %all-gather.3.cloned.1.call-update) | async-done | bytes 1966096 | tf_op jit(solution)/shard_map/all_gather | solution.py:412
  53.7 0.7 slice.33.refs_5_
  54.4 0.7 shard_map.131
  55.1 0.0 all-gather.5.cloned.1.call-update
  55.2 1.5 %collective-permute-start.8 = (bf16[960,1024]{1,0:T(8,128)(2,1)}, bf16[960,1024]{1,0:T(8,128)(2,1)S(1)}, u32[]{:S(2)}, u32[]{:S(2)}) collective-permute-start(bf16[960,1024]{1,0:T(8,128)(2,1)} %all-gather.3.cloned.1.call-done.refs_2_), channel_id=1, source_target_pairs={{0,8},{8,16},{16,24},{24,0},{1,9},{9,17},{17,25},{25,1},{2,10},{10... | collective-permute-start | bytes 5898248 | tf_op jit(solution)/shard_map/ppermute | solution.py:34
  56.7 0.6 collective-permute-start.9
  57.3 0.1 collective-permute-start.7
  57.4 0.0 copy-start.5
  57.4 0.8 copy-done.5
  58.3 0.6 compare_select_fusion.refs_0_
  58.9 0.2 convert_reduce_fusion
  59.0 0.8 and_convert_fusion.refs_4_
  59.8 1.1 copy-done.6
  60.9 0.1 shard_map.124
  61.0 2.2 %copy-done.3 = bf16[512,2560]{1,0:T(8,128)(2,1)S(1)} copy-done((bf16[512,2560]{1,0:T(8,128)(2,1)S(1)}, bf16[512,2560]{1,0:T(8,128)(2,1)}, u32[]{:S(2)}) %copy-start.3) | copy-done | bytes 2621464
  63.2 1.8 %shard_map.125.refs_1_ = bf16[8,512,480]{2,1,0:T(8,128)(2,1)S(1)} custom-call(bf16[512,1280]{1,0:T(8,128)(2,1)S(1)} %bitcast.25, bf16[512,2560]{1,0:T(8,128)(2,1)S(1)} %copy-done.3), custom_call_target="tpu_custom_call" | custom-call | flops 1 | bytes 1 | tf_op jit(solution)/shard_map/pallas_call | solution.py:69
  65.1 0.6 slice.34.refs_7_
  65.7 2.0 %copy-done = bf16[8,512,480]{2,1,0:T(8,128)(2,1)} copy-done((bf16[8,512,480]{2,1,0:T(8,128)(2,1)}, bf16[8,512,480]{2,1,0:T(8,128)(2,1)S(1)}, u32[]{:S(2)}) %copy-start) | copy-done | bytes 3932184
  67.6 28.9 %all-gather.5.cloned.1.call-done.refs_3_ = bf16[3840,256]{1,0:T(8,128)(2,1)} async-done(((bf16[480,256]{1,0:T(8,128)(2,1)}), bf16[3840,256]{1,0:T(8,128)(2,1)}) %all-gather.5.cloned.1.call-update) | async-done | bytes 1966096 | tf_op jit(solution)/shard_map/all_gather | solution.py:451
  96.5 5.9 %shard_map.132 = bf16[32,64,256]{2,1,0:T(8,128)(2,1)} custom-call(s32[16]{0:T(128)} %compare_select_fusion.refs_0_, bf16[512,1280]{1,0:T(8,128)(2,1)} %bitcast.26, bf16[512,2560]{1,0:T(8,128)(2,1)} %refs_2_.3, bf16[3840,256]{1,0:T(8,128)(2,1)} %all-gather.5.cloned.1.call-done.refs_3_, bf16[256,128]{1,0:T(8,128)(2,1)} %and_convert_fusion.refs_4_, ...), custom_call_target="tpu_custom_call" | custom-call | flops 1 | bytes 1 | tf_op jit(solution)/shard_map/pallas_call | solution.py:267
  102.4 7.4 %all-to-all-start = ((bf16[32,64,256]{2,1,0:T(8,128)(2,1)}), bf16[32,64,256]{2,1,0:T(8,128)(2,1)S(1)}, u32[]{:S(2)}, u32[]{:S(2)}) async-start(bf16[32,64,256]{2,1,0:T(8,128)(2,1)} %shard_map.132), calls=%async_computation | async-start | bytes 2097152 | tf_op jit(solution)/shard_map/all_to_all | solution.py:465
  109.8 0.1 slice.28
  109.9 1.5 %collective-permute-start.10 = (bf16[480,1024]{1,0:T(8,128)(2,1)S(1)}, bf16[480,1024]{1,0:T(8,128)(2,1)S(1)}, u32[]{:S(2)}, u32[]{:S(2)}) collective-permute-start(bf16[480,1024]{1,0:T(8,128)(2,1)S(1)} %slice.28), channel_id=1, source_target_pairs={{0,8},{8,16},{16,24},{24,0},{1,9},{9,17},{17,25},{25,1},{2,10},{10... | collective-permute-start | bytes 2949128 | tf_op jit(solution)/shard_map/ppermute | solution.py:34
  111.4 1.3 slice.29
  112.7 0.9 collective-permute-start.11
  113.6 0.1 fusion.3
  113.7 0.1 select_reduce_fusion.1
  113.9 2.2 %copy-done.1 = bf16[8,512,480]{2,1,0:T(8,128)(2,1)S(1)} copy-done((bf16[8,512,480]{2,1,0:T(8,128)(2,1)S(1)}, bf16[8,512,480]{2,1,0:T(8,128)(2,1)}, u32[]{:S(2)}) %copy-start.1) | copy-done | bytes 3932184
  116.1 5.0 %shard_map.126 = (f32[512,1024]{1,0:T(8,128)S(1)}, bf16[2,512,480]{2,1,0:T(8,128)(2,1)S(1)}) custom-call(s32[1]{0:T(128)} %bitcast.refs_0_, bf16[8,512,480]{2,1,0:T(8,128)(2,1)S(1)} %copy-done.1, bf16[960,1024]{1,0:T(8,128)(2,1)S(1)} %copy-done.7, bf16[960,1024]{1,0:T(8,128)(2,1)S(1)} %collective-permute-done.8.refs_3_, ...), custom_call_target="tpu_custom_call" | custom-call | flops 1 | bytes 1 | tf_op jit(solution)/shard_map/pallas_call | solution.py:69
  121.1 18.2 %collective-permute-done.10.first = bf16[480,1024]{1,0:T(8,128)(2,1)S(1)} collective-permute-done((bf16[480,1024]{1,0:T(8,128)(2,1)S(1)}, bf16[480,1024]{1,0:T(8,128)(2,1)S(1)}, u32[]{:S(2)}, u32[]{:S(2)}) %collective-permute-start.10) | collective-permute-done | bytes 983072 | tf_op jit(solution)/shard_map/ppermute | solution.py:34
  139.3 3.0 %collective-permute-done.11.second = bf16[480,1024]{1,0:T(8,128)(2,1)S(1)} collective-permute-done((bf16[480,1024]{1,0:T(8,128)(2,1)S(1)}, bf16[480,1024]{1,0:T(8,128)(2,1)S(1)}, u32[]{:S(2)}, u32[]{:S(2)}) %collective-permute-start.11) | collective-permute-done | bytes 983072 | tf_op jit(solution)/shard_map/ppermute | solution.py:34
  142.3 2.9 %shard_map.127 = bf16[512,1024]{1,0:T(8,128)(2,1)} custom-call(f32[512,1024]{1,0:T(8,128)S(1)} %get-tuple-element.25.near, bf16[2,512,480]{2,1,0:T(8,128)(2,1)S(1)} %get-tuple-element.26.across, bf16[480,1024]{1,0:T(8,128)(2,1)S(1)} %collective-permute-done.10.first, bf16[480,1024]{1,0:T(8,128)(2,1)S(1)} %collective-permute-done.11.second), custom_call_target="tpu_custom_call" | custom-call | flops 1000000000 | bytes 1000000000 | tf_op jit(solution)/shard_map/pallas_call | solution.py:371
  145.2 1.8 %shard_map.133 = (bf16[8,128,256]{2,1,0:T(8,128)(2,1)}, bf16[8,1024]{1,0:T(8,128)(2,1)}) custom-call(s32[3,8]{1,0:T(4,128)S(1)} %pad_add_fusion.refs_0_, bf16[32,64,256]{2,1,0:T(8,128)(2,1)S(1)} %all-to-all-done.refs_1_), custom_call_target="tpu_custom_call" | custom-call | flops 1 | bytes 1 | tf_op jit(solution)/shard_map/pallas_call | solution.py:69
  (40 shorter events, 0.2 us)
Async XLA Ops:
  7.2 46.6 %all-gather.3.cloned.1.call-start = ((), (), s32[]{:S(2)}) async-start(), calls=%async_computation.1 | async-start | bytes 2211840 | tf_op jit(solution)/shard_map/all_gather | solution.py:412
  7.9 88.6 %all-gather.5.cloned.1.call-start = ((), (), s32[]{:S(2)}) async-start(), calls=%async_computation.2 | async-start | bytes 2211840 | tf_op jit(solution)/shard_map/all_gather | solution.py:451
  8.0 14.2 %copy-start.9 = (bf16[120,1024]{1,0:T(8,128)(2,1)S(1)}, bf16[120,1024]{1,0:T(8,128)(2,1)}, u32[]{:S(2)}) copy-start(bf16[120,1024]{1,0:T(8,128)(2,1)} %refs_1_.3) | copy-start | bytes 737284
  13.0 2.4 %collective-permute-start = (bf16[4,64,1280]{2,1,0:T(8,128)(2,1)}, bf16[4,64,1280]{2,1,0:T(8,128)(2,1)S(1)}, u32[]{:S(2)}, u32[]{:S(2)}) collective-permute-start(bf16[4,64,1280]{2,1,0:T(8,128)(2,1)} %get-tuple-element.19.refs_3_), channel_id=1, source_target_pairs={{0,1},{1,0},{2,3},{3,2},{4,5},{5,4},{6,7},{7,6},{8,9},{9,8},{10,11... | collective-permute-start | bytes 1966088 | tf_op jit(solution)/shard_map/ppermute | solution.py:34
  15.4 1.3 copy-start.8
  16.7 5.4 %copy-start.10 = (bf16[4,64,1280]{2,1,0:T(8,128)(2,1)S(1)}, bf16[4,64,1280]{2,1,0:T(8,128)(2,1)}, u32[]{:S(2)}) copy-start(bf16[4,64,1280]{2,1,0:T(8,128)(2,1)} %get-tuple-element.19.refs_3_) | copy-start | bytes 1966084
  16.9 8.4 %collective-permute-start.1 = (bf16[64,1280]{1,0:T(8,128)(2,1)S(1)}, bf16[64,1280]{1,0:T(8,128)(2,1)S(1)}, u32[]{:S(2)}, u32[]{:S(2)}) collective-permute-start(bf16[64,1280]{1,0:T(8,128)(2,1)S(1)} %get-tuple-element.22), channel_id=1, source_target_pairs={{0,2},{2,4},{4,6},{6,0},{1,3},{3,5},{5,7},{7,1},{8,10},{10,12},{12... | collective-permute-start | bytes 491528 | tf_op jit(solution)/shard_map/ppermute | solution.py:34
  18.5 8.8 %collective-permute-start.2 = (bf16[64,1280]{1,0:T(8,128)(2,1)S(1)}, bf16[64,1280]{1,0:T(8,128)(2,1)S(1)}, u32[]{:S(2)}, u32[]{:S(2)}) collective-permute-start(bf16[64,1280]{1,0:T(8,128)(2,1)S(1)} %get-tuple-element.23), channel_id=1, source_target_pairs={{0,6},{2,0},{4,2},{6,4},{1,7},{3,1},{5,3},{7,5},{8,14},{10,8},{12,... | collective-permute-start | bytes 491528 | tf_op jit(solution)/shard_map/ppermute | solution.py:34
  20.2 9.0 %collective-permute-start.3 = (bf16[64,1280]{1,0:T(8,128)(2,1)S(1)}, bf16[64,1280]{1,0:T(8,128)(2,1)S(1)}, u32[]{:S(2)}, u32[]{:S(2)}) collective-permute-start(bf16[64,1280]{1,0:T(8,128)(2,1)S(1)} %get-tuple-element.24), channel_id=1, source_target_pairs={{0,4},{2,6},{4,0},{6,2},{1,5},{3,7},{5,1},{7,3},{8,12},{10,14},{12... | collective-permute-start | bytes 491528 | tf_op jit(solution)/shard_map/ppermute | solution.py:34
  22.2 2.2 %copy-start.4 = (bf16[1024,2048]{1,0:T(8,128)(2,1)S(1)}, bf16[1024,2048]{1,0:T(8,128)(2,1)}, u32[]{:S(2)}) copy-start(bf16[1024,2048]{1,0:T(8,128)(2,1)} %refs_2_.2) | copy-start | bytes 12582916
  25.1 8.5 %collective-permute-start.12 = (bf16[4,120,256]{2,1,0:T(8,128)(2,1)S(1)}, bf16[4,120,256]{2,1,0:T(8,128)(2,1)S(1)}, u32[]{:S(2)}, u32[]{:S(2)}) collective-permute-start(bf16[4,120,256]{2,1,0:T(8,128)(2,1)S(1)} %get-tuple-element.27), channel_id=1, source_target_pairs={{0,1},{1,0},{2,3},{3,2},{4,5},{5,4},{6,7},{7,6},{8,9},{9,8},{10,11... | collective-permute-start | bytes 737288 | tf_op jit(solution)/shard_map/ppermute | solution.py:34
  29.1 29.1 %copy-start.11 = (s32[128]{0:T(128)S(1)}, s32[128]{0:T(128)}, u32[]{:S(2)}) copy-start(s32[128]{0:T(128)} %param.17) | copy-start | bytes 1540
  29.1 29.1 %copy-start.12 = (s32[128]{0:T(128)S(1)}, s32[128]{0:T(128)}, u32[]{:S(2)}) copy-start(s32[128]{0:T(128)} %param.16) | copy-start | bytes 1540
  30.2 9.8 %collective-permute-start.4 = (bf16[64,1280]{1,0:T(8,128)(2,1)S(1)}, bf16[64,1280]{1,0:T(8,128)(2,1)S(1)}, u32[]{:S(2)}, u32[]{:S(2)}) collective-permute-start(bf16[64,1280]{1,0:T(8,128)(2,1)S(1)} %fusion.refs_1_), channel_id=1, source_target_pairs={{0,2},{2,4},{4,6},{6,0},{1,3},{3,5},{5,7},{7,1},{8,10},{10,12},{12... | collective-permute-start | bytes 491528 | tf_op jit(solution)/shard_map/ppermute | solution.py:34
  31.4 10.3 %collective-permute-start.5 = (bf16[64,1280]{1,0:T(8,128)(2,1)S(1)}, bf16[64,1280]{1,0:T(8,128)(2,1)S(1)}, u32[]{:S(2)}, u32[]{:S(2)}) collective-permute-start(bf16[64,1280]{1,0:T(8,128)(2,1)S(1)} %fusion.refs_1_), channel_id=1, source_target_pairs={{0,6},{2,0},{4,2},{6,4},{1,7},{3,1},{5,3},{7,5},{8,14},{10,8},{12,... | collective-permute-start | bytes 491528 | tf_op jit(solution)/shard_map/ppermute | solution.py:34
  33.5 8.3 %collective-permute-start.6 = (bf16[64,1280]{1,0:T(8,128)(2,1)S(1)}, bf16[64,1280]{1,0:T(8,128)(2,1)S(1)}, u32[]{:S(2)}, u32[]{:S(2)}) collective-permute-start(bf16[64,1280]{1,0:T(8,128)(2,1)S(1)} %fusion.refs_1_), channel_id=1, source_target_pairs={{0,4},{2,6},{4,0},{6,2},{1,5},{3,7},{5,1},{7,3},{8,12},{10,14},{12... | collective-permute-start | bytes 491528 | tf_op jit(solution)/shard_map/ppermute | solution.py:34
  33.7 8.7 %collective-permute-start.13 = (bf16[120,256]{1,0:T(8,128)(2,1)S(1)}, bf16[120,256]{1,0:T(8,128)(2,1)S(1)}, u32[]{:S(2)}, u32[]{:S(2)}) collective-permute-start(bf16[120,256]{1,0:T(8,128)(2,1)S(1)} %get-tuple-element.30), channel_id=1, source_target_pairs={{0,2},{2,4},{4,6},{6,0},{1,3},{3,5},{5,7},{7,1},{8,10},{10,12},{12... | collective-permute-start | bytes 184328 | tf_op jit(solution)/shard_map/ppermute | solution.py:34
  35.2 7.2 %collective-permute-start.14 = (bf16[120,256]{1,0:T(8,128)(2,1)S(1)}, bf16[120,256]{1,0:T(8,128)(2,1)S(1)}, u32[]{:S(2)}, u32[]{:S(2)}) collective-permute-start(bf16[120,256]{1,0:T(8,128)(2,1)S(1)} %get-tuple-element.31), channel_id=1, source_target_pairs={{0,6},{2,0},{4,2},{6,4},{1,7},{3,1},{5,3},{7,5},{8,14},{10,8},{12,... | collective-permute-start | bytes 184328 | tf_op jit(solution)/shard_map/ppermute | solution.py:34
  40.0 5.7 %collective-permute-start.15 = (bf16[120,256]{1,0:T(8,128)(2,1)S(1)}, bf16[120,256]{1,0:T(8,128)(2,1)S(1)}, u32[]{:S(2)}, u32[]{:S(2)}) collective-permute-start(bf16[120,256]{1,0:T(8,128)(2,1)S(1)} %get-tuple-element.32), channel_id=1, source_target_pairs={{0,4},{2,6},{4,0},{6,2},{1,5},{3,7},{5,1},{7,3},{8,12},{10,14},{12... | collective-permute-start | bytes 184328 | tf_op jit(solution)/shard_map/ppermute | solution.py:34
  45.7 8.7 %collective-permute-start.16 = (bf16[120,256]{1,0:T(8,128)(2,1)S(1)}, bf16[120,256]{1,0:T(8,128)(2,1)S(1)}, u32[]{:S(2)}, u32[]{:S(2)}) collective-permute-start(bf16[120,256]{1,0:T(8,128)(2,1)S(1)} %shard_map.130.refs_1_), channel_id=1, source_target_pairs={{0,8},{8,16},{16,24},{24,0},{1,9},{9,17},{17,25},{25,1},{2,10},{10... | collective-permute-start | bytes 184328 | tf_op jit(solution)/shard_map/ppermute | solution.py:34
  47.3 7.1 %collective-permute-start.17 = (bf16[120,256]{1,0:T(8,128)(2,1)S(1)}, bf16[120,256]{1,0:T(8,128)(2,1)S(1)}, u32[]{:S(2)}, u32[]{:S(2)}) collective-permute-start(bf16[120,256]{1,0:T(8,128)(2,1)S(1)} %shard_map.130.refs_1_), channel_id=1, source_target_pairs={{0,24},{8,0},{16,8},{24,16},{1,25},{9,1},{17,9},{25,17},{2,26},{10... | collective-permute-start | bytes 184328 | tf_op jit(solution)/shard_map/ppermute | solution.py:34
  47.8 6.6 %collective-permute-start.18 = (bf16[120,256]{1,0:T(8,128)(2,1)S(1)}, bf16[120,256]{1,0:T(8,128)(2,1)S(1)}, u32[]{:S(2)}, u32[]{:S(2)}) collective-permute-start(bf16[120,256]{1,0:T(8,128)(2,1)S(1)} %shard_map.130.refs_1_), channel_id=1, source_target_pairs={{0,16},{8,24},{16,0},{24,8},{1,17},{9,25},{17,1},{25,9},{2,18},{10... | collective-permute-start | bytes 184328 | tf_op jit(solution)/shard_map/ppermute | solution.py:34
  55.2 54.6 %collective-permute-start.8 = (bf16[960,1024]{1,0:T(8,128)(2,1)}, bf16[960,1024]{1,0:T(8,128)(2,1)S(1)}, u32[]{:S(2)}, u32[]{:S(2)}) collective-permute-start(bf16[960,1024]{1,0:T(8,128)(2,1)} %all-gather.3.cloned.1.call-done.refs_2_), channel_id=1, source_target_pairs={{0,8},{8,16},{16,24},{24,0},{1,9},{9,17},{17,25},{25,1},{2,10},{10... | collective-permute-start | bytes 5898248 | tf_op jit(solution)/shard_map/ppermute | solution.py:34
  56.7 54.7 %collective-permute-start.9 = (bf16[960,1024]{1,0:T(8,128)(2,1)}, bf16[960,1024]{1,0:T(8,128)(2,1)}, u32[]{:S(2)}, u32[]{:S(2)}) collective-permute-start(bf16[960,1024]{1,0:T(8,128)(2,1)} %all-gather.3.cloned.1.call-done.refs_2_), channel_id=1, source_target_pairs={{0,24},{8,0},{16,8},{24,16},{1,25},{9,1},{17,9},{25,17},{2,26},{10... | collective-permute-start | bytes 5898248 | tf_op jit(solution)/shard_map/ppermute | solution.py:34
  57.3 2.5 %collective-permute-start.7 = (bf16[256,1280]{1,0:T(8,128)(2,1)S(1)}, bf16[256,1280]{1,0:T(8,128)(2,1)S(1)}, u32[]{:S(2)}, u32[]{:S(2)}) collective-permute-start(bf16[256,1280]{1,0:T(8,128)(2,1)S(1)} %bitcast.27), channel_id=1, source_target_pairs={{0,1},{1,0},{2,3},{3,2},{4,5},{5,4},{6,7},{7,6},{8,9},{9,8},{10,11... | collective-permute-start | bytes 1966088 | tf_op jit(solution)/shard_map/ppermute | solution.py:34
  57.4 0.8 copy-start.5
  59.8 1.1 copy-start.6
  61.0 4.1 %copy-start.2 = (bf16[2,256,1280]{2,1,0:T(8,128)(2,1)}, bf16[2,256,1280]{2,1,0:T(8,128)(2,1)S(1)}, u32[]{:S(2)}) copy-start(bf16[2,256,1280]{2,1,0:T(8,128)(2,1)S(1)} %shard_map.124) | copy-start | bytes 3932164
  61.0 2.2 %copy-start.3 = (bf16[512,2560]{1,0:T(8,128)(2,1)S(1)}, bf16[512,2560]{1,0:T(8,128)(2,1)}, u32[]{:S(2)}) copy-start(bf16[512,2560]{1,0:T(8,128)(2,1)} %refs_2_.3) | copy-start | bytes 7864324
  65.7 2.0 %copy-start = (bf16[8,512,480]{2,1,0:T(8,128)(2,1)}, bf16[8,512,480]{2,1,0:T(8,128)(2,1)S(1)}, u32[]{:S(2)}) copy-start(bf16[8,512,480]{2,1,0:T(8,128)(2,1)S(1)} %shard_map.125.refs_1_) | copy-start | bytes 11796484
  102.4 42.8 %all-to-all-start = ((bf16[32,64,256]{2,1,0:T(8,128)(2,1)}), bf16[32,64,256]{2,1,0:T(8,128)(2,1)S(1)}, u32[]{:S(2)}, u32[]{:S(2)}) async-start(bf16[32,64,256]{2,1,0:T(8,128)(2,1)} %shard_map.132), calls=%async_computation | async-start | bytes 2097152 | tf_op jit(solution)/shard_map/all_to_all | solution.py:465
  109.8 4.1 %copy-start.7 = (bf16[960,1024]{1,0:T(8,128)(2,1)S(1)}, bf16[960,1024]{1,0:T(8,128)(2,1)}, u32[]{:S(2)}) copy-start(bf16[960,1024]{1,0:T(8,128)(2,1)} %all-gather.3.cloned.1.call-done.refs_2_) | copy-start | bytes 5898244
  109.9 29.4 %collective-permute-start.10 = (bf16[480,1024]{1,0:T(8,128)(2,1)S(1)}, bf16[480,1024]{1,0:T(8,128)(2,1)S(1)}, u32[]{:S(2)}, u32[]{:S(2)}) collective-permute-start(bf16[480,1024]{1,0:T(8,128)(2,1)S(1)} %slice.28), channel_id=1, source_target_pairs={{0,8},{8,16},{16,24},{24,0},{1,9},{9,17},{17,25},{25,1},{2,10},{10... | collective-permute-start | bytes 2949128 | tf_op jit(solution)/shard_map/ppermute | solution.py:34
  112.7 29.6 %collective-permute-start.11 = (bf16[480,1024]{1,0:T(8,128)(2,1)S(1)}, bf16[480,1024]{1,0:T(8,128)(2,1)S(1)}, u32[]{:S(2)}, u32[]{:S(2)}) collective-permute-start(bf16[480,1024]{1,0:T(8,128)(2,1)S(1)} %slice.29), channel_id=1, source_target_pairs={{0,24},{8,0},{16,8},{24,16},{1,25},{9,1},{17,9},{25,17},{2,26},{10... | collective-permute-start | bytes 2949128 | tf_op jit(solution)/shard_map/ppermute | solution.py:34
  113.9 2.2 %copy-start.1 = (bf16[8,512,480]{2,1,0:T(8,128)(2,1)S(1)}, bf16[8,512,480]{2,1,0:T(8,128)(2,1)}, u32[]{:S(2)}) copy-start(bf16[8,512,480]{2,1,0:T(8,128)(2,1)} %copy-done) | copy-start | bytes 11796484
Sparse Core Ops, SparseCore 0:
  9.8 43.9 all-gather.2
  56.1 40.3 all-gather.4
